TPU v7x, 256 devices: a whole 4x4x8 slice. The times are simulated.
256 devices in a mesh: band: 4 (over z_lo), rail: 64 (over x, z_hi, y, core).
Axes of the slice: x: 4, y: 4, z: 8 (z_hi: 2, z_lo: 4; z = z_hi * 4 + z_lo), core: 2. Of those that a mesh axis runs over, the one named last changes fastest.
Arguments:
- features: bfloat16 [64, 64, 96, 256], P('rail', 'band'), may hold values from -6 to 6
- first_kernel: bfloat16 [3, 3, 256, 256], replicated, may hold values from -0.125 to 0.125
- second_kernel: bfloat16 [3, 3, 256, 256], replicated, may hold values from -0.125 to 0.125
- classifier: bfloat16 [256, 3], replicated, may hold values from -0.011962891 to 0.011962891
- class_bias: float32 [3], replicated, may hold values from -0.04 to 0.04
- labels: int32 [64, 64, 96], P('rail', 'band'), may hold values from 0 to 2
Outputs:
- grad_features: bfloat16 [64, 64, 96, 256], P('rail', 'band')
- grad_first: float32 [3, 3, 256, 256], replicated
- grad_second: float32 [3, 3, 256, 256], replicated
- grad_classifier: float32 [256, 3], replicated
- grad_bias: float32 [3], replicated
All inputs are finite; a program needn't handle non-finite values.
Results may differ from a plain program's by a relative error of at most 0.013.
Values may be sent and summed in bfloat16 or wider, within the bound.
No kernel may reach another device: no remote copies, remote signals or barrier semaphores. Data moves between devices by JAX's collectives and lax.ppermute only.
A program may use at most 64 MiB of HBM per device.

v0:
```python
import jax
import jax.numpy as jnp
from jax import lax
from jax.sharding import PartitionSpec as P


def padded_2(block, sides, width):
    for axis, dim in sides:
        count = lax.axis_size(axis)
        forward = [(i, i + 1) for i in range(count - 1)]
        backward = [(target, source) for source, target in forward]
        low = lax.ppermute(
            lax.slice_in_dim(block, block.shape[dim] - width, None, axis=dim), axis, forward
        )
        high = lax.ppermute(lax.slice_in_dim(block, 0, width, axis=dim), axis, backward)
        block = jnp.concatenate([low, block, high], axis=dim)
    return block


def with_rows(field):
    return padded_2(field, (("band", 1),), 1)


def convolve(extended, kernel):
    return lax.conv_general_dilated(
        extended,
        kernel,
        (1, 1),
        ((0, 0), (1, 1)),
        dimension_numbers=("NHWC", "HWIO", "NHWC"),
        preferred_element_type=jnp.float32,
    )


def flipped(kernel):
    return jnp.transpose(kernel[::-1, ::-1], (0, 1, 3, 2))


def silu_slope(value):
    sig = jax.nn.sigmoid(value)
    return sig * (1.0 + value * (1.0 - sig))


def kernel_grad(extended, grad):
    height = grad.shape[1]
    width = grad.shape[2]
    chans = grad.shape[3]
    padded = jnp.pad(extended, ((0, 0), (0, 0), (1, 1), (0, 0)))
    grad_rows = grad.reshape(-1, chans)
    taps = []
    for row_tap in range(3):
        line = []
        for col_tap in range(3):
            window = padded[:, row_tap : row_tap + height, col_tap : col_tap + width, :].reshape(
                -1, padded.shape[3]
            )
            line.append(
                lax.dot_general(
                    window, grad_rows, (((0,), (0,)), ((), ())), preferred_element_type=jnp.float32
                )
            )
        taps.append(jnp.stack(line))
    return jnp.stack(taps)


def reduce_bucket(pieces):
    flat = jnp.concatenate([piece.reshape(-1) for piece in pieces])
    total = lax.psum(flat, ("band", "rail"))
    results = []
    offset = 0
    for piece in pieces:
        results.append(total[offset : offset + piece.size].reshape(piece.shape))
        offset = offset + piece.size
    return results


def per_device(features, first_kernel, second_kernel, classifier, class_bias, labels):
    chans = features.shape[3]
    classes = classifier.shape[1]
    count = (
        features.shape[0]
        * features.shape[1]
        * features.shape[2]
        * lax.axis_size("band")
        * lax.axis_size("rail")
    )
    scale = float(count) ** (-0.5)
    feat_ext = with_rows(features)
    first_pre = convolve(feat_ext, first_kernel)
    first_act = jax.nn.silu(first_pre).astype(jnp.bfloat16)
    first_ext = with_rows(first_act)
    second_pre = convolve(first_ext, second_kernel)
    second_act = jax.nn.silu(second_pre).astype(jnp.bfloat16)
    flat_act = second_act.reshape(-1, chans)
    logits = jnp.dot(flat_act, classifier, preferred_element_type=jnp.float32) + class_bias
    onehot = (labels.reshape(-1)[:, None] == jnp.arange(classes, dtype=jnp.int32)[None, :]).astype(
        jnp.float32
    )
    dlogits = (jax.nn.softmax(logits, axis=-1) - onehot) * scale
    bias_term = jnp.sum(dlogits, axis=0)
    class_term = jnp.dot(flat_act.astype(jnp.float32).T, dlogits, precision=lax.Precision.HIGHEST)
    back = jnp.dot(
        dlogits, classifier.astype(jnp.float32).T, precision=lax.Precision.HIGHEST
    ).reshape(second_pre.shape)
    second_grad = (back * silu_slope(second_pre)).astype(jnp.bfloat16)
    second_term = kernel_grad(first_ext, second_grad)
    grad_second, grad_classifier, grad_bias = reduce_bucket([second_term, class_term, bias_term])
    second_ext = with_rows(second_grad)
    first_grad = (convolve(second_ext, flipped(second_kernel)) * silu_slope(first_pre)).astype(
        jnp.bfloat16
    )
    first_term = kernel_grad(feat_ext, first_grad)
    grad_first = reduce_bucket([first_term])[0]
    first_ext_grad = with_rows(first_grad)
    grad_features = convolve(first_ext_grad, flipped(first_kernel)).astype(jnp.bfloat16)
    return (grad_features, grad_first, grad_second, grad_classifier, grad_bias)


def solution(mesh):
    placed = (P("rail", "band", None, None), P(), P(), P(), P(), P("rail", "band", None))
    return jax.shard_map(
        per_device,
        mesh=mesh,
        in_specs=placed,
        out_specs=(P("rail", "band", None, None), P(), P(), P(), P()),
        check_vma=False,
    )
```

profile of v0, /device:TPU:1, one launch (start us, length us, event | category | flops | bytes accessed | tf_op | source)
XLA Modules:
  0.0 371.4 jit_solution(4302401183678262196)
XLA Ops:
  8.1 4.4 %collective-permute-start = (bf16[1,1,96,256]{3,2,1,0:T(8,128)(2,1)S(1)}, bf16[1,1,96,256]{3,2,1,0:T(8,128)(2,1)S(1)}, u32[]{:S(2)}, u32[]{:S(2)}) collective-permute-start(bf16[1,1,96,256]{3,2,1,0:T(8,128)(2,1)S(1)} %get-tuple-element.30), channel_id=1, source_target_pairs={{0,64},{64,128},{128,192},{1,65},{65,129},{129,193},{2,66},{66,130... | collective-permute-start | bytes 147464 | tf_op jit(solution)/shard_map/ppermute | solution.py:12
  12.5 1.3 collective-permute-start.1
  15.0 2.5 collective-permute-done.1
  21.1 3.5 multiply_convert_fusion.2
  26.1 4.2 %collective-permute-start.2 = (bf16[1,1,96,256]{3,2,1,0:T(8,128)(2,1)S(1)}, bf16[1,1,96,256]{3,2,1,0:T(8,128)(2,1)S(1)}, u32[]{:S(2)}, u32[]{:S(2)}) collective-permute-start(bf16[1,1,96,256]{3,2,1,0:T(8,128)(2,1)S(1)} %slice.147), channel_id=1, source_target_pairs={{0,64},{64,128},{128,192},{1,65},{65,129},{129,193},{2,66},{66,130... | collective-permute-start | bytes 147464 | tf_op jit(solution)/shard_map/ppermute | solution.py:12
  34.0 2.6 multiply_convert_fusion.1
  42.7 1.4 convolution_bitcast_fusion
  44.1 1.4 convolution_bitcast_fusion.2
  46.9 1.4 convolution_bitcast_fusion.3
  48.3 1.6 convolution_bitcast_fusion.4
  49.9 1.4 convolution_bitcast_fusion.5
  52.6 5.2 %collective-permute-start.4 = (bf16[1,1,96,256]{3,1,2,0:T(2,128)(2,1)}, bf16[1,1,96,256]{3,1,2,0:T(2,128)(2,1)}, u32[]{:S(2)}, u32[]{:S(2)}) collective-permute-start(bf16[1,1,96,256]{3,1,2,0:T(2,128)(2,1)} %get-tuple-element.27), channel_id=1, source_target_pairs={{0,64},{64,128},{128,192},{1,65},{65,129},{129,193},{2,66},{66,130... | collective-permute-start | bytes 147464 | tf_op jit(solution)/shard_map/ppermute | solution.py:12
  58.6 1.5 convolution_bitcast_fusion.1
  62.8 1.6 pad_maximum_fusion
  64.4 1.6 maximum_bitcast_fusion
  67.6 2.5 multiply_convert_fusion
  78.3 1.6 pad_maximum_fusion.1
  80.0 1.3 collective-permute-start.7
  81.4 4.0 %collective-permute-start.6 = (bf16[1,1,96,256]{3,2,1,0:T(8,128)(2,1)S(1)}, bf16[1,1,96,256]{3,2,1,0:T(8,128)(2,1)S(1)}, u32[]{:S(2)}, u32[]{:S(2)}) collective-permute-start(bf16[1,1,96,256]{3,2,1,0:T(8,128)(2,1)S(1)} %slice.158), channel_id=1, source_target_pairs={{0,64},{64,128},{128,192},{1,65},{65,129},{129,193},{2,66},{66,130... | collective-permute-start | bytes 147464 | tf_op jit(solution)/shard_map/ppermute | solution.py:12
  88.7 2.2 select_convert_fusion
  92.3 262.6 %all-reduce.5.cloned.1.call-done = (f32[3,3,256,256]{3,2,1,0:T(8,128)}, f32[590595]{0:T(1024)}) async-done(((f32[3,3,256,256]{3,2,1,0:T(8,128)}, f32[590595]{0:T(1024)}), (f32[3,3,256,256]{3,2,1,0:T(8,128)}, f32[590595]{0:T(1024)})) %all-reduce.5.cloned.1.call-update) | async-done | bytes 4721692 | tf_op jit(solution)/shard_map/psum | solution.py:68
  354.9 1.8 slice.164
  358.6 1.7 reshape.168
  361.2 3.3 copy.157
  (150 shorter events, 40.0 us)
Async XLA Ops:
  7.2 26.8 %copy-start = (bf16[3,3,256,256]{3,2,1,0:T(8,128)(2,1)S(1)}, bf16[3,3,256,256]{3,2,1,0:T(8,128)(2,1)}, u32[]{:S(2)}) copy-start(bf16[3,3,256,256]{3,2,1,0:T(8,128)(2,1)} %param.8) | copy-start | bytes 3538948
  7.2 347.7 %all-reduce.5.cloned.1.call-start = ((), (), s32[]{:S(2)}) async-start(), calls=%async_computation | async-start | bytes 9445376 | tf_op jit(solution)/shard_map/psum | solution.py:68
  8.1 5.7 %collective-permute-start = (bf16[1,1,96,256]{3,2,1,0:T(8,128)(2,1)S(1)}, bf16[1,1,96,256]{3,2,1,0:T(8,128)(2,1)S(1)}, u32[]{:S(2)}, u32[]{:S(2)}) collective-permute-start(bf16[1,1,96,256]{3,2,1,0:T(8,128)(2,1)S(1)} %get-tuple-element.30), channel_id=1, source_target_pairs={{0,64},{64,128},{128,192},{1,65},{65,129},{129,193},{2,66},{66,130... | collective-permute-start | bytes 147464 | tf_op jit(solution)/shard_map/ppermute | solution.py:12
  12.5 5.0 %collective-permute-start.1 = (bf16[1,1,96,256]{3,2,1,0:T(8,128)(2,1)S(1)}, bf16[1,1,96,256]{3,2,1,0:T(8,128)(2,1)S(1)}, u32[]{:S(2)}, u32[]{:S(2)}) collective-permute-start(bf16[1,1,96,256]{3,2,1,0:T(8,128)(2,1)S(1)} %get-tuple-element.29), channel_id=1, source_target_pairs={{64,0},{128,64},{192,128},{65,1},{129,65},{193,129},{66,2},{130,66... | collective-permute-start | bytes 147464 | tf_op jit(solution)/shard_map/ppermute | solution.py:15
  19.8 1.3 copy-start.25
  19.9 1.3 copy-start.27
  21.1 9.1 %copy-start.22 = (s32[1,16,96]{2,1,0:T(8,128)S(1)}, s32[1,16,96]{2,1,0:T(8,128)}, u32[]{:S(2)}) copy-start(s32[1,16,96]{2,1,0:T(8,128)} %param.11) | copy-start | bytes 18436
  24.7 6.1 %collective-permute-start.3 = (bf16[1,1,96,256]{3,2,1,0:T(8,128)(2,1)S(1)}, bf16[1,1,96,256]{3,2,1,0:T(8,128)(2,1)S(1)}, u32[]{:S(2)}, u32[]{:S(2)}) collective-permute-start(bf16[1,1,96,256]{3,2,1,0:T(8,128)(2,1)S(1)} %slice.150), channel_id=1, source_target_pairs={{64,0},{128,64},{192,128},{65,1},{129,65},{193,129},{66,2},{130,66... | collective-permute-start | bytes 147464 | tf_op jit(solution)/shard_map/ppermute | solution.py:15
  26.1 5.3 %collective-permute-start.2 = (bf16[1,1,96,256]{3,2,1,0:T(8,128)(2,1)S(1)}, bf16[1,1,96,256]{3,2,1,0:T(8,128)(2,1)S(1)}, u32[]{:S(2)}, u32[]{:S(2)}) collective-permute-start(bf16[1,1,96,256]{3,2,1,0:T(8,128)(2,1)S(1)} %slice.147), channel_id=1, source_target_pairs={{0,64},{64,128},{128,192},{1,65},{65,129},{129,193},{2,66},{66,130... | collective-permute-start | bytes 147464 | tf_op jit(solution)/shard_map/ppermute | solution.py:12
  30.8 1.7 copy-start.4
  30.9 1.7 copy-start.17
  40.8 1.9 copy-start.9
  46.9 1.4 copy-start.3
  49.9 8.6 %copy-start.5 = (bf16[16,1,96,256]{3,2,0,1:T(8,128)(2,1)S(1)}, bf16[16,1,96,256]{3,2,0,1:T(8,128)(2,1)}, u32[]{:S(2)}) copy-start(bf16[16,1,96,256]{3,2,0,1:T(8,128)(2,1)} %copy-done.4) | copy-start | bytes 2359300
  51.3 13.1 %collective-permute-start.5 = (bf16[1,1,96,256]{3,1,2,0:T(2,128)(2,1)}, bf16[1,1,96,256]{3,1,2,0:T(2,128)(2,1)S(1)}, u32[]{:S(2)}, u32[]{:S(2)}) collective-permute-start(bf16[1,1,96,256]{3,1,2,0:T(2,128)(2,1)} %get-tuple-element.28), channel_id=1, source_target_pairs={{64,0},{128,64},{192,128},{65,1},{129,65},{193,129},{66,2},{130,66... | collective-permute-start | bytes 147464 | tf_op jit(solution)/shard_map/ppermute | solution.py:15
  52.6 11.8 %collective-permute-start.4 = (bf16[1,1,96,256]{3,1,2,0:T(2,128)(2,1)}, bf16[1,1,96,256]{3,1,2,0:T(2,128)(2,1)}, u32[]{:S(2)}, u32[]{:S(2)}) collective-permute-start(bf16[1,1,96,256]{3,1,2,0:T(2,128)(2,1)} %get-tuple-element.27), channel_id=1, source_target_pairs={{0,64},{64,128},{128,192},{1,65},{65,129},{129,193},{2,66},{66,130... | collective-permute-start | bytes 147464 | tf_op jit(solution)/shard_map/ppermute | solution.py:12
  58.6 1.5 copy-start.13
  58.6 1.5 copy-start.14
  58.6 1.6 copy-start.19
  66.2 1.5 copy-start.29
  80.0 5.6 %collective-permute-start.7 = (bf16[1,1,96,256]{3,2,1,0:T(8,128)(2,1)S(1)}, bf16[1,1,96,256]{3,2,1,0:T(8,128)(2,1)S(1)}, u32[]{:S(2)}, u32[]{:S(2)}) collective-permute-start(bf16[1,1,96,256]{3,2,1,0:T(8,128)(2,1)S(1)} %slice.161), channel_id=1, source_target_pairs={{64,0},{128,64},{192,128},{65,1},{129,65},{193,129},{66,2},{130,66... | collective-permute-start | bytes 147464 | tf_op jit(solution)/shard_map/ppermute | solution.py:15
  81.4 5.2 %collective-permute-start.6 = (bf16[1,1,96,256]{3,2,1,0:T(8,128)(2,1)S(1)}, bf16[1,1,96,256]{3,2,1,0:T(8,128)(2,1)S(1)}, u32[]{:S(2)}, u32[]{:S(2)}) collective-permute-start(bf16[1,1,96,256]{3,2,1,0:T(8,128)(2,1)S(1)} %slice.158), channel_id=1, source_target_pairs={{0,64},{64,128},{128,192},{1,65},{65,129},{129,193},{2,66},{66,130... | collective-permute-start | bytes 147464 | tf_op jit(solution)/shard_map/ppermute | solution.py:12
  87.5 1.3 copy-start.26
  361.2 3.3 copy-start.1
  (15 other events, 14.2 us)
Sparse Core Ops, SparseCore 0:
  80.1 274.8 all-reduce.4
where the time goes:
time: 373 us; the launch traced here: 371 us
  waiting for transfers between devices  267 us (72%)
  matrix products  29.9 us (8%)
  local copies, waits for them, and re-layouts  29.1 us (8%)
  starting transfers between devices  22.9 us (6%)
  between operations  14.9 us (4%)
  other arithmetic  8.08 us (2%)
    psum x1, waiting for transfers between devices, reduce_bucket(): total = lax.psum(flat, ('band', 'rail'))  263 us
    ppermute x4, starting transfers between devices, padded_2(): lax.ppermute(lax.slice_in_dim(block, block.shape[dim] - width, None, axis...  17.7 us
    dot_general x18, matrix products, kernel_grad(): lax.dot_general(window, grad_rows, (((0,), (0,)), ((), ())), preferred_el...  17 us
    unnamed x68, local copies, waits for them, and re-layouts  14.7 us
    conv_general_dilated x4, matrix products, convolve(): lax.conv_general_dilated(extended, kernel, (1, 1), ((0, 0), (1, 1)), dime...  10.8 us
  transfers between devices with their start and end apart: 9, of which 4 were waited for; matrix products, arithmetic and copies ran while one was open for 4% of the time, Pallas kernels for 0%

commit v1 on v0

v1 whole, which is shorter than its diff:
```python
import jax
import jax.numpy as jnp
from jax import lax
from jax.experimental import pallas as pl
from jax.experimental.pallas import tpu as pltpu
from jax.sharding import Mesh, PartitionSpec as P

ROWS = 16
COLS = 96
CH = 256
F32 = jnp.float32
BF16 = jnp.bfloat16
PAR = (((0,), (0,)), ((), ()))


def conv_rows(wide, start, count, kernel):
    patch = jnp.concatenate(
        [wide[pl.ds(pl.multiple_of(start + a * COLS, COLS), count * COLS), :] for a in range(3)],
        axis=1,
    )
    out = jnp.dot(patch, kernel[...], preferred_element_type=F32)
    return out.reshape(count, COLS, CH)


def store_wide(wide, start, rows):
    count = rows.shape[0]
    col = lax.broadcasted_iota(jnp.int32, rows.shape, 1)
    left = jnp.where(col == 0, 0.0, pltpu.roll(rows, 1, 1))
    right = jnp.where(col == COLS - 1, 0.0, pltpu.roll(rows, COLS - 1, 1))
    at = pl.ds(pl.multiple_of(start, COLS), count * COLS)
    wide[at, 0:CH] = left.astype(BF16).reshape(count * COLS, CH)
    wide[at, CH:2 * CH] = rows.astype(BF16).reshape(count * COLS, CH)
    wide[at, 2 * CH:3 * CH] = right.astype(BF16).reshape(count * COLS, CH)


def sigmoid(value):
    return 0.5 * jnp.tanh(0.5 * value) + 0.5


def keep_rows(rows, first, height):
    parts = []
    for r in range(rows.shape[0]):
        inside = jnp.logical_and(first + r >= 0, first + r < height)
        parts.append(rows[r] * jnp.where(inside, 1.0, 0.0))
    return jnp.stack(parts)


def make_main(height, scale, r1=2, r2=4, rt=2):
    def main(band_ref, f_ref, k1, k2, k2t, cls, bias, lab, own, g1, g2, small, fg,
             fw, aw, sw, gt, slope):
        base = band_ref[0] * ROWS
        n1, n2, nt = 22 // r1, 20 // r2, 18 // rt

        def widen(t, c):
            at = t * (2 * COLS)
            rows = f_ref[pl.ds(pl.multiple_of(at, COLS), 2 * COLS), :].astype(F32)
            store_wide(fw, at, rows.reshape(2, COLS, CH))
            return c

        lax.fori_loop(0, 12, widen, 0)

        def first(t, c):
            at = t * (r1 * COLS)
            v = conv_rows(fw, at, r1, k1)
            s = sigmoid(v)
            slope[pl.ds(pl.multiple_of(at, COLS), r1 * COLS), :] = (
                s * (1.0 + v * (1.0 - s))
            ).reshape(r1 * COLS, CH)
            store_wide(aw, at, keep_rows(v * s, base - 3 + t * r1, height))
            return c

        lax.fori_loop(0, n1, first, 0)

        small[...] = jnp.zeros_like(small)
        lane = lax.broadcasted_iota(jnp.int32, (8, CH), 1)

        def second(t, c):
            at = t * (r2 * COLS)
            v = conv_rows(aw, at, r2, k2)
            s = sigmoid(v)
            act = (v * s).astype(BF16).reshape(r2 * COLS, CH)
            logit = lax.dot_general(
                cls[...], act, (((1,), (1,)), ((), ())), preferred_element_type=F32
            )
            rows = [logit[k:k + 1, :] + bias[k:k + 1, 0:1] for k in range(3)]
            top = jnp.maximum(jnp.maximum(rows[0], rows[1]), rows[2])
            ex = [jnp.exp(row - top) for row in rows]
            den = ex[0] + ex[1] + ex[2]
            label = lab[t]
            mine = own[t]
            dl = [(ex[k] / den - jnp.where(label == k, 1.0, 0.0)) * scale for k in range(3)]
            hi = [d.astype(BF16).astype(F32) for d in dl]
            lo = [d - h for d, h in zip(dl, hi)]
            zero = jnp.zeros((10, r2 * COLS), F32)
            pack = jnp.concatenate(hi + lo + [zero], axis=0)
            back = lax.dot_general(pack.astype(BF16), cls[...], PAR, preferred_element_type=F32)
            grad = back.reshape(r2, COLS, CH) * (s * (1.0 + v * (1.0 - s)))
            store_wide(sw, at, keep_rows(grad, base - 2 + t * r2, height))
            part = jnp.dot((pack * mine).astype(BF16), act, preferred_element_type=F32)
            sums = [jnp.sum(d * mine, axis=1, keepdims=True) for d in dl]
            bias_row = jnp.where(
                lane[0:1] == 0, sums[0], jnp.where(lane[0:1] == 1, sums[1], jnp.where(lane[0:1] == 2, sums[2], 0.0))
            )
            small[0:3, :] += part[0:3] + part[3:6]
            small[3:4, :] += bias_row
            return c

        lax.fori_loop(0, n2, second, 0)

        def weight(grad_wide, skip, src, src_skip, out):
            gt[...] = grad_wide[skip * COLS:(skip + ROWS) * COLS, CH:2 * CH].T
            for a in range(3):
                win = src[(src_skip + a) * COLS:(src_skip + a + ROWS) * COLS, :]
                res = jnp.dot(gt[...], win, preferred_element_type=F32)
                for b in range(3):
                    out[(3 * a + b) * CH:(3 * a + b + 1) * CH, :] = (
                        res[:, b * CH:(b + 1) * CH].T.astype(BF16)
                    )

        weight(sw, 2, aw, 2, g2)

        def third(t, c):
            at = t * (rt * COLS)
            v = conv_rows(sw, at, rt, k2t)
            sl = slope[pl.ds(pl.multiple_of(at + 2 * COLS, COLS), rt * COLS), :]
            g = keep_rows(v * sl.reshape(rt, COLS, CH), base - 1 + t * rt, height)
            store_wide(fg, at, g)
            return c

        lax.fori_loop(0, nt, third, 0)
        weight(fg, 1, fw, 3, g1)

    return main


def main_call(band, f, k1, k2, k2t, cls, bias, lab, own, height, scale, **kw):
    vm = pl.BlockSpec(memory_space=pltpu.VMEM)
    return pl.pallas_call(
        make_main(height, scale, **kw),
        out_shape=(
            jax.ShapeDtypeStruct((9 * CH, CH), BF16),
            jax.ShapeDtypeStruct((9 * CH, CH), BF16),
            jax.ShapeDtypeStruct((8, CH), F32),
            jax.ShapeDtypeStruct((18 * COLS, 3 * CH), BF16),
        ),
        in_specs=[pl.BlockSpec(memory_space=pltpu.SMEM)] + [vm] * 8,
        out_specs=(vm,) * 4,
        scratch_shapes=[
            pltpu.VMEM((24 * COLS, 3 * CH), BF16),
            pltpu.VMEM((22 * COLS, 3 * CH), BF16),
            pltpu.VMEM((20 * COLS, 3 * CH), BF16),
            pltpu.VMEM((CH, ROWS * COLS), BF16),
            pltpu.VMEM((22 * COLS, CH), F32),
        ],
        compiler_params=pltpu.CompilerParams(vmem_limit_bytes=40 * 1024 * 1024),
        cost_estimate=pl.CostEstimate(flops=11_000_000_000, bytes_accessed=8_000_000, transcendentals=1_000_000),
        name="main",
    )(band, f, k1, k2, k2t, cls, bias, lab, own)


def feat_kernel(fg, k1t, out):
    def step(t, c):
        at = t * (4 * COLS)
        v = conv_rows(fg, at, 4, k1t)
        out[pl.ds(pl.multiple_of(at, COLS), 4 * COLS), :] = v.astype(BF16).reshape(4 * COLS, CH)
        return c

    lax.fori_loop(0, 4, step, 0)


def feat_call(fg, k1t):
    vm = pl.BlockSpec(memory_space=pltpu.VMEM)
    return pl.pallas_call(
        feat_kernel,
        out_shape=jax.ShapeDtypeStruct((ROWS * COLS, CH), BF16),
        in_specs=[vm] * 2,
        out_specs=vm,
        compiler_params=pltpu.CompilerParams(vmem_limit_bytes=16 * 1024 * 1024),
        cost_estimate=pl.CostEstimate(flops=1_800_000_000, bytes_accessed=4_000_000, transcendentals=0),
        name="feat",
    )(fg, k1t)


AXES = ("b", "x", "h", "y", "c")


def shift(value, axis, step, size):
    return lax.ppermute(value, axis, [(i, (i + step) % size) for i in range(size)])


def split_small(small):
    hi = small.astype(BF16)
    return jnp.concatenate([hi, (small - hi.astype(F32)).astype(BF16)], axis=0)


def join_small(rows):
    full = rows.astype(F32)
    return full[..., 0:8, :] + full[..., 8:16, :]


def per_device(features, first_kernel, second_kernel, classifier, class_bias, labels):
    height = ROWS * lax.axis_size("b")
    count = height * COLS * lax.axis_size("x") * lax.axis_size("h") * lax.axis_size("y") * lax.axis_size("c")
    scale = float(count) ** (-0.5)
    band = lax.axis_index("b")
    core = lax.axis_index("c")

    flat = features.reshape(ROWS * COLS, CH)
    lab = labels.reshape(ROWS * COLS)

    def edge(rows, tags):
        tag = jnp.pad(tags.astype(BF16), (0, 16 * CH - 2 * COLS)).reshape(16, CH)
        return jnp.concatenate([rows, tag], axis=0)

    down = [(i, i + 1) for i in range(3)]
    up = [(i + 1, i) for i in range(3)]
    above = lax.ppermute(edge(flat[12 * COLS:], lab[14 * COLS:]), "b", down)
    below = lax.ppermute(edge(flat[:4 * COLS], lab[:2 * COLS]), "b", up)
    ext = jnp.concatenate([above[:4 * COLS], flat, below[:4 * COLS]], axis=0)

    def tags(block):
        return block[4 * COLS:].reshape(-1)[:2 * COLS].astype(jnp.int32)

    lab_ext = jnp.concatenate([tags(above), lab, tags(below)]).reshape(5, 1, 4 * COLS)
    own = jnp.pad(jnp.ones((ROWS * COLS,), F32), (2 * COLS, 2 * COLS)).reshape(5, 1, 4 * COLS)
    cls = jnp.pad(jnp.concatenate([classifier.T, classifier.T], axis=0), ((0, 10), (0, 0)))
    bias = jnp.broadcast_to(jnp.pad(class_bias, (0, 5))[:, None], (8, 128))

    def flipped(kernel):
        return jnp.transpose(kernel[::-1, ::-1], (0, 1, 3, 2)).reshape(9 * CH, CH)

    g1, g2, small, fg = main_call(
        band.reshape(1), ext, first_kernel.reshape(9 * CH, CH), second_kernel.reshape(9 * CH, CH),
        flipped(second_kernel), cls, bias, lab_ext, own, height, scale, r1=11, rt=6,
    )
    grad_features = feat_call(fg, flipped(first_kernel)).reshape(features.shape)

    keep = jnp.where(core == 0, g1, g2)
    give = jnp.where(core == 0, g2, g1)
    got = shift(jnp.concatenate([give, split_small(small)], axis=0), "c", 1, 2)
    total = (keep.astype(F32) + got[:9 * CH].astype(F32)).astype(BF16)
    small = small + join_small(got[9 * CH:])

    part = 9 * CH // 16
    spread = jnp.concatenate(
        [total.reshape(16, part, CH), jnp.broadcast_to(split_small(small), (16, 16, CH))], axis=1
    )
    spread = lax.all_to_all(spread, ("x", "y"), 0, 0, tiled=True)
    piece = jnp.sum(spread[:, :part].astype(F32), axis=0).astype(BF16)
    small = jnp.sum(join_small(spread[:, part:]), axis=0)

    for axis, size in (("b", 4), ("h", 2)):
        send = jnp.concatenate([piece, split_small(small)], axis=0)
        others = [shift(send, axis, k, size) for k in range(1, size)]
        wide = piece.astype(F32)
        for other in others:
            wide = wide + other[:part].astype(F32)
            small = small + join_small(other[part:])
        piece = wide.astype(BF16)

    full = lax.all_to_all(jnp.broadcast_to(piece, (16, part, CH)), ("x", "y"), 0, 0, tiled=True)
    mine = full.reshape(9 * CH, CH)
    other = shift(mine, "c", 1, 2)
    grad_first = jnp.where(core == 0, mine, other).astype(F32).reshape(3, 3, CH, CH)
    grad_second = jnp.where(core == 0, other, mine).astype(F32).reshape(3, 3, CH, CH)
    return (grad_features, grad_first, grad_second, small[0:3].T, small[3, 0:3])


def solution(mesh):
    fine = Mesh(mesh.devices.reshape(4, 4, 2, 4, 2), AXES)
    rail = ("x", "h", "y", "c")
    placed = (P(rail, "b", None, None), P(), P(), P(), P(), P(rail, "b", None))
    return jax.shard_map(
        per_device,
        mesh=fine,
        in_specs=placed,
        out_specs=(P(rail, "b", None, None), P(), P(), P(), P()),
        check_vma=False,
    )
```

time: 373 us -> 125 us (0.34)
  waiting for transfers between devices: 267 us -> 10.8 us
  blocking collectives: 0 us -> 44.5 us
  matrix products: 29.9 us -> 0 us
  Pallas kernels: 0 us -> 20.4 us
  local copies, waits for them, and re-layouts: 29.1 us -> 12.7 us
  between operations: 14.9 us -> 0.95 us
    psum x1 -> x0, waiting for transfers between devices: 263 us -> none  [reduce_bucket(): total = lax.psum(flat, ('band', 'rail'))]
    all_to_all x0 -> x2, blocking collectives: none -> 44.5 us  [the longest x1 24.7 us: per_device(): spread = lax.all_to_all(spread, ('x', 'y'), 0, 0, tiled=True)]
    pallas_call x0 -> x2, Pallas kernels: none -> 20.4 us  [the longest x1 17 us: main_call(): pl.pallas_call(make_main(height, scale, **kw), out_shape=(jax.ShapeDtypeS...]
    dot_general x21 -> x0, matrix products: 19.1 us -> none  [the longest x18 17 us: kernel_grad(): lax.dot_general(window, grad_rows, (((0,), (0,)), ((), ())), preferred_el...]
    conv_general_dilated x4 -> x0, matrix products: 10.8 us -> none  [convolve(): lax.conv_general_dilated(extended, kernel, (1, 1), ((0, 0), (1, 1)), dime...]
    unnamed x68 -> x22, local copies, waits for them, and re-layouts: 14.7 us -> 6.36 us
    ppermute x8, waiting for transfers between devices: 3.96 us -> 10.8 us  [the longest x6 10.3 us: shift(): lax.ppermute(value, axis, [(i, (i + step) % size) for i in range(size)])]
  transfers between devices with their start and end apart: 9 -> 8, of which waited for: 4 -> 5; matrix products, arithmetic and copies ran while one was open for 4% -> 4% of each run, Pallas kernels for 0% -> 3%
where the time goes in v1:
time: 125 us; the launch traced here: 124 us
  blocking collectives  44.5 us (36%)
  starting transfers between devices  26.2 us (21%)
  Pallas kernels  20.4 us (16%)
  local copies, waits for them, and re-layouts  12.7 us (10%)
  waiting for transfers between devices  10.8 us (9%)
  other arithmetic  8.79 us (7%)
    all_to_all x1, blocking collectives, per_device(): spread = lax.all_to_all(spread, ('x', 'y'), 0, 0, tiled=True)  24.7 us
    all_to_all x1, blocking collectives, per_device(): lax.all_to_all(jnp.broadcast_to(piece, (16, part, CH)), ('x', 'y'), 0, 0,...  19.8 us
    ppermute x6, starting transfers between devices, shift(): lax.ppermute(value, axis, [(i, (i + step) % size) for i in range(size)])  19.2 us
    pallas_call x1, Pallas kernels, main_call(): pl.pallas_call(make_main(height, scale, **kw), out_shape=(jax.ShapeDtypeS...  17 us
    ppermute x6, waiting for transfers between devices, shift(): lax.ppermute(value, axis, [(i, (i + step) % size) for i in range(size)])  10.3 us
    unnamed x22, local copies, waits for them, and re-layouts  6.36 us
    ppermute x1, starting transfers between devices, per_device(): above = lax.ppermute(edge(flat[12 * COLS:], lab[14 * COLS:]), 'b', down)  5.67 us
    pallas_call x1, Pallas kernels, feat_call(): pl.pallas_call(feat_kernel, out_shape=jax.ShapeDtypeStruct((ROWS * COLS,...  3.4 us
  transfers between devices with their start and end apart: 8, of which 5 were waited for; matrix products, arithmetic and copies ran while one was open for 4% of the time, Pallas kernels for 3%

profile of v1, /device:TPU:1, one launch (start us, length us, event | category | flops | bytes accessed | tf_op | source)
XLA Modules:
  0.0 124.2 jit_solution(8272270860464526855)
XLA Ops:
  0.7 0.8 convert.7
  1.6 1.0 fusion.12
  3.3 1.3 %collective-permute-start.1 = (bf16[400,256]{1,0:T(8,128)(2,1)}, bf16[400,256]{1,0:T(8,128)(2,1)}, u32[]{:S(2)}, u32[]{:S(2)}) collective-permute-start(bf16[400,256]{1,0:T(8,128)(2,1)} %pad_maximum_fusion.4), channel_id=1, source_target_pairs={{64,0},{128,64},{192,128},{65,1},{129,65},{193,129},{66,2},{130,66... | collective-permute-start | bytes 614408 | tf_op jit(solution)/shard_map/ppermute | solution.py:218
  5.4 5.7 %collective-permute-start = (bf16[400,256]{1,0:T(8,128)(2,1)}, bf16[400,256]{1,0:T(8,128)(2,1)}, u32[]{:S(2)}, u32[]{:S(2)}) collective-permute-start(bf16[400,256]{1,0:T(8,128)(2,1)} %pad_maximum_fusion.3), channel_id=1, source_target_pairs={{0,64},{64,128},{128,192},{1,65},{65,129},{129,193},{2,66},{66,130... | collective-permute-start | bytes 614408 | tf_op jit(solution)/shard_map/ppermute | solution.py:217
  14.2 0.9 slice.159
  15.2 0.9 slice.157
  16.3 1.1 copy-done.1
  17.4 17.0 %main.1 = (bf16[2304,256]{1,0:T(8,128)(2,1)S(1)}, bf16[2304,256]{1,0:T(8,128)(2,1)S(1)}, f32[8,256]{1,0:T(8,128)S(1)}, bf16[1728,768]{1,0:T(8,128)(2,1)S(1)}) custom-call(s32[1]{0:T(128)} %bitcast.band_ref, bf16[2304,256]{1,0:T(8,128)(2,1)S(1)} %pad_maximum_fusion.2.f_ref, bf16[2304,256]{1,0:T(8,128)(2,1)S(1)} %bitcast.33, bf16[2304,256]{1,0:T(8,128)(2,1)S(1)} %bitcast.32, ...), custom_call_target="tpu_custom_call" | custom-call | flops 11000000512 | bytes 8000000 | tf_op jit(solution)/shard_map/main/pallas_call | solution.py:138
  34.6 1.4 %copy-done.2 = bf16[1728,768]{1,0:T(8,128)(2,1)} copy-done((bf16[1728,768]{1,0:T(8,128)(2,1)}, bf16[1728,768]{1,0:T(8,128)(2,1)S(1)}, u32[]{:S(2)}) %copy-start.2) | copy-done | bytes 2654232
  36.0 3.5 %collective-permute-start.2 = (bf16[2320,256]{1,0:T(8,128)(2,1)S(1)}, bf16[2320,256]{1,0:T(8,128)(2,1)S(1)}, u32[]{:S(2)}, u32[]{:S(2)}) collective-permute-start(bf16[2320,256]{1,0:T(8,128)(2,1)S(1)} %pad_maximum_fusion.1), channel_id=1, source_target_pairs={{0,1},{1,0},{2,3},{3,2},{4,5},{5,4},{6,7},{7,6},{8,9},{9,8},{10,11... | collective-permute-start | bytes 3563528 | tf_op jit(solution)/shard_map/ppermute | solution.py:188
  39.5 2.5 %collective-permute-done.2 = bf16[2320,256]{1,0:T(8,128)(2,1)S(1)} collective-permute-done((bf16[2320,256]{1,0:T(8,128)(2,1)S(1)}, bf16[2320,256]{1,0:T(8,128)(2,1)S(1)}, u32[]{:S(2)}, u32[]{:S(2)}) %collective-permute-start.2) | collective-permute-done | bytes 1187872 | tf_op jit(solution)/shard_map/ppermute | solution.py:188
  42.6 24.7 %all_to_all.10 = bf16[16,160,256]{2,1,0:T(8,128)(2,1)S(1)} all-to-all(bf16[16,160,256]{2,1,0:T(8,128)(2,1)S(1)} %pad_maximum_fusion), channel_id=1, replica_groups=mesh['b'=4,'x'=4,'h'=2,'y'=4,'c'=2] {'x','y'}, dimensions={0} | all-to-all | bytes 2621440 | tf_op jit(solution)/shard_map/all_to_all | solution.py:248
  67.5 5.5 %collective-permute-start.5 = (bf16[160,256]{1,0:T(8,128)(2,1)S(1)}, bf16[160,256]{1,0:T(8,128)(2,1)S(1)}, u32[]{:S(2)}, u32[]{:S(2)}) collective-permute-start(bf16[160,256]{1,0:T(8,128)(2,1)S(1)} %pad_maximum_fusion.5), channel_id=1, source_target_pairs={{0,192},{64,0},{128,64},{192,128},{1,193},{65,1},{129,65},{193,129... | collective-permute-start | bytes 245768 | tf_op jit(solution)/shard_map/ppermute | solution.py:188
  73.4 1.1 collective-permute-done.5
  74.5 4.8 %collective-permute-done.4 = bf16[160,256]{1,0:T(8,128)(2,1)S(1)} collective-permute-done((bf16[160,256]{1,0:T(8,128)(2,1)S(1)}, bf16[160,256]{1,0:T(8,128)(2,1)S(1)}, u32[]{:S(2)}, u32[]{:S(2)}) %collective-permute-start.4) | collective-permute-done | bytes 81952 | tf_op jit(solution)/shard_map/ppermute | solution.py:188
  79.3 6.0 %collective-permute-start.6 = (bf16[160,256]{1,0:T(8,128)(2,1)S(1)}, bf16[160,256]{1,0:T(8,128)(2,1)S(1)}, u32[]{:S(2)}, u32[]{:S(2)}) collective-permute-start(bf16[160,256]{1,0:T(8,128)(2,1)S(1)} %pad_maximum_fusion.6), channel_id=1, source_target_pairs={{0,8},{8,0},{1,9},{9,1},{2,10},{10,2},{3,11},{11,3},{4,12},{12,4},... | collective-permute-start | bytes 245768 | tf_op jit(solution)/shard_map/ppermute | solution.py:188
  85.3 1.9 %collective-permute-done.6 = bf16[160,256]{1,0:T(8,128)(2,1)S(1)} collective-permute-done((bf16[160,256]{1,0:T(8,128)(2,1)S(1)}, bf16[160,256]{1,0:T(8,128)(2,1)S(1)}, u32[]{:S(2)}, u32[]{:S(2)}) %collective-permute-start.6) | collective-permute-done | bytes 81952 | tf_op jit(solution)/shard_map/ppermute | solution.py:188
  88.0 19.8 %all_to_all.11 = bf16[16,144,256]{2,1,0:T(8,128)(2,1)S(1)} all-to-all(bf16[16,144,256]{2,1,0:T(8,128)(2,1)S(1)} %broadcast_in_dim.18), channel_id=1, replica_groups=mesh['b'=4,'x'=4,'h'=2,'y'=4,'c'=2] {'x','y'}, dimensions={0} | all-to-all | bytes 2359296 | tf_op jit(solution)/shard_map/all_to_all | solution.py:261
  107.8 3.9 %collective-permute-start.7 = (bf16[2304,256]{1,0:T(8,128)(2,1)S(1)}, bf16[2304,256]{1,0:T(8,128)(2,1)}, u32[]{:S(2)}, u32[]{:S(2)}) collective-permute-start(bf16[2304,256]{1,0:T(8,128)(2,1)S(1)} %bitcast.38), channel_id=1, source_target_pairs={{0,1},{1,0},{2,3},{3,2},{4,5},{5,4},{6,7},{7,6},{8,9},{9,8},{10,11... | collective-permute-start | bytes 3538952 | tf_op jit(solution)/shard_map/ppermute | solution.py:188
  112.6 1.7 %copy-done.3 = bf16[1728,768]{1,0:T(8,128)(2,1)S(1)} copy-done((bf16[1728,768]{1,0:T(8,128)(2,1)S(1)}, bf16[1728,768]{1,0:T(8,128)(2,1)}, u32[]{:S(2)}) %copy-start.3) | copy-done | bytes 2654232
  114.3 3.4 %feat.1 = bf16[1536,256]{1,0:T(8,128)(2,1)} custom-call(bf16[1728,768]{1,0:T(8,128)(2,1)S(1)} %copy-done.3, bf16[2304,256]{1,0:T(8,128)(2,1)S(1)} %bitcast.35), custom_call_target="tpu_custom_call" | custom-call | flops 1800000000 | bytes 4000000 | tf_op jit(solution)/shard_map/feat/pallas_call | solution.py:173
  119.6 1.4 %broadcast_select_fusion = (bf16[2304,256]{1,0:T(8,128)(2,1)S(1)}, bf16[2304,256]{1,0:T(8,128)(2,1)S(1)}) fusion(bf16[2304,256]{1,0:T(8,128)(2,1)} %collective-permute-done.7, pred[]{:T(512)S(6)} %eq.2, bf16[16,144,256]{2,1,0:T(8,128)(2,1)S(1)} %all_to_all.11), kind=kLoop, calls=%fused_computation.7 | loop fusion | flops 1179648 | bytes 4718593 | tf_op jit(solution)/shard_map/jit(_where)/select_n | solution.py:265
  121.0 1.6 %convert.8 = f32[3,3,256,256]{3,2,1,0:T(8,128)} convert(bf16[3,3,256,256]{3,2,1,0:T(8,128)(2,1)S(1)} %bitcast.37) | non-fusion elementwise | flops 589824 | bytes 3538944 | tf_op jit(solution)/shard_map/reshape | solution.py:264
  122.6 1.6 %convert.9 = f32[3,3,256,256]{3,2,1,0:T(8,128)} convert(bf16[3,3,256,256]{3,2,1,0:T(8,128)(2,1)S(1)} %bitcast.36) | non-fusion elementwise | flops 589824 | bytes 3538944 | tf_op jit(solution)/shard_map/reshape | solution.py:265
  (75 shorter events, 9.7 us)
Async XLA Ops:
  0.6 10.4 %copy-start.6 = (s32[1,16,96]{2,1,0:T(8,128)S(1)}, s32[1,16,96]{2,1,0:T(8,128)}, u32[]{:S(2)}) copy-start(s32[1,16,96]{2,1,0:T(8,128)} %param.11) | copy-start | bytes 18436
  0.6 10.5 %copy-start = (bf16[3,3,256,256]{3,2,1,0:T(8,128)(2,1)S(1)}, bf16[3,3,256,256]{3,2,1,0:T(8,128)(2,1)}, u32[]{:S(2)}) copy-start(bf16[3,3,256,256]{3,2,1,0:T(8,128)(2,1)} %param.8) | copy-start | bytes 3538948
  3.3 8.8 %collective-permute-start.1 = (bf16[400,256]{1,0:T(8,128)(2,1)}, bf16[400,256]{1,0:T(8,128)(2,1)}, u32[]{:S(2)}, u32[]{:S(2)}) collective-permute-start(bf16[400,256]{1,0:T(8,128)(2,1)} %pad_maximum_fusion.4), channel_id=1, source_target_pairs={{64,0},{128,64},{192,128},{65,1},{129,65},{193,129},{66,2},{130,66... | collective-permute-start | bytes 614408 | tf_op jit(solution)/shard_map/ppermute | solution.py:218
  5.4 8.0 %collective-permute-start = (bf16[400,256]{1,0:T(8,128)(2,1)}, bf16[400,256]{1,0:T(8,128)(2,1)}, u32[]{:S(2)}, u32[]{:S(2)}) collective-permute-start(bf16[400,256]{1,0:T(8,128)(2,1)} %pad_maximum_fusion.3), channel_id=1, source_target_pairs={{0,64},{64,128},{128,192},{1,65},{65,129},{129,193},{2,66},{66,130... | collective-permute-start | bytes 614408 | tf_op jit(solution)/shard_map/ppermute | solution.py:217
  11.2 0.8 copy-start.8
  11.2 0.9 copy-start.7
  12.0 4.1 %copy-start.4 = (bf16[1,16,96,256]{3,2,1,0:T(8,128)(2,1)S(1)}, bf16[1,16,96,256]{3,2,1,0:T(8,128)(2,1)}, u32[]{:S(2)}) copy-start(bf16[1,16,96,256]{3,2,1,0:T(8,128)(2,1)} %param.6) | copy-start | bytes 2359300
  16.1 1.3 %copy-start.1 = (bf16[3,3,256,256]{3,2,1,0:T(8,128)(2,1)S(1)}, bf16[3,3,256,256]{3,2,1,0:T(8,128)(2,1)}, u32[]{:S(2)}) copy-start(bf16[3,3,256,256]{3,2,1,0:T(8,128)(2,1)} %param.7) | copy-start | bytes 3538948
  34.4 1.5 %copy-start.2 = (bf16[1728,768]{1,0:T(8,128)(2,1)}, bf16[1728,768]{1,0:T(8,128)(2,1)S(1)}, u32[]{:S(2)}) copy-start(bf16[1728,768]{1,0:T(8,128)(2,1)S(1)} %get-tuple-element.9.fg) | copy-start | bytes 7962628
  36.0 5.9 %collective-permute-start.2 = (bf16[2320,256]{1,0:T(8,128)(2,1)S(1)}, bf16[2320,256]{1,0:T(8,128)(2,1)S(1)}, u32[]{:S(2)}, u32[]{:S(2)}) collective-permute-start(bf16[2320,256]{1,0:T(8,128)(2,1)S(1)} %pad_maximum_fusion.1), channel_id=1, source_target_pairs={{0,1},{1,0},{2,3},{3,2},{4,5},{5,4},{6,7},{7,6},{8,9},{9,8},{10,11... | collective-permute-start | bytes 3563528 | tf_op jit(solution)/shard_map/ppermute | solution.py:188
  67.5 6.9 %collective-permute-start.5 = (bf16[160,256]{1,0:T(8,128)(2,1)S(1)}, bf16[160,256]{1,0:T(8,128)(2,1)S(1)}, u32[]{:S(2)}, u32[]{:S(2)}) collective-permute-start(bf16[160,256]{1,0:T(8,128)(2,1)S(1)} %pad_maximum_fusion.5), channel_id=1, source_target_pairs={{0,192},{64,0},{128,64},{192,128},{1,193},{65,1},{129,65},{193,129... | collective-permute-start | bytes 245768 | tf_op jit(solution)/shard_map/ppermute | solution.py:188
  73.0 6.3 %collective-permute-start.4 = (bf16[160,256]{1,0:T(8,128)(2,1)S(1)}, bf16[160,256]{1,0:T(8,128)(2,1)S(1)}, u32[]{:S(2)}, u32[]{:S(2)}) collective-permute-start(bf16[160,256]{1,0:T(8,128)(2,1)S(1)} %pad_maximum_fusion.5), channel_id=1, source_target_pairs={{0,128},{64,192},{128,0},{192,64},{1,129},{65,193},{129,1},{193,65... | collective-permute-start | bytes 245768 | tf_op jit(solution)/shard_map/ppermute | solution.py:188
  73.0 6.3 %collective-permute-start.3 = (bf16[160,256]{1,0:T(8,128)(2,1)S(1)}, bf16[160,256]{1,0:T(8,128)(2,1)S(1)}, u32[]{:S(2)}, u32[]{:S(2)}) collective-permute-start(bf16[160,256]{1,0:T(8,128)(2,1)S(1)} %pad_maximum_fusion.5), channel_id=1, source_target_pairs={{0,64},{64,128},{128,192},{192,0},{1,65},{65,129},{129,193},{193,1... | collective-permute-start | bytes 245768 | tf_op jit(solution)/shard_map/ppermute | solution.py:188
  79.3 7.9 %collective-permute-start.6 = (bf16[160,256]{1,0:T(8,128)(2,1)S(1)}, bf16[160,256]{1,0:T(8,128)(2,1)S(1)}, u32[]{:S(2)}, u32[]{:S(2)}) collective-permute-start(bf16[160,256]{1,0:T(8,128)(2,1)S(1)} %pad_maximum_fusion.6), channel_id=1, source_target_pairs={{0,8},{8,0},{1,9},{9,1},{2,10},{10,2},{3,11},{11,3},{4,12},{12,4},... | collective-permute-start | bytes 245768 | tf_op jit(solution)/shard_map/ppermute | solution.py:188
  87.3 0.6 copy-start.5
  107.8 11.7 %collective-permute-start.7 = (bf16[2304,256]{1,0:T(8,128)(2,1)S(1)}, bf16[2304,256]{1,0:T(8,128)(2,1)}, u32[]{:S(2)}, u32[]{:S(2)}) collective-permute-start(bf16[2304,256]{1,0:T(8,128)(2,1)S(1)} %bitcast.38), channel_id=1, source_target_pairs={{0,1},{1,0},{2,3},{3,2},{4,5},{5,4},{6,7},{7,6},{8,9},{9,8},{10,11... | collective-permute-start | bytes 3538952 | tf_op jit(solution)/shard_map/ppermute | solution.py:188
  112.6 1.8 %copy-start.3 = (bf16[1728,768]{1,0:T(8,128)(2,1)S(1)}, bf16[1728,768]{1,0:T(8,128)(2,1)}, u32[]{:S(2)}) copy-start(bf16[1728,768]{1,0:T(8,128)(2,1)} %copy-done.2) | copy-start | bytes 7962628

commit v2 on v1

v2 whole, which is shorter than its diff:
```python
import jax
import jax.numpy as jnp
from jax import lax
from jax.experimental import pallas as pl
from jax.experimental.pallas import tpu as pltpu
from jax.sharding import Mesh, PartitionSpec as P

ROWS = 16
COLS = 96
CH = 256
HALO = 4
PIX = ROWS * COLS
EDGE = HALO * COLS
BLOCK = EDGE + 16
F32 = jnp.float32
BF16 = jnp.bfloat16
ROWWISE = (((0,), (0,)), ((), ()))
VMEM = pl.BlockSpec(memory_space=pltpu.VMEM)
SMEM = pl.BlockSpec(memory_space=pltpu.SMEM)
AXES = ("b", "x", "h", "y", "c")


def call(kernel, outs, args, scratch=(), limit=24, flops=0, name=None, scalars=0, out_specs=None):
    moved = sum(a.size * a.dtype.itemsize for a in args)
    shapes = tuple(jax.ShapeDtypeStruct(s, d) for s, d in outs)
    return pl.pallas_call(
        kernel,
        out_shape=shapes,
        in_specs=[SMEM] * scalars + [VMEM] * (len(args) - scalars),
        out_specs=(VMEM,) * len(outs) if out_specs is None else out_specs,
        scratch_shapes=list(scratch),
        compiler_params=pltpu.CompilerParams(vmem_limit_bytes=limit * 1024 * 1024),
        cost_estimate=pl.CostEstimate(flops=flops, bytes_accessed=moved, transcendentals=0),
        name=name,
    )(*args)


def conv_rows(wide, start, count, kernel):
    patch = jnp.concatenate(
        [wide[pl.ds(pl.multiple_of(start + a * COLS, COLS), count * COLS), :] for a in range(3)],
        axis=1,
    )
    out = jnp.dot(patch, kernel[...], preferred_element_type=F32)
    return out.reshape(count, COLS, CH)


def store_wide(wide, start, rows):
    count = rows.shape[0]
    col = lax.broadcasted_iota(jnp.int32, rows.shape, 1)
    left = jnp.where(col == 0, 0.0, pltpu.roll(rows, 1, 1))
    right = jnp.where(col == COLS - 1, 0.0, pltpu.roll(rows, COLS - 1, 1))
    at = pl.ds(pl.multiple_of(start, COLS), count * COLS)
    wide[at, 0:CH] = left.astype(BF16).reshape(count * COLS, CH)
    wide[at, CH:2 * CH] = rows.astype(BF16).reshape(count * COLS, CH)
    wide[at, 2 * CH:3 * CH] = right.astype(BF16).reshape(count * COLS, CH)


def load_rows(ref, start, count):
    at = pl.ds(pl.multiple_of(start, COLS), count * COLS)
    return ref[at, :].astype(F32).reshape(count, COLS, CH)


def sigmoid(value):
    return 0.5 * jnp.tanh(0.5 * value) + 0.5


def keep_rows(rows, first, height):
    parts = []
    for r in range(rows.shape[0]):
        inside = jnp.logical_and(first + r >= 0, first + r < height)
        parts.append(rows[r] * jnp.where(inside, 1.0, 0.0))
    return jnp.stack(parts)


def edge_kernel(f, lab, up, down, tag):
    for out, row, label in ((up, 0, 0), (down, ROWS - HALO, ROWS - 2)):
        out[0:EDGE, :] = f[row * COLS:(row + HALO) * COLS, :]
        tag[...] = jnp.zeros_like(tag)
        tag[0:2, 0:COLS] = lab[label:label + 2, :].astype(F32)
        out[EDGE:BLOCK, :] = tag[...].astype(BF16)


def inner_kernel(f, k1, k2, fw, aw, slope, k1t, k2t):
    def widen(t, c):
        store_wide(fw, t * (2 * COLS), load_rows(f, t * (2 * COLS), 2))
        return c

    lax.fori_loop(0, 8, widen, 0)

    def first(t, c):
        at = t * (7 * COLS)
        v = conv_rows(fw, at, 7, k1)
        s = sigmoid(v)
        rows = pl.ds(pl.multiple_of(at, COLS), 7 * COLS)
        slope[rows, :] = (s * (1.0 + v * (1.0 - s))).reshape(7 * COLS, CH)
        store_wide(aw, at, v * s)
        return c

    lax.fori_loop(0, 2, first, 0)

    for t in range(9):
        for src, dst in ((k1, k1t), (k2, k2t)):
            dst[t * CH:(t + 1) * CH, :] = src[(8 - t) * CH:(9 - t) * CH, :].T


def make_main(height, scale):
    def main(ids, above, below, fwi, awi, slopei, k1, k2, k2t, cls, bias, lab, g1, g2, small, fg,
             fw, aw, sw, fgw, gt, slope, labs):
        base = ids[0] * ROWS
        fw[EDGE:EDGE + PIX, :] = fwi[...]
        for half in range(2):
            at = half * 2 * COLS
            rows = keep_rows(load_rows(above, at, 2), base - HALO + half * 2, height)
            store_wide(fw, at, rows)
            rows = keep_rows(load_rows(below, at, 2), base + ROWS + half * 2, height)
            store_wide(fw, EDGE + PIX + at, rows)
        aw[4 * COLS:18 * COLS, :] = awi[...]
        slope[4 * COLS:18 * COLS, :] = slopei[...]

        tags = [above[EDGE:BLOCK, :].astype(F32), below[EDGE:BLOCK, :].astype(F32)]
        mine = lab[...].astype(F32)
        lines = [tags[0][0:1, 0:COLS], tags[0][1:2, 0:COLS]]
        lines += [mine[r:r + 1, :] for r in range(ROWS)]
        lines += [tags[1][0:1, 0:COLS], tags[1][1:2, 0:COLS]]
        for r, line in enumerate(lines):
            labs[r // 10, 0:1, (r % 10) * COLS:(r % 10 + 1) * COLS] = line

        def first(t, c):
            at = t * (18 * COLS)
            v = conv_rows(fw, at, 4, k1)
            s = sigmoid(v)
            rows = pl.ds(pl.multiple_of(at, COLS), 4 * COLS)
            slope[rows, :] = (s * (1.0 + v * (1.0 - s))).reshape(4 * COLS, CH)
            store_wide(aw, at, keep_rows(v * s, base - 3 + t * 18, height))
            return c

        lax.fori_loop(0, 2, first, 0)

        small[...] = jnp.zeros_like(small)
        lane = lax.broadcasted_iota(jnp.int32, (1, CH), 1)
        pixel = lax.broadcasted_iota(jnp.int32, (1, 10 * COLS), 1)

        def second(t, c):
            at = t * (10 * COLS)
            v = conv_rows(aw, at, 10, k2)
            s = sigmoid(v)
            act = (v * s).astype(BF16).reshape(10 * COLS, CH)
            logit = lax.dot_general(
                cls[...], act, (((1,), (1,)), ((), ())), preferred_element_type=F32
            )
            rows = [logit[k:k + 1, :] + bias[k:k + 1, 0:1] for k in range(3)]
            top = jnp.maximum(jnp.maximum(rows[0], rows[1]), rows[2])
            ex = [jnp.exp(row - top) for row in rows]
            den = ex[0] + ex[1] + ex[2]
            label = labs[t][0:1, 0:10 * COLS]
            place = pixel + at
            own = jnp.where(jnp.logical_and(place >= 2 * COLS, place < 18 * COLS), 1.0, 0.0)
            dl = [(ex[k] / den - jnp.where(label == k, 1.0, 0.0)) * scale for k in range(3)]
            hi = [d.astype(BF16).astype(F32) for d in dl]
            lo = [d - h for d, h in zip(dl, hi)]
            zero = jnp.zeros((10, 10 * COLS), F32)
            pack = jnp.concatenate(hi + lo + [zero], axis=0)
            back = lax.dot_general(pack.astype(BF16), cls[...], ROWWISE, preferred_element_type=F32)
            grad = back.reshape(10, COLS, CH) * (s * (1.0 + v * (1.0 - s)))
            store_wide(sw, at, keep_rows(grad, base - 2 + t * 10, height))
            part = jnp.dot((pack * own).astype(BF16), act, preferred_element_type=F32)
            sums = [jnp.sum(d * own, axis=1, keepdims=True) for d in dl]
            row = jnp.where(lane == 0, sums[0], jnp.where(lane == 1, sums[1], 0.0))
            small[0:3, :] += part[0:3] + part[3:6]
            small[3:4, :] += jnp.where(lane == 2, sums[2], row)
            return c

        lax.fori_loop(0, 2, second, 0)

        def weight(grad_wide, skip, src, src_skip, out):
            gt[...] = grad_wide[skip * COLS:(skip + ROWS) * COLS, CH:2 * CH].T
            for a in range(3):
                win = src[(src_skip + a) * COLS:(src_skip + a + ROWS) * COLS, :]
                res = jnp.dot(gt[...], win, preferred_element_type=F32)
                for b in range(3):
                    out[(3 * a + b) * CH:(3 * a + b + 1) * CH, :] = (
                        res[:, b * CH:(b + 1) * CH].T.astype(BF16)
                    )

        weight(sw, 2, aw, 2, g2)

        def third(t, c):
            at = t * (6 * COLS)
            v = conv_rows(sw, at, 6, k2t)
            sl = slope[pl.ds(pl.multiple_of(at + 2 * COLS, COLS), 6 * COLS), :]
            g = keep_rows(v * sl.reshape(6, COLS, CH), base - 1 + t * 6, height)
            store_wide(fgw, at, g)
            return c

        lax.fori_loop(0, 3, third, 0)
        weight(fgw, 1, fw, 3, g1)
        fg[...] = fgw[:, CH:2 * CH]

    return main


def feature_kernel(fg, k1t, out, fgw):
    def widen(t, c):
        store_wide(fgw, t * (2 * COLS), load_rows(fg, t * (2 * COLS), 2))
        return c

    lax.fori_loop(0, 9, widen, 0)

    def step(t, c):
        at = t * (8 * COLS)
        v = conv_rows(fgw, at, 8, k1t)
        out[pl.ds(pl.multiple_of(at, COLS), 8 * COLS), :] = v.astype(BF16).reshape(8 * COLS, CH)
        return c

    lax.fori_loop(0, 2, step, 0)


def final_kernel(ids, mine, other, g1, g2, wide, sems):
    copies = []
    for t in range(3):
        at = pl.ds(t * 768, 768)
        for k, block in enumerate((mine, other)):
            wide[k, at, :] = block[at, :].astype(F32)
        for k, out in enumerate((g1, g2)):
            slot = ids[1] if k == 0 else 1 - ids[1]
            copy = pltpu.make_async_copy(wide.at[slot, at], out.at[at], sems.at[k, t])
            copy.start()
            copies.append(copy)
    for copy in copies:
        copy.wait()


def ring(step):
    def place(z):
        return (z % 4) * 2 + z // 4

    return [(place(z), place((z + step) % 8)) for z in range(8)]


def shift(value, axis, step, size):
    return lax.ppermute(value, axis, [(i, (i + step) % size) for i in range(size)])


def split_small(small):
    hi = small.astype(BF16)
    return jnp.concatenate([hi, (small - hi.astype(F32)).astype(BF16)], axis=0)


def join_small(rows):
    full = rows.astype(F32)
    return full[..., 0:8, :] + full[..., 8:16, :]


def per_device(features, first_kernel, second_kernel, classifier, class_bias, labels):
    height = ROWS * lax.axis_size("b")
    count = height * COLS * lax.axis_size("x") * lax.axis_size("h") * lax.axis_size("y") * lax.axis_size("c")
    scale = float(count) ** (-0.5)
    band = lax.axis_index("b")
    core = lax.axis_index("c")
    ids = jnp.stack([band, core])

    flat = features.reshape(PIX, CH)
    lab = labels.reshape(ROWS, COLS)
    k1 = first_kernel.reshape(9 * CH, CH)
    k2 = second_kernel.reshape(9 * CH, CH)
    up, down = call(
        edge_kernel, [((BLOCK, CH), BF16)] * 2, (flat, lab),
        [pltpu.VMEM((16, CH), F32)], limit=8, name="edge",
    )
    above = lax.ppermute(down, ("b", "h"), ring(1))
    below = lax.ppermute(up, ("b", "h"), ring(7))

    fwi, awi, slopei, k1t, k2t = call(
        inner_kernel,
        [((PIX, 3 * CH), BF16), ((14 * COLS, 3 * CH), BF16), ((14 * COLS, CH), F32),
         ((9 * CH, CH), BF16), ((9 * CH, CH), BF16)],
        (flat, k1, k2), flops=5_000_000_000, name="inner",
    )

    cls = jnp.pad(jnp.concatenate([classifier.T, classifier.T], axis=0), ((0, 10), (0, 0)))
    bias = jnp.broadcast_to(jnp.pad(class_bias, (0, 5))[:, None], (8, 128))
    g1, g2, small, fg = call(
        make_main(height, scale),
        [((9 * CH, CH), BF16), ((9 * CH, CH), BF16), ((8, CH), F32), ((18 * COLS, CH), BF16)],
        (ids, above, below, fwi, awi, slopei, k1, k2, k2t, cls, bias, lab),
        [
            pltpu.VMEM((24 * COLS, 3 * CH), BF16),
            pltpu.VMEM((22 * COLS, 3 * CH), BF16),
            pltpu.VMEM((20 * COLS, 3 * CH), BF16),
            pltpu.VMEM((18 * COLS, 3 * CH), BF16),
            pltpu.VMEM((CH, PIX), BF16),
            pltpu.VMEM((22 * COLS, CH), F32),
            pltpu.VMEM((2, 8, 1024), F32),
        ],
        limit=40, flops=9_000_000_000, name="main", scalars=1,
    )
    (grad_features,) = call(
        feature_kernel, [((PIX, CH), BF16)], (fg, k1t),
        [pltpu.VMEM((18 * COLS, 3 * CH), BF16)], limit=16, flops=2_500_000_000, name="feature",
    )

    keep = jnp.where(core == 0, g1, g2)
    give = jnp.where(core == 0, g2, g1)
    got = shift(jnp.concatenate([give, split_small(small)], axis=0), "c", 1, 2)
    total = (keep.astype(F32) + got[:9 * CH].astype(F32)).astype(BF16)
    small = small + join_small(got[9 * CH:])

    part = 9 * CH // 16
    spread = jnp.concatenate(
        [total.reshape(16, part, CH), jnp.broadcast_to(split_small(small), (16, 16, CH))], axis=1
    )
    spread = lax.all_to_all(spread, ("x", "y"), 0, 0, tiled=True)
    piece = jnp.sum(spread[:, :part].astype(F32), axis=0).astype(BF16)
    small = jnp.sum(join_small(spread[:, part:]), axis=0)

    pair = [(0, 1), (1, 0), (2, 3), (3, 2)]
    for moves in ((("b", pair),), tuple((("b", "h"), ring(k)) for k in (2, 6, 4))):
        send = jnp.concatenate([piece, split_small(small)], axis=0)
        others = [lax.ppermute(send, axis, move) for axis, move in moves]
        wide = piece.astype(F32)
        for other in others:
            wide = wide + other[:part].astype(F32)
            small = small + join_small(other[part:])
        piece = wide.astype(BF16)

    full = lax.all_to_all(jnp.broadcast_to(piece, (16, part, CH)), ("x", "y"), 0, 0, tiled=True)
    mine = full.reshape(9 * CH, CH)
    other = shift(mine, "c", 1, 2)
    hbm = pl.BlockSpec(memory_space=pl.ANY)
    grad_first, grad_second = call(
        final_kernel, [((9 * CH, CH), F32)] * 2, (ids, mine, other),
        [pltpu.VMEM((2, 9 * CH, CH), F32), pltpu.SemaphoreType.DMA((2, 3))],
        limit=16, name="final", scalars=1, out_specs=(hbm, hbm),
    )
    shape = (3, 3, CH, CH)
    return (
        grad_features.reshape(features.shape), grad_first.reshape(shape), grad_second.reshape(shape),
        small[0:3].T, small[3, 0:3],
    )


def solution(mesh):
    fine = Mesh(mesh.devices.reshape(4, 4, 2, 4, 2), AXES)
    rail = ("x", "h", "y", "c")
    placed = (P(rail, "b", None, None), P(), P(), P(), P(), P(rail, "b", None))
    return jax.shard_map(
        per_device,
        mesh=fine,
        in_specs=placed,
        out_specs=(P(rail, "b", None, None), P(), P(), P(), P()),
        check_vma=False,
    )
```

time: 125 us -> 105 us (0.84)
  blocking collectives: 44.5 us -> 25.5 us
  waiting for transfers between devices: 10.8 us -> 20.3 us
  other arithmetic: 8.79 us -> 1.27 us
  local copies, waits for them, and re-layouts: 12.7 us -> 8.45 us
  Pallas kernels: 20.4 us -> 23.5 us
  starting transfers between devices: 26.2 us -> 24.4 us
    all_to_all x1 -> x0, blocking collectives: 19.8 us -> none  [per_device(): lax.all_to_all(jnp.broadcast_to(piece, (16, part, CH)), ('x', 'y'), 0, 0,...]
    ppermute x6 -> x2, starting transfers between devices: 19.2 us -> 7.38 us  [shift(): lax.ppermute(value, axis, [(i, (i + step) % size) for i in range(size)])]
    all_to_all x0 -> x1, waiting for transfers between devices: none -> 9.75 us  [per_device(): lax.all_to_all(jnp.broadcast_to(piece, (16, part, CH)), ('x', 'y'), 0, 0,...]
    ppermute x6 -> x2, waiting for transfers between devices: 10.3 us -> 3.82 us  [shift(): lax.ppermute(value, axis, [(i, (i + step) % size) for i in range(size)])]
    ppermute x2 -> x6, starting transfers between devices: 6.95 us -> 13.3 us  [the longest x4 6.74 us: per_device(): others = [lax.ppermute(send, axis, move) for axis, move in moves]]
    ppermute x2 -> x6, waiting for transfers between devices: 0.45 us -> 6.74 us  [the longest x4 6.73 us: per_device(): others = [lax.ppermute(send, axis, move) for axis, move in moves]]
    all_to_all x0 -> x1, starting transfers between devices: none -> 3.7 us  [per_device(): lax.all_to_all(jnp.broadcast_to(piece, (16, part, CH)), ('x', 'y'), 0, 0,...]
    reshape x2 -> x0, other arithmetic: 3.26 us -> none  [the longest x1 1.63 us: per_device(): jnp.where(core == 0, mine, other).astype(F32).reshape(3, 3, CH, CH)]
  transfers between devices with their start and end apart: 8 -> 9, of which waited for: 5 -> 7; matrix products, arithmetic and copies ran while one was open for 4% -> 2% of each run, Pallas kernels for 3% -> 7%
where the time goes in v2:
time: 105 us; the launch traced here: 104 us
  blocking collectives  25.5 us (24%)
  starting transfers between devices  24.4 us (23%)
  Pallas kernels  23.5 us (22%)
  waiting for transfers between devices  20.3 us (19%)
  local copies, waits for them, and re-layouts  8.45 us (8%)
  other arithmetic  1.27 us (1%)
    all_to_all x1, blocking collectives, per_device(): spread = lax.all_to_all(spread, ('x', 'y'), 0, 0, tiled=True)  25.5 us
    pallas_call x5, Pallas kernels, call(): pl.pallas_call(kernel, out_shape=shapes, in_specs=[SMEM] * scalars + [VME...  23.5 us
    all_to_all x1, waiting for transfers between devices, per_device(): lax.all_to_all(jnp.broadcast_to(piece, (16, part, CH)), ('x', 'y'), 0, 0,...  9.75 us
    ppermute x2, starting transfers between devices, shift(): lax.ppermute(value, axis, [(i, (i + step) % size) for i in range(size)])  7.38 us
    ppermute x4, starting transfers between devices, per_device(): others = [lax.ppermute(send, axis, move) for axis, move in moves]  6.74 us
    ppermute x4, waiting for transfers between devices, per_device(): others = [lax.ppermute(send, axis, move) for axis, move in moves]  6.73 us
    unnamed x18, local copies, waits for them, and re-layouts  5.51 us
    ppermute x1, starting transfers between devices, per_device(): below = lax.ppermute(up, ('b', 'h'), ring(7))  4.03 us
  transfers between devices with their start and end apart: 9, of which 7 were waited for; matrix products, arithmetic and copies ran while one was open for 2% of the time, Pallas kernels for 7%

profile of v2, /device:TPU:1, one launch (start us, length us, event | category | flops | bytes accessed | tf_op | source)
XLA Modules:
  0.0 104.4 jit_solution(14829298021194765012)
XLA Ops:
  0.6 1.1 %copy-done = bf16[1,16,96,256]{3,2,1,0:T(8,128)(2,1)S(1)} copy-done((bf16[1,16,96,256]{3,2,1,0:T(8,128)(2,1)S(1)}, bf16[1,16,96,256]{3,2,1,0:T(8,128)(2,1)}, u32[]{:S(2)}) %copy-start) | copy-done | bytes 786456
  1.8 0.7 copy-done.2
  2.5 2.5 %collective-permute-start = (bf16[400,256]{1,0:T(8,128)(2,1)S(1)}, bf16[400,256]{1,0:T(8,128)(2,1)S(1)}, u32[]{:S(2)}, u32[]{:S(2)}) collective-permute-start(bf16[400,256]{1,0:T(8,128)(2,1)S(1)} %get-tuple-element.18), channel_id=1, source_target_pairs={{0,64},{64,128},{128,192},{192,8},{8,72},{72,136},{136,200},{200,0... | collective-permute-start | bytes 614408 | tf_op jit(solution)/shard_map/ppermute | solution.py:270
  5.0 4.0 %collective-permute-start.1 = (bf16[400,256]{1,0:T(8,128)(2,1)S(1)}, bf16[400,256]{1,0:T(8,128)(2,1)S(1)}, u32[]{:S(2)}, u32[]{:S(2)}) collective-permute-start(bf16[400,256]{1,0:T(8,128)(2,1)S(1)} %get-tuple-element.19), channel_id=1, source_target_pairs={{0,200},{64,0},{128,64},{192,128},{8,192},{72,8},{136,72},{200,136... | collective-permute-start | bytes 614408 | tf_op jit(solution)/shard_map/ppermute | solution.py:271
  9.1 0.7 pad.9
  9.7 1.1 %copy-done.1 = bf16[1,16,96,256]{3,2,1,0:T(8,128)(2,1)S(1)} copy-done((bf16[1,16,96,256]{3,2,1,0:T(8,128)(2,1)S(1)}, bf16[1,16,96,256]{3,2,1,0:T(8,128)(2,1)}, u32[]{:S(2)}) %copy-start.1) | copy-done | bytes 786456
  10.9 1.3 %copy-done.4 = bf16[3,3,256,256]{3,2,1,0:T(8,128)(2,1)S(1)} copy-done((bf16[3,3,256,256]{3,2,1,0:T(8,128)(2,1)S(1)}, bf16[3,3,256,256]{3,2,1,0:T(8,128)(2,1)}, u32[]{:S(2)}) %copy-start.4) | copy-done | bytes 1179672
  12.1 1.3 %copy-done.6 = bf16[3,3,256,256]{3,2,1,0:T(8,128)(2,1)S(1)} copy-done((bf16[3,3,256,256]{3,2,1,0:T(8,128)(2,1)S(1)}, bf16[3,3,256,256]{3,2,1,0:T(8,128)(2,1)}, u32[]{:S(2)}) %copy-start.6) | copy-done | bytes 1179672
  13.4 3.4 %inner.1 = (bf16[1536,768]{1,0:T(8,128)(2,1)S(1)}, bf16[1344,768]{1,0:T(8,128)(2,1)S(1)}, f32[1344,256]{1,0:T(8,128)S(1)}, bf16[2304,256]{1,0:T(8,128)(2,1)S(1)}, bf16[2304,256]{1,0:T(8,128)(2,1)S(1)}) custom-call(bf16[1536,256]{1,0:T(8,128)(2,1)S(1)} %bitcast.19, bf16[2304,256]{1,0:T(8,128)(2,1)S(1)} %bitcast.22, bf16[2304,256]{1,0:T(8,128)(2,1)S(1)} %bitcast.24), custom_call_target="tpu_custom_call" | custom-call | flops 5000000000 | bytes 3145728 | tf_op jit(solution)/shard_map/inner/pallas_call | solution.py:26
  17.0 13.8 %main.1 = (bf16[2304,256]{1,0:T(8,128)(2,1)S(1)}, bf16[2304,256]{1,0:T(8,128)(2,1)S(1)}, f32[8,256]{1,0:T(8,128)S(1)}, bf16[1728,256]{1,0:T(8,128)(2,1)S(1)}) custom-call(s32[2]{0:T(128)S(1)} %pad_add_fusion.ids, bf16[400,256]{1,0:T(8,128)(2,1)S(1)} %collective-permute-done.above, bf16[400,256]{1,0:T(8,128)(2,1)S(1)} %collective-permute-done.1.below, ...), custom_call_target="tpu_custom_call" | custom-call | flops 8999999488 | bytes 9766920 | tf_op jit(solution)/shard_map/main/pallas_call | solution.py:26
  31.0 1.0 collective-permute-start.2
  32.0 2.5 %collective-permute-done.2 = bf16[2320,256]{1,0:T(8,128)(2,1)S(1)} collective-permute-done((bf16[2320,256]{1,0:T(8,128)(2,1)S(1)}, bf16[2320,256]{1,0:T(8,128)(2,1)S(1)}, u32[]{:S(2)}, u32[]{:S(2)}) %collective-permute-start.2) | collective-permute-done | bytes 1187872 | tf_op jit(solution)/shard_map/ppermute | solution.py:241
  35.2 25.5 %all_to_all.10 = bf16[16,160,256]{2,1,0:T(8,128)(2,1)S(1)} all-to-all(bf16[16,160,256]{2,1,0:T(8,128)(2,1)S(1)} %pad_maximum_fusion), channel_id=1, replica_groups=mesh['b'=4,'x'=4,'h'=2,'y'=4,'c'=2] {'x','y'}, dimensions={0} | all-to-all | bytes 2621440 | tf_op jit(solution)/shard_map/all_to_all | solution.py:312
  61.0 3.3 %collective-permute-done.3 = bf16[160,256]{1,0:T(8,128)(2,1)S(1)} collective-permute-done((bf16[160,256]{1,0:T(8,128)(2,1)S(1)}, bf16[160,256]{1,0:T(8,128)(2,1)S(1)}, u32[]{:S(2)}, u32[]{:S(2)}) %collective-permute-start.3) | collective-permute-done | bytes 81952 | tf_op jit(solution)/shard_map/ppermute | solution.py:319
  64.4 4.3 %collective-permute-start.6 = (bf16[160,256]{1,0:T(8,128)(2,1)S(1)}, bf16[160,256]{1,0:T(8,128)(2,1)S(1)}, u32[]{:S(2)}, u32[]{:S(2)}) collective-permute-start(bf16[160,256]{1,0:T(8,128)(2,1)S(1)} %pad_maximum_fusion.3), channel_id=1, source_target_pairs={{0,8},{64,72},{128,136},{192,200},{8,0},{72,64},{136,128},{200,192... | collective-permute-start | bytes 245768 | tf_op jit(solution)/shard_map/ppermute | solution.py:319
  68.6 2.4 %collective-permute-start.4 = (bf16[160,256]{1,0:T(8,128)(2,1)S(1)}, bf16[160,256]{1,0:T(8,128)(2,1)S(1)}, u32[]{:S(2)}, u32[]{:S(2)}) collective-permute-start(bf16[160,256]{1,0:T(8,128)(2,1)S(1)} %pad_maximum_fusion.3), channel_id=1, source_target_pairs={{0,128},{64,192},{128,8},{192,72},{8,136},{72,200},{136,0},{200,64... | collective-permute-start | bytes 245768 | tf_op jit(solution)/shard_map/ppermute | solution.py:319
  71.6 2.7 %collective-permute-done.5 = bf16[160,256]{1,0:T(8,128)(2,1)S(1)} collective-permute-done((bf16[160,256]{1,0:T(8,128)(2,1)S(1)}, bf16[160,256]{1,0:T(8,128)(2,1)S(1)}, u32[]{:S(2)}, u32[]{:S(2)}) %collective-permute-start.5) | collective-permute-done | bytes 81952 | tf_op jit(solution)/shard_map/ppermute | solution.py:319
  74.5 1.1 %broadcast_in_dim.14 = bf16[16,144,256]{2,1,0:T(8,128)(2,1)} broadcast(bf16[144,256]{1,0:T(8,128)(2,1)S(1)} %add_convert_fusion.1), dimensions={1,2} | broadcast | bytes 1253376 | tf_op jit(solution)/shard_map/broadcast_in_dim | solution.py:326
  75.6 3.7 %all-to-all-start.1 = ((bf16[16,144,256]{2,1,0:T(8,128)(2,1)}), bf16[16,144,256]{2,1,0:T(8,128)(2,1)S(1)}, u32[]{:S(2)}, u32[]{:S(2)}) async-start(bf16[16,144,256]{2,1,0:T(8,128)(2,1)} %broadcast_in_dim.14), calls=%async_computation.1 | async-start | bytes 2359296 | tf_op jit(solution)/shard_map/all_to_all | solution.py:326
  79.3 3.5 %feature.1 = bf16[1536,256]{1,0:T(8,128)(2,1)} custom-call(bf16[1728,256]{1,0:T(8,128)(2,1)S(1)} %get-tuple-element.24.fg, bf16[2304,256]{1,0:T(8,128)(2,1)S(1)} %get-tuple-element.25.k1t), custom_call_target="tpu_custom_call" | custom-call | flops 2500000000 | bytes 2064384 | tf_op jit(solution)/shard_map/feature/pallas_call | solution.py:26
  82.8 9.7 %all-to-all-done.1 = bf16[16,144,256]{2,1,0:T(8,128)(2,1)S(1)} async-done(((bf16[16,144,256]{2,1,0:T(8,128)(2,1)}), bf16[16,144,256]{2,1,0:T(8,128)(2,1)S(1)}, u32[]{:S(2)}, u32[]{:S(2)}) %all-to-all-start.1) | async-done | bytes 1179680 | tf_op jit(solution)/shard_map/all_to_all | solution.py:326
  92.6 6.3 %collective-permute-start.7 = (bf16[2304,256]{1,0:T(8,128)(2,1)S(1)}, bf16[2304,256]{1,0:T(8,128)(2,1)S(1)}, u32[]{:S(2)}, u32[]{:S(2)}) collective-permute-start(bf16[2304,256]{1,0:T(8,128)(2,1)S(1)} %bitcast.16), channel_id=1, source_target_pairs={{0,1},{1,0},{2,3},{3,2},{4,5},{5,4},{6,7},{7,6},{8,9},{9,8},{10,11... | collective-permute-start | bytes 3538952 | tf_op jit(solution)/shard_map/ppermute | solution.py:241
  100.0 1.3 %collective-permute-done.7.other = bf16[2304,256]{1,0:T(8,128)(2,1)S(1)} collective-permute-done((bf16[2304,256]{1,0:T(8,128)(2,1)S(1)}, bf16[2304,256]{1,0:T(8,128)(2,1)S(1)}, u32[]{:S(2)}, u32[]{:S(2)}) %collective-permute-start.7) | collective-permute-done | bytes 1179680 | tf_op jit(solution)/shard_map/ppermute | solution.py:241
  101.4 2.9 %final.1 = (f32[2304,256]{1,0:T(8,128)}, f32[2304,256]{1,0:T(8,128)}) custom-call(s32[2]{0:T(128)S(1)} %pad_add_fusion.ids, bf16[2304,256]{1,0:T(8,128)(2,1)S(1)} %bitcast.17, bf16[2304,256]{1,0:T(8,128)(2,1)S(1)} %collective-permute-done.7.other), custom_call_target="tpu_custom_call" | custom-call | bytes 2359304 | tf_op jit(solution)/shard_map/final/pallas_call | solution.py:26
  (48 shorter events, 3.4 us)
Async XLA Ops:
  0.6 1.1 %copy-start = (bf16[1,16,96,256]{3,2,1,0:T(8,128)(2,1)S(1)}, bf16[1,16,96,256]{3,2,1,0:T(8,128)(2,1)}, u32[]{:S(2)}) copy-start(bf16[1,16,96,256]{3,2,1,0:T(8,128)(2,1)} %param.6) | copy-start | bytes 2359300
  1.8 0.7 copy-start.2
  2.5 14.4 %collective-permute-start = (bf16[400,256]{1,0:T(8,128)(2,1)S(1)}, bf16[400,256]{1,0:T(8,128)(2,1)S(1)}, u32[]{:S(2)}, u32[]{:S(2)}) collective-permute-start(bf16[400,256]{1,0:T(8,128)(2,1)S(1)} %get-tuple-element.18), channel_id=1, source_target_pairs={{0,64},{64,128},{128,192},{192,8},{8,72},{72,136},{136,200},{200,0... | collective-permute-start | bytes 614408 | tf_op jit(solution)/shard_map/ppermute | solution.py:270
  5.0 11.9 %collective-permute-start.1 = (bf16[400,256]{1,0:T(8,128)(2,1)S(1)}, bf16[400,256]{1,0:T(8,128)(2,1)S(1)}, u32[]{:S(2)}, u32[]{:S(2)}) collective-permute-start(bf16[400,256]{1,0:T(8,128)(2,1)S(1)} %get-tuple-element.19), channel_id=1, source_target_pairs={{0,200},{64,0},{128,64},{192,128},{8,192},{72,8},{136,72},{200,136... | collective-permute-start | bytes 614408 | tf_op jit(solution)/shard_map/ppermute | solution.py:271
  9.7 1.1 %copy-start.1 = (bf16[1,16,96,256]{3,2,1,0:T(8,128)(2,1)S(1)}, bf16[1,16,96,256]{3,2,1,0:T(8,128)(2,1)}, u32[]{:S(2)}) copy-start(bf16[1,16,96,256]{3,2,1,0:T(8,128)(2,1)} %param.6) | copy-start | bytes 2359300
  10.9 1.3 %copy-start.4 = (bf16[3,3,256,256]{3,2,1,0:T(8,128)(2,1)S(1)}, bf16[3,3,256,256]{3,2,1,0:T(8,128)(2,1)}, u32[]{:S(2)}) copy-start(bf16[3,3,256,256]{3,2,1,0:T(8,128)(2,1)} %param.7) | copy-start | bytes 3538948
  12.1 1.3 %copy-start.6 = (bf16[3,3,256,256]{3,2,1,0:T(8,128)(2,1)S(1)}, bf16[3,3,256,256]{3,2,1,0:T(8,128)(2,1)}, u32[]{:S(2)}) copy-start(bf16[3,3,256,256]{3,2,1,0:T(8,128)(2,1)} %param.8) | copy-start | bytes 3538948
  13.4 3.5 %copy-start.8 = (bf16[256,3]{0,1:T(4,128)(2,1)S(1)}, bf16[256,3]{0,1:T(4,128)(2,1)}, u32[]{:S(2)}) copy-start(bf16[256,3]{0,1:T(4,128)(2,1)} %param.9) | copy-start | bytes 4612
  13.4 3.6 %copy-start.3 = (s32[1,16,96]{2,1,0:T(8,128)S(1)}, s32[1,16,96]{2,1,0:T(8,128)}, u32[]{:S(2)}) copy-start(s32[1,16,96]{2,1,0:T(8,128)} %param.11) | copy-start | bytes 18436
  13.4 3.6 %copy-start.5 = (bf16[3,3,256,256]{3,2,1,0:T(8,128)(2,1)S(1)}, bf16[3,3,256,256]{3,2,1,0:T(8,128)(2,1)}, u32[]{:S(2)}) copy-start(bf16[3,3,256,256]{3,2,1,0:T(8,128)(2,1)} %param.7) | copy-start | bytes 3538948
  13.4 3.6 %copy-start.7 = (bf16[3,3,256,256]{3,2,1,0:T(8,128)(2,1)S(1)}, bf16[3,3,256,256]{3,2,1,0:T(8,128)(2,1)}, u32[]{:S(2)}) copy-start(bf16[3,3,256,256]{3,2,1,0:T(8,128)(2,1)} %param.8) | copy-start | bytes 3538948
  31.0 3.5 %collective-permute-start.2 = (bf16[2320,256]{1,0:T(8,128)(2,1)S(1)}, bf16[2320,256]{1,0:T(8,128)(2,1)S(1)}, u32[]{:S(2)}, u32[]{:S(2)}) collective-permute-start(bf16[2320,256]{1,0:T(8,128)(2,1)S(1)} %pad_maximum_fusion.1), channel_id=1, source_target_pairs={{0,1},{1,0},{2,3},{3,2},{4,5},{5,4},{6,7},{7,6},{8,9},{9,8},{10,11... | collective-permute-start | bytes 3563528 | tf_op jit(solution)/shard_map/ppermute | solution.py:241
  60.9 3.4 %collective-permute-start.3 = (bf16[160,256]{1,0:T(8,128)(2,1)S(1)}, bf16[160,256]{1,0:T(8,128)(2,1)S(1)}, u32[]{:S(2)}, u32[]{:S(2)}) collective-permute-start(bf16[160,256]{1,0:T(8,128)(2,1)S(1)} %pad_maximum_fusion.2), channel_id=1, source_target_pairs={{0,64},{64,0},{128,192},{192,128},{1,65},{65,1},{129,193},{193,129... | collective-permute-start | bytes 245768 | tf_op jit(solution)/shard_map/ppermute | solution.py:319
  64.4 7.3 %collective-permute-start.6 = (bf16[160,256]{1,0:T(8,128)(2,1)S(1)}, bf16[160,256]{1,0:T(8,128)(2,1)S(1)}, u32[]{:S(2)}, u32[]{:S(2)}) collective-permute-start(bf16[160,256]{1,0:T(8,128)(2,1)S(1)} %pad_maximum_fusion.3), channel_id=1, source_target_pairs={{0,8},{64,72},{128,136},{192,200},{8,0},{72,64},{136,128},{200,192... | collective-permute-start | bytes 245768 | tf_op jit(solution)/shard_map/ppermute | solution.py:319
  68.6 5.7 %collective-permute-start.5 = (bf16[160,256]{1,0:T(8,128)(2,1)S(1)}, bf16[160,256]{1,0:T(8,128)(2,1)S(1)}, u32[]{:S(2)}, u32[]{:S(2)}) collective-permute-start(bf16[160,256]{1,0:T(8,128)(2,1)S(1)} %pad_maximum_fusion.3), channel_id=1, source_target_pairs={{0,136},{64,200},{128,0},{192,64},{8,128},{72,192},{136,8},{200,72... | collective-permute-start | bytes 245768 | tf_op jit(solution)/shard_map/ppermute | solution.py:319
  68.6 5.8 %collective-permute-start.4 = (bf16[160,256]{1,0:T(8,128)(2,1)S(1)}, bf16[160,256]{1,0:T(8,128)(2,1)S(1)}, u32[]{:S(2)}, u32[]{:S(2)}) collective-permute-start(bf16[160,256]{1,0:T(8,128)(2,1)S(1)} %pad_maximum_fusion.3), channel_id=1, source_target_pairs={{0,128},{64,192},{128,8},{192,72},{8,136},{72,200},{136,0},{200,64... | collective-permute-start | bytes 245768 | tf_op jit(solution)/shard_map/ppermute | solution.py:319
  75.6 17.0 %all-to-all-start.1 = ((bf16[16,144,256]{2,1,0:T(8,128)(2,1)}), bf16[16,144,256]{2,1,0:T(8,128)(2,1)S(1)}, u32[]{:S(2)}, u32[]{:S(2)}) async-start(bf16[16,144,256]{2,1,0:T(8,128)(2,1)} %broadcast_in_dim.14), calls=%async_computation.1 | async-start | bytes 2359296 | tf_op jit(solution)/shard_map/all_to_all | solution.py:326
  92.6 8.8 %collective-permute-start.7 = (bf16[2304,256]{1,0:T(8,128)(2,1)S(1)}, bf16[2304,256]{1,0:T(8,128)(2,1)S(1)}, u32[]{:S(2)}, u32[]{:S(2)}) collective-permute-start(bf16[2304,256]{1,0:T(8,128)(2,1)S(1)} %bitcast.16), channel_id=1, source_target_pairs={{0,1},{1,0},{2,3},{3,2},{4,5},{5,4},{6,7},{7,6},{8,9},{9,8},{10,11... | collective-permute-start | bytes 3538952 | tf_op jit(solution)/shard_map/ppermute | solution.py:241

commit v3 on v2

--- a/solution.py
+++ b/solution.py
@@ -17,16 +17,18 @@
 ROWWISE = (((0,), (0,)), ((), ()))
 VMEM = pl.BlockSpec(memory_space=pltpu.VMEM)
 SMEM = pl.BlockSpec(memory_space=pltpu.SMEM)
+HBM = pl.BlockSpec(memory_space=pltpu.HBM)
 AXES = ("b", "x", "h", "y", "c")
 
 
-def call(kernel, outs, args, scratch=(), limit=24, flops=0, name=None, scalars=0, out_specs=None):
+def call(kernel, outs, args, ins, scratch=(), limit=24, flops=0, name=None, out_specs=None, aliases={}):
     moved = sum(a.size * a.dtype.itemsize for a in args)
     shapes = tuple(jax.ShapeDtypeStruct(s, d) for s, d in outs)
     return pl.pallas_call(
         kernel,
         out_shape=shapes,
-        in_specs=[SMEM] * scalars + [VMEM] * (len(args) - scalars),
+        in_specs=list(ins),
+        input_output_aliases=aliases,
         out_specs=(VMEM,) * len(outs) if out_specs is None else out_specs,
         scratch_shapes=list(scratch),
         compiler_params=pltpu.CompilerParams(vmem_limit_bytes=limit * 1024 * 1024),
@@ -35,10 +37,13 @@
     )(*args)
 
 
+def aligned(start):
+    return start if isinstance(start, int) else pl.multiple_of(start, COLS)
+
+
 def conv_rows(wide, start, count, kernel):
     patch = jnp.concatenate(
-        [wide[pl.ds(pl.multiple_of(start + a * COLS, COLS), count * COLS), :] for a in range(3)],
-        axis=1,
+        [wide[pl.ds(aligned(start + a * COLS), count * COLS), :] for a in range(3)], axis=1
     )
     out = jnp.dot(patch, kernel[...], preferred_element_type=F32)
     return out.reshape(count, COLS, CH)
@@ -49,14 +54,14 @@
     col = lax.broadcasted_iota(jnp.int32, rows.shape, 1)
     left = jnp.where(col == 0, 0.0, pltpu.roll(rows, 1, 1))
     right = jnp.where(col == COLS - 1, 0.0, pltpu.roll(rows, COLS - 1, 1))
-    at = pl.ds(pl.multiple_of(start, COLS), count * COLS)
+    at = pl.ds(aligned(start), count * COLS)
     wide[at, 0:CH] = left.astype(BF16).reshape(count * COLS, CH)
     wide[at, CH:2 * CH] = rows.astype(BF16).reshape(count * COLS, CH)
     wide[at, 2 * CH:3 * CH] = right.astype(BF16).reshape(count * COLS, CH)
 
 
 def load_rows(ref, start, count):
-    at = pl.ds(pl.multiple_of(start, COLS), count * COLS)
+    at = pl.ds(aligned(start), count * COLS)
     return ref[at, :].astype(F32).reshape(count, COLS, CH)
 
 
@@ -72,12 +77,14 @@
     return jnp.stack(parts)
 
 
-def edge_kernel(f, lab, up, down, tag):
+def edge_kernel(f, lab, up, down, fv, labels, tag):
     for out, row, label in ((up, 0, 0), (down, ROWS - HALO, ROWS - 2)):
         out[0:EDGE, :] = f[row * COLS:(row + HALO) * COLS, :]
         tag[...] = jnp.zeros_like(tag)
         tag[0:2, 0:COLS] = lab[label:label + 2, :].astype(F32)
         out[EDGE:BLOCK, :] = tag[...].astype(BF16)
+    fv[...] = f[...]
+    labels[...] = lab[...]
 
 
 def inner_kernel(f, k1, k2, fw, aw, slope, k1t, k2t):
@@ -87,16 +94,12 @@
 
     lax.fori_loop(0, 8, widen, 0)
 
-    def first(t, c):
-        at = t * (7 * COLS)
-        v = conv_rows(fw, at, 7, k1)
+    for t in range(7):
+        at = t * (2 * COLS)
+        v = conv_rows(fw, at, 2, k1)
         s = sigmoid(v)
-        rows = pl.ds(pl.multiple_of(at, COLS), 7 * COLS)
-        slope[rows, :] = (s * (1.0 + v * (1.0 - s))).reshape(7 * COLS, CH)
+        slope[pl.ds(at, 2 * COLS), :] = (s * (1.0 + v * (1.0 - s))).reshape(2 * COLS, CH)
         store_wide(aw, at, v * s)
-        return c
-
-    lax.fori_loop(0, 2, first, 0)
 
     for t in range(9):
         for src, dst in ((k1, k1t), (k2, k2t)):
@@ -129,7 +132,7 @@
             at = t * (18 * COLS)
             v = conv_rows(fw, at, 4, k1)
             s = sigmoid(v)
-            rows = pl.ds(pl.multiple_of(at, COLS), 4 * COLS)
+            rows = pl.ds(aligned(at), 4 * COLS)
             slope[rows, :] = (s * (1.0 + v * (1.0 - s))).reshape(4 * COLS, CH)
             store_wide(aw, at, keep_rows(v * s, base - 3 + t * 18, height))
             return c
@@ -184,15 +187,12 @@
 
         weight(sw, 2, aw, 2, g2)
 
-        def third(t, c):
-            at = t * (6 * COLS)
-            v = conv_rows(sw, at, 6, k2t)
-            sl = slope[pl.ds(pl.multiple_of(at + 2 * COLS, COLS), 6 * COLS), :]
-            g = keep_rows(v * sl.reshape(6, COLS, CH), base - 1 + t * 6, height)
+        for t in range(6):
+            at = t * (3 * COLS)
+            v = conv_rows(sw, at, 3, k2t)
+            sl = slope[pl.ds(at + 2 * COLS, 3 * COLS), :]
+            g = keep_rows(v * sl.reshape(3, COLS, CH), base - 1 + t * 3, height)
             store_wide(fgw, at, g)
-            return c
-
-        lax.fori_loop(0, 3, third, 0)
         weight(fgw, 1, fw, 3, g1)
         fg[...] = fgw[:, CH:2 * CH]
 
@@ -209,25 +209,35 @@
     def step(t, c):
         at = t * (8 * COLS)
         v = conv_rows(fgw, at, 8, k1t)
-        out[pl.ds(pl.multiple_of(at, COLS), 8 * COLS), :] = v.astype(BF16).reshape(8 * COLS, CH)
+        out[pl.ds(aligned(at), 8 * COLS), :] = v.astype(BF16).reshape(8 * COLS, CH)
         return c
 
     lax.fori_loop(0, 2, step, 0)
 
 
-def final_kernel(ids, mine, other, g1, g2, wide, sems):
+def convert_out(block, wide, out, sems):
     copies = []
     for t in range(3):
         at = pl.ds(t * 768, 768)
-        for k, block in enumerate((mine, other)):
-            wide[k, at, :] = block[at, :].astype(F32)
-        for k, out in enumerate((g1, g2)):
-            slot = ids[1] if k == 0 else 1 - ids[1]
-            copy = pltpu.make_async_copy(wide.at[slot, at], out.at[at], sems.at[k, t])
-            copy.start()
-            copies.append(copy)
+        wide[at, :] = block[at, :].astype(F32)
+        copies.append(pltpu.make_async_copy(wide.at[at], out.at[at], sems.at[t]))
+        copies[-1].start()
     for copy in copies:
         copy.wait()
+
+
+def mine_kernel(ids, mine, g1, g2, wide, sems):
+    @pl.when(ids[1] == 0)
+    def _():
+        convert_out(mine, wide, g1, sems)
+
+    @pl.when(ids[1] == 1)
+    def _():
+        convert_out(mine, wide, g2, sems)
+
+
+def other_kernel(ids, other, g1_in, g2_in, g1, g2, wide, sems):
+    mine_kernel(ids, other, g2, g1, wide, sems)
 
 
 def ring(step):
@@ -248,7 +258,7 @@
 
 def join_small(rows):
     full = rows.astype(F32)
-    return full[..., 0:8, :] + full[..., 8:16, :]
+    return full[..., 0:4, :] + full[..., 4:8, :]
 
 
 def per_device(features, first_kernel, second_kernel, classifier, class_bias, labels):
@@ -263,9 +273,10 @@
     lab = labels.reshape(ROWS, COLS)
     k1 = first_kernel.reshape(9 * CH, CH)
     k2 = second_kernel.reshape(9 * CH, CH)
-    up, down = call(
-        edge_kernel, [((BLOCK, CH), BF16)] * 2, (flat, lab),
-        [pltpu.VMEM((16, CH), F32)], limit=8, name="edge",
+    up, down, fv, labels = call(
+        edge_kernel,
+        [((BLOCK, CH), BF16), ((BLOCK, CH), BF16), ((PIX, CH), BF16), ((ROWS, COLS), jnp.int32)],
+        (flat, lab), [VMEM] * 2, [pltpu.VMEM((16, CH), F32)], limit=8, name="edge",
     )
     above = lax.ppermute(down, ("b", "h"), ring(1))
     below = lax.ppermute(up, ("b", "h"), ring(7))
@@ -274,7 +285,8 @@
         inner_kernel,
         [((PIX, 3 * CH), BF16), ((14 * COLS, 3 * CH), BF16), ((14 * COLS, CH), F32),
          ((9 * CH, CH), BF16), ((9 * CH, CH), BF16)],
-        (flat, k1, k2), flops=5_000_000_000, name="inner",
+        (fv, k1, k2), [VMEM] * 3,
+        flops=5_000_000_000, name="inner",
     )
 
     cls = jnp.pad(jnp.concatenate([classifier.T, classifier.T], axis=0), ((0, 10), (0, 0)))
@@ -282,7 +294,7 @@
     g1, g2, small, fg = call(
         make_main(height, scale),
         [((9 * CH, CH), BF16), ((9 * CH, CH), BF16), ((8, CH), F32), ((18 * COLS, CH), BF16)],
-        (ids, above, below, fwi, awi, slopei, k1, k2, k2t, cls, bias, lab),
+        (ids, above, below, fwi, awi, slopei, k1, k2, k2t, cls, bias, labels), [SMEM] + [VMEM] * 11,
         [
             pltpu.VMEM((24 * COLS, 3 * CH), BF16),
             pltpu.VMEM((22 * COLS, 3 * CH), BF16),
@@ -292,13 +304,14 @@
             pltpu.VMEM((22 * COLS, CH), F32),
             pltpu.VMEM((2, 8, 1024), F32),
         ],
-        limit=40, flops=9_000_000_000, name="main", scalars=1,
+        limit=40, flops=9_000_000_000, name="main",
     )
     (grad_features,) = call(
-        feature_kernel, [((PIX, CH), BF16)], (fg, k1t),
+        feature_kernel, [((PIX, CH), BF16)], (fg, k1t), [VMEM] * 2,
         [pltpu.VMEM((18 * COLS, 3 * CH), BF16)], limit=16, flops=2_500_000_000, name="feature",
     )
 
+    small = small[0:4]
     keep = jnp.where(core == 0, g1, g2)
     give = jnp.where(core == 0, g2, g1)
     got = shift(jnp.concatenate([give, split_small(small)], axis=0), "c", 1, 2)
@@ -307,7 +320,7 @@
 
     part = 9 * CH // 16
     spread = jnp.concatenate(
-        [total.reshape(16, part, CH), jnp.broadcast_to(split_small(small), (16, 16, CH))], axis=1
+        [total.reshape(16, part, CH), jnp.broadcast_to(split_small(small), (16, 8, CH))], axis=1
     )
     spread = lax.all_to_all(spread, ("x", "y"), 0, 0, tiled=True)
     piece = jnp.sum(spread[:, :part].astype(F32), axis=0).astype(BF16)
@@ -326,11 +339,15 @@
     full = lax.all_to_all(jnp.broadcast_to(piece, (16, part, CH)), ("x", "y"), 0, 0, tiled=True)
     mine = full.reshape(9 * CH, CH)
     other = shift(mine, "c", 1, 2)
-    hbm = pl.BlockSpec(memory_space=pl.ANY)
+    outs = [((9 * CH, CH), F32)] * 2
+    scratch = [pltpu.VMEM((9 * CH, CH), F32), pltpu.SemaphoreType.DMA((3,))]
+    halves = call(
+        mine_kernel, outs, (ids, mine), [SMEM, VMEM], scratch,
+        limit=8, flops=1_000_000_000, name="mine", out_specs=(HBM, HBM),
+    )
     grad_first, grad_second = call(
-        final_kernel, [((9 * CH, CH), F32)] * 2, (ids, mine, other),
-        [pltpu.VMEM((2, 9 * CH, CH), F32), pltpu.SemaphoreType.DMA((2, 3))],
-        limit=16, name="final", scalars=1, out_specs=(hbm, hbm),
+        other_kernel, outs, (ids, other, *halves), [SMEM, VMEM, HBM, HBM], scratch,
+        limit=8, name="other", out_specs=(HBM, HBM), aliases={2: 0, 3: 1},
     )
     shape = (3, 3, CH, CH)
     return (

time: 105 us -> 111 us (1.057)
  local copies, waits for them, and re-layouts: 8.45 us -> 13.2 us
  waiting for transfers between devices: 20.3 us -> 25 us
  starting transfers between devices: 24.4 us -> 21.5 us
    concatenate x0 -> x1, local copies, waits for them, and re-layouts: none -> 4.67 us  [per_device(): got = shift(jnp.concatenate([give, split_small(small)], axis=0), 'c', 1, 2)]
    all_to_all x1, waiting for transfers between devices: 9.75 us -> 13 us  [per_device(): lax.all_to_all(jnp.broadcast_to(piece, (16, part, CH)), ('x', 'y'), 0, 0,...]
    ppermute x2, starting transfers between devices: 7.38 us -> 4.33 us  [shift(): lax.ppermute(value, axis, [(i, (i + step) % size) for i in range(size)])]
    ppermute x4, waiting for transfers between devices: 6.73 us -> 9.32 us  [per_device(): others = [lax.ppermute(send, axis, move) for axis, move in moves]]
    ppermute x2, waiting for transfers between devices: 3.82 us -> 2.69 us  [shift(): lax.ppermute(value, axis, [(i, (i + step) % size) for i in range(size)])]
    pallas_call x5 -> x6, Pallas kernels: 23.5 us -> 23.2 us  [call(): pl.pallas_call(kernel, out_shape=shapes, in_specs=list(ins), input_output...]
    unnamed x18 -> x22, local copies, waits for them, and re-layouts: 5.51 us -> 5.57 us
  transfers between devices with their start and end apart: 9 -> 9, of which waited for: 7 -> 6; matrix products, arithmetic and copies ran while one was open for 2% -> 2% of each run, Pallas kernels for 7% -> 7%
where the time goes in v3:
time: 111 us; the launch traced here: 110 us
  waiting for transfers between devices  25 us (23%)
  blocking collectives  24.7 us (22%)
  Pallas kernels  23.2 us (21%)
  starting transfers between devices  21.5 us (19%)
  local copies, waits for them, and re-layouts  13.2 us (12%)
  other arithmetic  1.73 us (2%)
    all_to_all x1, blocking collectives, per_device(): spread = lax.all_to_all(spread, ('x', 'y'), 0, 0, tiled=True)  24.7 us
    pallas_call x6, Pallas kernels, call(): pl.pallas_call(kernel, out_shape=shapes, in_specs=list(ins), input_output...  23.2 us
    all_to_all x1, waiting for transfers between devices, per_device(): lax.all_to_all(jnp.broadcast_to(piece, (16, part, CH)), ('x', 'y'), 0, 0,...  13 us
    ppermute x4, waiting for transfers between devices, per_device(): others = [lax.ppermute(send, axis, move) for axis, move in moves]  9.32 us
    ppermute x4, starting transfers between devices, per_device(): others = [lax.ppermute(send, axis, move) for axis, move in moves]  6.75 us
    unnamed x22, local copies, waits for them, and re-layouts  5.57 us
    concatenate x1, local copies, waits for them, and re-layouts, per_device(): got = shift(jnp.concatenate([give, split_small(small)], axis=0), 'c', 1, 2)  4.67 us
    ppermute x2, starting transfers between devices, shift(): lax.ppermute(value, axis, [(i, (i + step) % size) for i in range(size)])  4.33 us
  transfers between devices with their start and end apart: 9, of which 6 were waited for; matrix products, arithmetic and copies ran while one was open for 2% of the time, Pallas kernels for 7%

profile of v3, /device:TPU:1, one launch (start us, length us, event | category | flops | bytes accessed | tf_op | source)
XLA Modules:
  0.0 110.3 jit_solution(9190609431877781027)
XLA Ops:
  0.6 1.1 %copy-done = bf16[1,16,96,256]{3,2,1,0:T(8,128)(2,1)S(1)} copy-done((bf16[1,16,96,256]{3,2,1,0:T(8,128)(2,1)S(1)}, bf16[1,16,96,256]{3,2,1,0:T(8,128)(2,1)}, u32[]{:S(2)}) %copy-start) | copy-done | bytes 786456
  2.5 2.5 %collective-permute-start = (bf16[400,256]{1,0:T(8,128)(2,1)S(1)}, bf16[400,256]{1,0:T(8,128)(2,1)S(1)}, u32[]{:S(2)}, u32[]{:S(2)}) collective-permute-start(bf16[400,256]{1,0:T(8,128)(2,1)S(1)} %get-tuple-element.22), channel_id=1, source_target_pairs={{0,64},{64,128},{128,192},{192,8},{8,72},{72,136},{136,200},{200,0... | collective-permute-start | bytes 614408 | tf_op jit(solution)/shard_map/ppermute | solution.py:281
  5.1 4.0 %collective-permute-start.1 = (bf16[400,256]{1,0:T(8,128)(2,1)S(1)}, bf16[400,256]{1,0:T(8,128)(2,1)S(1)}, u32[]{:S(2)}, u32[]{:S(2)}) collective-permute-start(bf16[400,256]{1,0:T(8,128)(2,1)S(1)} %get-tuple-element.23), channel_id=1, source_target_pairs={{0,200},{64,0},{128,64},{192,128},{8,192},{72,8},{136,72},{200,136... | collective-permute-start | bytes 614408 | tf_op jit(solution)/shard_map/ppermute | solution.py:282
  9.8 1.3 %copy-done.2 = bf16[3,3,256,256]{3,2,1,0:T(8,128)(2,1)S(1)} copy-done((bf16[3,3,256,256]{3,2,1,0:T(8,128)(2,1)S(1)}, bf16[3,3,256,256]{3,2,1,0:T(8,128)(2,1)}, u32[]{:S(2)}) %copy-start.2) | copy-done | bytes 1179672
  11.1 1.3 %copy-done.4 = bf16[3,3,256,256]{3,2,1,0:T(8,128)(2,1)S(1)} copy-done((bf16[3,3,256,256]{3,2,1,0:T(8,128)(2,1)S(1)}, bf16[3,3,256,256]{3,2,1,0:T(8,128)(2,1)}, u32[]{:S(2)}) %copy-start.4) | copy-done | bytes 1179672
  12.3 2.5 %inner.1 = (bf16[1536,768]{1,0:T(8,128)(2,1)S(1)}, bf16[1344,768]{1,0:T(8,128)(2,1)S(1)}, f32[1344,256]{1,0:T(8,128)S(1)}, bf16[2304,256]{1,0:T(8,128)(2,1)S(1)}, bf16[2304,256]{1,0:T(8,128)(2,1)S(1)}) custom-call(bf16[1536,256]{1,0:T(8,128)(2,1)S(1)} %get-tuple-element.24.f, bf16[2304,256]{1,0:T(8,128)(2,1)S(1)} %bitcast.20, bf16[2304,256]{1,0:T(8,128)(2,1)S(1)} %bitcast.22), custom_call_target="tpu_custom_call" | custom-call | flops 5000000000 | bytes 3145728 | tf_op jit(solution)/shard_map/inner/pallas_call | solution.py:27
  14.8 1.0 copy-done.6
  16.0 13.1 %main.1 = (bf16[2304,256]{1,0:T(8,128)(2,1)S(1)}, bf16[2304,256]{1,0:T(8,128)(2,1)S(1)}, f32[8,256]{1,0:T(8,128)S(1)}, bf16[1728,256]{1,0:T(8,128)(2,1)S(1)}) custom-call(s32[2]{0:T(128)S(1)} %pad_add_fusion.ids, bf16[400,256]{1,0:T(8,128)(2,1)S(1)} %collective-permute-done.above, bf16[400,256]{1,0:T(8,128)(2,1)S(1)} %collective-permute-done.1.below, ...), custom_call_target="tpu_custom_call" | custom-call | flops 8999999488 | bytes 9766920 | tf_op jit(solution)/shard_map/main/pallas_call | solution.py:27
  30.1 4.7 %concatenate.19 = bf16[2312,256]{1,0:T(8,128)(2,1)} concatenate(bf16[2304,256]{1,0:T(8,128)(2,1)S(1)} %broadcast_select_fusion, bf16[4,256]{1,0:T(4,128)(2,1)} %get-tuple-element.47, bf16[4,256]{1,0:T(4,128)(2,1)S(1)} %get-tuple-element.46), dimensions={0} | concatenate | bytes 2367488 | tf_op jit(solution)/shard_map/concatenate | solution.py:317
  34.8 1.0 collective-permute-start.2
  35.7 2.7 %collective-permute-done.2 = bf16[2312,256]{1,0:T(8,128)(2,1)S(1)} collective-permute-done((bf16[2312,256]{1,0:T(8,128)(2,1)}, bf16[2312,256]{1,0:T(8,128)(2,1)S(1)}, u32[]{:S(2)}, u32[]{:S(2)}) %collective-permute-start.2) | collective-permute-done | bytes 1183776 | tf_op jit(solution)/shard_map/ppermute | solution.py:251
  39.0 24.7 %all_to_all.10 = bf16[16,152,256]{2,1,0:T(8,128)(2,1)S(1)} all-to-all(bf16[16,152,256]{2,1,0:T(8,128)(2,1)S(1)} %pad_maximum_fusion), channel_id=1, replica_groups=mesh['b'=4,'x'=4,'h'=2,'y'=4,'c'=2] {'x','y'}, dimensions={0} | all-to-all | bytes 2490368 | tf_op jit(solution)/shard_map/all_to_all | solution.py:325
  64.0 3.2 %collective-permute-done.3 = bf16[152,256]{1,0:T(8,128)(2,1)S(1)} collective-permute-done((bf16[152,256]{1,0:T(8,128)(2,1)S(1)}, bf16[152,256]{1,0:T(8,128)(2,1)S(1)}, u32[]{:S(2)}, u32[]{:S(2)}) %collective-permute-start.3) | collective-permute-done | bytes 77856 | tf_op jit(solution)/shard_map/ppermute | solution.py:332
  67.3 4.3 %collective-permute-start.6 = (bf16[152,256]{1,0:T(8,128)(2,1)S(1)}, bf16[152,256]{1,0:T(8,128)(2,1)S(1)}, u32[]{:S(2)}, u32[]{:S(2)}) collective-permute-start(bf16[152,256]{1,0:T(8,128)(2,1)S(1)} %pad_maximum_fusion.2), channel_id=1, source_target_pairs={{0,8},{64,72},{128,136},{192,200},{8,0},{72,64},{136,128},{200,192... | collective-permute-start | bytes 233480 | tf_op jit(solution)/shard_map/ppermute | solution.py:332
  72.0 2.0 %collective-permute-start.4 = (bf16[152,256]{1,0:T(8,128)(2,1)S(1)}, bf16[152,256]{1,0:T(8,128)(2,1)S(1)}, u32[]{:S(2)}, u32[]{:S(2)}) collective-permute-start(bf16[152,256]{1,0:T(8,128)(2,1)S(1)} %pad_maximum_fusion.2), channel_id=1, source_target_pairs={{0,128},{64,192},{128,8},{192,72},{8,136},{72,200},{136,0},{200,64... | collective-permute-start | bytes 233480 | tf_op jit(solution)/shard_map/ppermute | solution.py:332
  74.6 1.7 %collective-permute-done.5 = bf16[152,256]{1,0:T(8,128)(2,1)S(1)} collective-permute-done((bf16[152,256]{1,0:T(8,128)(2,1)S(1)}, bf16[152,256]{1,0:T(8,128)(2,1)S(1)}, u32[]{:S(2)}, u32[]{:S(2)}) %collective-permute-start.5) | collective-permute-done | bytes 77856 | tf_op jit(solution)/shard_map/ppermute | solution.py:332
  76.3 3.7 %collective-permute-done.4 = bf16[152,256]{1,0:T(8,128)(2,1)S(1)} collective-permute-done((bf16[152,256]{1,0:T(8,128)(2,1)S(1)}, bf16[152,256]{1,0:T(8,128)(2,1)S(1)}, u32[]{:S(2)}, u32[]{:S(2)}) %collective-permute-start.4) | collective-permute-done | bytes 77856 | tf_op jit(solution)/shard_map/ppermute | solution.py:332
  80.1 1.1 broadcast_in_dim.14
  81.2 3.8 %all-to-all-start.1 = ((bf16[16,144,256]{2,1,0:T(8,128)(2,1)}), bf16[16,144,256]{2,1,0:T(8,128)(2,1)S(1)}, u32[]{:S(2)}, u32[]{:S(2)}) async-start(bf16[16,144,256]{2,1,0:T(8,128)(2,1)} %broadcast_in_dim.14), calls=%async_computation.1 | async-start | bytes 2359296 | tf_op jit(solution)/shard_map/all_to_all | solution.py:339
  85.1 3.5 %feature.1 = bf16[1536,256]{1,0:T(8,128)(2,1)} custom-call(bf16[1728,256]{1,0:T(8,128)(2,1)S(1)} %copy-done.9, bf16[2304,256]{1,0:T(8,128)(2,1)S(1)} %copy-done.7), custom_call_target="tpu_custom_call" | custom-call | flops 2500000000 | bytes 2064384 | tf_op jit(solution)/shard_map/feature/pallas_call | solution.py:27
  88.6 13.0 %all-to-all-done.1 = bf16[16,144,256]{2,1,0:T(8,128)(2,1)S(1)} async-done(((bf16[16,144,256]{2,1,0:T(8,128)(2,1)}), bf16[16,144,256]{2,1,0:T(8,128)(2,1)S(1)}, u32[]{:S(2)}, u32[]{:S(2)}) %all-to-all-start.1) | async-done | bytes 1179680 | tf_op jit(solution)/shard_map/all_to_all | solution.py:339
  101.5 3.4 %collective-permute-start.7 = (bf16[2304,256]{1,0:T(8,128)(2,1)S(1)}, bf16[2304,256]{1,0:T(8,128)(2,1)S(1)}, u32[]{:S(2)}, u32[]{:S(2)}) collective-permute-start(bf16[2304,256]{1,0:T(8,128)(2,1)S(1)} %bitcast.16), channel_id=1, source_target_pairs={{0,1},{1,0},{2,3},{3,2},{4,5},{5,4},{6,7},{7,6},{8,9},{9,8},{10,11... | collective-permute-start | bytes 3538952 | tf_op jit(solution)/shard_map/ppermute | solution.py:251
  106.0 2.0 %mine.1 = (f32[2304,256]{1,0:T(8,128)}, f32[2304,256]{1,0:T(8,128)}) custom-call(s32[2]{0:T(128)S(1)} %pad_add_fusion.ids, bf16[2304,256]{1,0:T(8,128)(2,1)S(1)} %bitcast.17), custom_call_target="tpu_custom_call" | custom-call | flops 1000000000 | bytes 1179656 | tf_op jit(solution)/shard_map/mine/pallas_call | solution.py:27
  108.1 2.0 %other.1 = (f32[2304,256]{1,0:T(8,128)}, f32[2304,256]{1,0:T(8,128)}) custom-call(s32[2]{0:T(128)S(1)} %pad_add_fusion.ids, bf16[2304,256]{1,0:T(8,128)(2,1)S(1)} %collective-permute-done.7.other, f32[2304,256]{1,0:T(8,128)} %get-tuple-element.35.g1_in, f32[2304,256]{1,0:T(8,128)} %get-tuple-element.36.g2_in), custom_call_target="tpu_custom_call", output_to_operand_aliasing={{0}: (2, {}), {1}: (3, {})} | custom-call | bytes 5898248 | tf_op jit(solution)/shard_map/other/pallas_call | solution.py:27
  (53 shorter events, 5.6 us)
Async XLA Ops:
  0.6 1.1 %copy-start = (bf16[1,16,96,256]{3,2,1,0:T(8,128)(2,1)S(1)}, bf16[1,16,96,256]{3,2,1,0:T(8,128)(2,1)}, u32[]{:S(2)}) copy-start(bf16[1,16,96,256]{3,2,1,0:T(8,128)(2,1)} %param.6) | copy-start | bytes 2359300
  1.8 0.7 copy-start.1
  2.5 13.4 %collective-permute-start = (bf16[400,256]{1,0:T(8,128)(2,1)S(1)}, bf16[400,256]{1,0:T(8,128)(2,1)S(1)}, u32[]{:S(2)}, u32[]{:S(2)}) collective-permute-start(bf16[400,256]{1,0:T(8,128)(2,1)S(1)} %get-tuple-element.22), channel_id=1, source_target_pairs={{0,64},{64,128},{128,192},{192,8},{8,72},{72,136},{136,200},{200,0... | collective-permute-start | bytes 614408 | tf_op jit(solution)/shard_map/ppermute | solution.py:281
  5.1 10.8 %collective-permute-start.1 = (bf16[400,256]{1,0:T(8,128)(2,1)S(1)}, bf16[400,256]{1,0:T(8,128)(2,1)S(1)}, u32[]{:S(2)}, u32[]{:S(2)}) collective-permute-start(bf16[400,256]{1,0:T(8,128)(2,1)S(1)} %get-tuple-element.23), channel_id=1, source_target_pairs={{0,200},{64,0},{128,64},{192,128},{8,192},{72,8},{136,72},{200,136... | collective-permute-start | bytes 614408 | tf_op jit(solution)/shard_map/ppermute | solution.py:282
  9.8 1.3 %copy-start.2 = (bf16[3,3,256,256]{3,2,1,0:T(8,128)(2,1)S(1)}, bf16[3,3,256,256]{3,2,1,0:T(8,128)(2,1)}, u32[]{:S(2)}) copy-start(bf16[3,3,256,256]{3,2,1,0:T(8,128)(2,1)} %param.7) | copy-start | bytes 3538948
  11.1 1.3 %copy-start.4 = (bf16[3,3,256,256]{3,2,1,0:T(8,128)(2,1)S(1)}, bf16[3,3,256,256]{3,2,1,0:T(8,128)(2,1)}, u32[]{:S(2)}) copy-start(bf16[3,3,256,256]{3,2,1,0:T(8,128)(2,1)} %param.8) | copy-start | bytes 3538948
  12.3 3.6 %copy-start.10 = (bf16[256,3]{0,1:T(4,128)(2,1)S(1)}, bf16[256,3]{0,1:T(4,128)(2,1)}, u32[]{:S(2)}) copy-start(bf16[256,3]{0,1:T(4,128)(2,1)} %param.9) | copy-start | bytes 4612
  12.3 3.7 %copy-start.3 = (bf16[3,3,256,256]{3,2,1,0:T(8,128)(2,1)S(1)}, bf16[3,3,256,256]{3,2,1,0:T(8,128)(2,1)}, u32[]{:S(2)}) copy-start(bf16[3,3,256,256]{3,2,1,0:T(8,128)(2,1)} %param.7) | copy-start | bytes 3538948
  12.3 3.7 %copy-start.5 = (bf16[3,3,256,256]{3,2,1,0:T(8,128)(2,1)S(1)}, bf16[3,3,256,256]{3,2,1,0:T(8,128)(2,1)}, u32[]{:S(2)}) copy-start(bf16[3,3,256,256]{3,2,1,0:T(8,128)(2,1)} %param.8) | copy-start | bytes 3538948
  14.8 1.0 copy-start.6
  29.2 0.9 copy-start.8
  34.8 3.6 %collective-permute-start.2 = (bf16[2312,256]{1,0:T(8,128)(2,1)}, bf16[2312,256]{1,0:T(8,128)(2,1)S(1)}, u32[]{:S(2)}, u32[]{:S(2)}) collective-permute-start(bf16[2312,256]{1,0:T(8,128)(2,1)} %concatenate.19), channel_id=1, source_target_pairs={{0,1},{1,0},{2,3},{3,2},{4,5},{5,4},{6,7},{7,6},{8,9},{9,8},{10,11... | collective-permute-start | bytes 3551240 | tf_op jit(solution)/shard_map/ppermute | solution.py:251
  63.9 3.3 %collective-permute-start.3 = (bf16[152,256]{1,0:T(8,128)(2,1)S(1)}, bf16[152,256]{1,0:T(8,128)(2,1)S(1)}, u32[]{:S(2)}, u32[]{:S(2)}) collective-permute-start(bf16[152,256]{1,0:T(8,128)(2,1)S(1)} %pad_maximum_fusion.1), channel_id=1, source_target_pairs={{0,64},{64,0},{128,192},{192,128},{1,65},{65,1},{129,193},{193,129... | collective-permute-start | bytes 233480 | tf_op jit(solution)/shard_map/ppermute | solution.py:332
  67.3 7.3 %collective-permute-start.6 = (bf16[152,256]{1,0:T(8,128)(2,1)S(1)}, bf16[152,256]{1,0:T(8,128)(2,1)S(1)}, u32[]{:S(2)}, u32[]{:S(2)}) collective-permute-start(bf16[152,256]{1,0:T(8,128)(2,1)S(1)} %pad_maximum_fusion.2), channel_id=1, source_target_pairs={{0,8},{64,72},{128,136},{192,200},{8,0},{72,64},{136,128},{200,192... | collective-permute-start | bytes 233480 | tf_op jit(solution)/shard_map/ppermute | solution.py:332
  71.6 4.7 %collective-permute-start.5 = (bf16[152,256]{1,0:T(8,128)(2,1)S(1)}, bf16[152,256]{1,0:T(8,128)(2,1)S(1)}, u32[]{:S(2)}, u32[]{:S(2)}) collective-permute-start(bf16[152,256]{1,0:T(8,128)(2,1)S(1)} %pad_maximum_fusion.2), channel_id=1, source_target_pairs={{0,136},{64,200},{128,0},{192,64},{8,128},{72,192},{136,8},{200,72... | collective-permute-start | bytes 233480 | tf_op jit(solution)/shard_map/ppermute | solution.py:332
  72.0 8.1 %collective-permute-start.4 = (bf16[152,256]{1,0:T(8,128)(2,1)S(1)}, bf16[152,256]{1,0:T(8,128)(2,1)S(1)}, u32[]{:S(2)}, u32[]{:S(2)}) collective-permute-start(bf16[152,256]{1,0:T(8,128)(2,1)S(1)} %pad_maximum_fusion.2), channel_id=1, source_target_pairs={{0,128},{64,192},{128,8},{192,72},{8,136},{72,200},{136,0},{200,64... | collective-permute-start | bytes 233480 | tf_op jit(solution)/shard_map/ppermute | solution.py:332
  81.2 3.8 %copy-start.7 = (bf16[2304,256]{1,0:T(8,128)(2,1)S(1)}, bf16[2304,256]{1,0:T(8,128)(2,1)}, u32[]{:S(2)}) copy-start(bf16[2304,256]{1,0:T(8,128)(2,1)} %copy-done.6) | copy-start | bytes 3538948
  81.2 3.9 %copy-start.9 = (bf16[1728,256]{1,0:T(8,128)(2,1)S(1)}, bf16[1728,256]{1,0:T(8,128)(2,1)}, u32[]{:S(2)}) copy-start(bf16[1728,256]{1,0:T(8,128)(2,1)} %copy-done.8) | copy-start | bytes 2654212
  81.2 20.3 %all-to-all-start.1 = ((bf16[16,144,256]{2,1,0:T(8,128)(2,1)}), bf16[16,144,256]{2,1,0:T(8,128)(2,1)S(1)}, u32[]{:S(2)}, u32[]{:S(2)}) async-start(bf16[16,144,256]{2,1,0:T(8,128)(2,1)} %broadcast_in_dim.14), calls=%async_computation.1 | async-start | bytes 2359296 | tf_op jit(solution)/shard_map/all_to_all | solution.py:339
  101.5 6.5 %collective-permute-start.7 = (bf16[2304,256]{1,0:T(8,128)(2,1)S(1)}, bf16[2304,256]{1,0:T(8,128)(2,1)S(1)}, u32[]{:S(2)}, u32[]{:S(2)}) collective-permute-start(bf16[2304,256]{1,0:T(8,128)(2,1)S(1)} %bitcast.16), channel_id=1, source_target_pairs={{0,1},{1,0},{2,3},{3,2},{4,5},{5,4},{6,7},{7,6},{8,9},{9,8},{10,11... | collective-permute-start | bytes 3538952 | tf_op jit(solution)/shard_map/ppermute | solution.py:251

commit v4 on v3

--- a/solution.py
+++ b/solution.py
@@ -18,7 +18,11 @@
 VMEM = pl.BlockSpec(memory_space=pltpu.VMEM)
 SMEM = pl.BlockSpec(memory_space=pltpu.SMEM)
 HBM = pl.BlockSpec(memory_space=pltpu.HBM)
-AXES = ("b", "x", "h", "y", "c")
+AXES = ("q", "p", "x", "h", "y", "c")
+BAND = ("q", "p")
+DEPTH = ("q", "p", "h")
+PLANE = ("p", "x", "y")
+RAIL = ("x", "h", "y", "c")
 
 
 def call(kernel, outs, args, ins, scratch=(), limit=24, flops=0, name=None, out_specs=None, aliases={}):
@@ -217,8 +221,8 @@
 
 def convert_out(block, wide, out, sems):
     copies = []
-    for t in range(3):
-        at = pl.ds(t * 768, 768)
+    for t in range(9):
+        at = pl.ds(t * CH, CH)
         wide[at, :] = block[at, :].astype(F32)
         copies.append(pltpu.make_async_copy(wide.at[at], out.at[at], sems.at[t]))
         copies[-1].start()
@@ -262,10 +266,10 @@
 
 
 def per_device(features, first_kernel, second_kernel, classifier, class_bias, labels):
-    height = ROWS * lax.axis_size("b")
-    count = height * COLS * lax.axis_size("x") * lax.axis_size("h") * lax.axis_size("y") * lax.axis_size("c")
+    height = ROWS * lax.axis_size(BAND)
+    count = height * COLS * lax.axis_size(RAIL)
     scale = float(count) ** (-0.5)
-    band = lax.axis_index("b")
+    band = lax.axis_index(BAND)
     core = lax.axis_index("c")
     ids = jnp.stack([band, core])
 
@@ -278,8 +282,8 @@
         [((BLOCK, CH), BF16), ((BLOCK, CH), BF16), ((PIX, CH), BF16), ((ROWS, COLS), jnp.int32)],
         (flat, lab), [VMEM] * 2, [pltpu.VMEM((16, CH), F32)], limit=8, name="edge",
     )
-    above = lax.ppermute(down, ("b", "h"), ring(1))
-    below = lax.ppermute(up, ("b", "h"), ring(7))
+    above = lax.ppermute(down, DEPTH, ring(1))
+    below = lax.ppermute(up, DEPTH, ring(7))
 
     fwi, awi, slopei, k1t, k2t = call(
         inner_kernel,
@@ -314,33 +318,33 @@
     small = small[0:4]
     keep = jnp.where(core == 0, g1, g2)
     give = jnp.where(core == 0, g2, g1)
-    got = shift(jnp.concatenate([give, split_small(small)], axis=0), "c", 1, 2)
+    tail = jnp.pad(split_small(small), ((0, 8), (0, 0)))
+    got = shift(jnp.concatenate([give, tail], axis=0), "c", 1, 2)
     total = (keep.astype(F32) + got[:9 * CH].astype(F32)).astype(BF16)
     small = small + join_small(got[9 * CH:])
 
-    part = 9 * CH // 16
+    part = 9 * CH // 32
     spread = jnp.concatenate(
-        [total.reshape(16, part, CH), jnp.broadcast_to(split_small(small), (16, 8, CH))], axis=1
-    )
-    spread = lax.all_to_all(spread, ("x", "y"), 0, 0, tiled=True)
+        [total.reshape(32, part, CH), jnp.broadcast_to(split_small(small), (32, 8, CH))], axis=1
+    )
+    spread = lax.all_to_all(spread, PLANE, 0, 0, tiled=True)
     piece = jnp.sum(spread[:, :part].astype(F32), axis=0).astype(BF16)
     small = jnp.sum(join_small(spread[:, part:]), axis=0)
 
-    pair = [(0, 1), (1, 0), (2, 3), (3, 2)]
-    for moves in ((("b", pair),), tuple((("b", "h"), ring(k)) for k in (2, 6, 4))):
-        send = jnp.concatenate([piece, split_small(small)], axis=0)
-        others = [lax.ppermute(send, axis, move) for axis, move in moves]
-        wide = piece.astype(F32)
-        for other in others:
-            wide = wide + other[:part].astype(F32)
-            small = small + join_small(other[part:])
-        piece = wide.astype(BF16)
-
-    full = lax.all_to_all(jnp.broadcast_to(piece, (16, part, CH)), ("x", "y"), 0, 0, tiled=True)
+    send = jnp.concatenate([piece, split_small(small)], axis=0)
+    one, two, three = [lax.ppermute(send, DEPTH, ring(k)) for k in (2, 4, 6)]
+
+    def four(mine, pick):
+        return (mine + pick(two)) + (pick(one) + pick(three))
+
+    small = four(small, lambda block: join_small(block[part:]))
+    piece = four(piece.astype(F32), lambda block: block[:part].astype(F32)).astype(BF16)
+
+    full = lax.all_to_all(jnp.broadcast_to(piece, (32, part, CH)), PLANE, 0, 0, tiled=True)
     mine = full.reshape(9 * CH, CH)
     other = shift(mine, "c", 1, 2)
     outs = [((9 * CH, CH), F32)] * 2
-    scratch = [pltpu.VMEM((9 * CH, CH), F32), pltpu.SemaphoreType.DMA((3,))]
+    scratch = [pltpu.VMEM((9 * CH, CH), F32), pltpu.SemaphoreType.DMA((9,))]
     halves = call(
         mine_kernel, outs, (ids, mine), [SMEM, VMEM], scratch,
         limit=8, flops=1_000_000_000, name="mine", out_specs=(HBM, HBM),
@@ -357,13 +361,13 @@
 
 
 def solution(mesh):
-    fine = Mesh(mesh.devices.reshape(4, 4, 2, 4, 2), AXES)
-    rail = ("x", "h", "y", "c")
-    placed = (P(rail, "b", None, None), P(), P(), P(), P(), P(rail, "b", None))
+    fine = Mesh(mesh.devices.reshape(2, 2, 4, 2, 4, 2), AXES)
+    pixels = P(RAIL, BAND, None, None)
+    placed = (pixels, P(), P(), P(), P(), P(RAIL, BAND, None))
     return jax.shard_map(
         per_device,
         mesh=fine,
         in_specs=placed,
-        out_specs=(P(rail, "b", None, None), P(), P(), P(), P()),
+        out_specs=(pixels, P(), P(), P(), P()),
         check_vma=False,
     )

time: 111 us -> 101 us (0.910)
  waiting for transfers between devices: 25 us -> 16.4 us
  local copies, waits for them, and re-layouts: 13.2 us -> 9.22 us
  starting transfers between devices: 21.5 us -> 23.7 us
  blocking collectives: 24.7 us -> 25.9 us
    ppermute x6 -> x5, waiting for transfers between devices: 9.32 us -> 3.67 us  [the longest x3 3.66 us: per_device(): one, two, three = [lax.ppermute(send, DEPTH, ring(k)) for k in (2, 4, 6)]]
    concatenate x1 -> x0, local copies, waits for them, and re-layouts: 4.67 us -> none  [per_device(): got = shift(jnp.concatenate([give, split_small(small)], axis=0), 'c', 1, 2)]
    all_to_all x1, waiting for transfers between devices: 13 us -> 10.2 us  [per_device(): lax.all_to_all(jnp.broadcast_to(piece, (32, part, CH)), PLANE, 0, 0, tile...]
    all_to_all x1, blocking collectives: 24.7 us -> 25.9 us  [per_device(): spread = lax.all_to_all(spread, PLANE, 0, 0, tiled=True)]
    unnamed x22 -> x18, local copies, waits for them, and re-layouts: 5.57 us -> 6.28 us
    ppermute x6 -> x5, starting transfers between devices: 13.3 us -> 13.5 us  [the longest x3 6.91 us: per_device(): one, two, three = [lax.ppermute(send, DEPTH, ring(k)) for k in (2, 4, 6)]]
  transfers between devices with their start and end apart: 9 -> 8, of which waited for: 6 -> 4; matrix products, arithmetic and copies ran while one was open for 2% -> 2% of each run, Pallas kernels for 7% -> 8%
where the time goes in v4:
time: 101 us; the launch traced here: 100 us
  blocking collectives  25.9 us (26%)
  starting transfers between devices  23.7 us (23%)
  Pallas kernels  23.1 us (23%)
  waiting for transfers between devices  16.4 us (16%)
  local copies, waits for them, and re-layouts  9.22 us (9%)
  other arithmetic  1.14 us (1%)
    all_to_all x1, blocking collectives, per_device(): spread = lax.all_to_all(spread, PLANE, 0, 0, tiled=True)  25.9 us
    pallas_call x6, Pallas kernels, call(): pl.pallas_call(kernel, out_shape=shapes, in_specs=list(ins), input_output...  23.1 us
    all_to_all x1, waiting for transfers between devices, per_device(): lax.all_to_all(jnp.broadcast_to(piece, (32, part, CH)), PLANE, 0, 0, tile...  10.2 us
    ppermute x3, starting transfers between devices, per_device(): one, two, three = [lax.ppermute(send, DEPTH, ring(k)) for k in (2, 4, 6)]  6.91 us
    unnamed x18, local copies, waits for them, and re-layouts  6.28 us
    ppermute x2, starting transfers between devices, shift(): lax.ppermute(value, axis, [(i, (i + step) % size) for i in range(size)])  5.36 us
    all_to_all x1, starting transfers between devices, per_device(): lax.all_to_all(jnp.broadcast_to(piece, (32, part, CH)), PLANE, 0, 0, tile...  4.81 us
    ppermute x1, starting transfers between devices, per_device(): below = lax.ppermute(up, DEPTH, ring(7))  4.03 us
  transfers between devices with their start and end apart: 8, of which 4 were waited for; matrix products, arithmetic and copies ran while one was open for 2% of the time, Pallas kernels for 8%

profile of v4, /device:TPU:1, one launch (start us, length us, event | category | flops | bytes accessed | tf_op | source)
XLA Modules:
  0.0 100.4 jit_solution(15255765252812476620)
XLA Ops:
  0.6 1.1 %copy-done = bf16[1,16,96,256]{3,2,1,0:T(8,128)(2,1)S(1)} copy-done((bf16[1,16,96,256]{3,2,1,0:T(8,128)(2,1)S(1)}, bf16[1,16,96,256]{3,2,1,0:T(8,128)(2,1)}, u32[]{:S(2)}) %copy-start) | copy-done | bytes 786456
  2.5 2.5 %collective-permute-start = (bf16[400,256]{1,0:T(8,128)(2,1)S(1)}, bf16[400,256]{1,0:T(8,128)(2,1)S(1)}, u32[]{:S(2)}, u32[]{:S(2)}) collective-permute-start(bf16[400,256]{1,0:T(8,128)(2,1)S(1)} %get-tuple-element.22), channel_id=1, source_target_pairs={{0,64},{64,128},{128,192},{192,8},{8,72},{72,136},{136,200},{200,0... | collective-permute-start | bytes 614408 | tf_op jit(solution)/shard_map/ppermute | solution.py:285
  5.1 4.0 %collective-permute-start.1 = (bf16[400,256]{1,0:T(8,128)(2,1)S(1)}, bf16[400,256]{1,0:T(8,128)(2,1)S(1)}, u32[]{:S(2)}, u32[]{:S(2)}) collective-permute-start(bf16[400,256]{1,0:T(8,128)(2,1)S(1)} %get-tuple-element.23), channel_id=1, source_target_pairs={{0,200},{64,0},{128,64},{192,128},{8,192},{72,8},{136,72},{200,136... | collective-permute-start | bytes 614408 | tf_op jit(solution)/shard_map/ppermute | solution.py:286
  9.8 1.3 %copy-done.2 = bf16[3,3,256,256]{3,2,1,0:T(8,128)(2,1)S(1)} copy-done((bf16[3,3,256,256]{3,2,1,0:T(8,128)(2,1)S(1)}, bf16[3,3,256,256]{3,2,1,0:T(8,128)(2,1)}, u32[]{:S(2)}) %copy-start.2) | copy-done | bytes 1179672
  11.1 1.3 %copy-done.4 = bf16[3,3,256,256]{3,2,1,0:T(8,128)(2,1)S(1)} copy-done((bf16[3,3,256,256]{3,2,1,0:T(8,128)(2,1)S(1)}, bf16[3,3,256,256]{3,2,1,0:T(8,128)(2,1)}, u32[]{:S(2)}) %copy-start.4) | copy-done | bytes 1179672
  12.3 2.4 %inner.1 = (bf16[1536,768]{1,0:T(8,128)(2,1)S(1)}, bf16[1344,768]{1,0:T(8,128)(2,1)S(1)}, f32[1344,256]{1,0:T(8,128)S(1)}, bf16[2304,256]{1,0:T(8,128)(2,1)S(1)}, bf16[2304,256]{1,0:T(8,128)(2,1)S(1)}) custom-call(bf16[1536,256]{1,0:T(8,128)(2,1)S(1)} %get-tuple-element.24.f, bf16[2304,256]{1,0:T(8,128)(2,1)S(1)} %bitcast.20, bf16[2304,256]{1,0:T(8,128)(2,1)S(1)} %bitcast.22), custom_call_target="tpu_custom_call" | custom-call | flops 5000000000 | bytes 3145728 | tf_op jit(solution)/shard_map/inner/pallas_call | solution.py:31
  14.9 13.1 %main.1 = (bf16[2304,256]{1,0:T(8,128)(2,1)S(1)}, bf16[2304,256]{1,0:T(8,128)(2,1)S(1)}, f32[8,256]{1,0:T(8,128)S(1)}, bf16[1728,256]{1,0:T(8,128)(2,1)S(1)}) custom-call(s32[2]{0:T(128)S(1)} %pad_add_fusion.ids, bf16[400,256]{1,0:T(8,128)(2,1)S(1)} %collective-permute-done.above, bf16[400,256]{1,0:T(8,128)(2,1)S(1)} %collective-permute-done.1.below, ...), custom_call_target="tpu_custom_call" | custom-call | flops 8999999488 | bytes 9766920 | tf_op jit(solution)/shard_map/main/pallas_call | solution.py:31
  28.2 0.7 copy-done.6
  29.0 1.2 %collective-permute-start.2 = (bf16[2320,256]{1,0:T(8,128)(2,1)S(1)}, bf16[2320,256]{1,0:T(8,128)(2,1)S(1)}, u32[]{:S(2)}, u32[]{:S(2)}) collective-permute-start(bf16[2320,256]{1,0:T(8,128)(2,1)S(1)} %pad_maximum_fusion.1), channel_id=1, source_target_pairs={{0,1},{1,0},{2,3},{3,2},{4,5},{5,4},{6,7},{7,6},{8,9},{9,8},{10,11... | collective-permute-start | bytes 3563528 | tf_op jit(solution)/shard_map/ppermute | solution.py:255
  30.2 2.5 %collective-permute-done.2 = bf16[2320,256]{1,0:T(8,128)(2,1)S(1)} collective-permute-done((bf16[2320,256]{1,0:T(8,128)(2,1)S(1)}, bf16[2320,256]{1,0:T(8,128)(2,1)S(1)}, u32[]{:S(2)}, u32[]{:S(2)}) %collective-permute-start.2) | collective-permute-done | bytes 1187872 | tf_op jit(solution)/shard_map/ppermute | solution.py:255
  33.3 25.9 %all_to_all.10 = bf16[32,80,256]{2,1,0:T(8,128)(2,1)S(1)} all-to-all(bf16[32,80,256]{2,1,0:T(8,128)(2,1)S(1)} %pad_maximum_fusion), channel_id=1, replica_groups=mesh['q'=2,'p'=2,'x'=4,'h'=2,'y'=4,'c'=2] {'p','x','y'}, dimensions={0} | all-to-all | bytes 2621440 | tf_op jit(solution)/shard_map/all_to_all | solution.py:330
  59.5 3.0 %collective-permute-start.5 = (bf16[80,256]{1,0:T(8,128)(2,1)S(1)}, bf16[80,256]{1,0:T(8,128)(2,1)S(1)}, u32[]{:S(2)}, u32[]{:S(2)}) collective-permute-start(bf16[80,256]{1,0:T(8,128)(2,1)S(1)} %pad_maximum_fusion.2), channel_id=1, source_target_pairs={{0,136},{64,200},{128,0},{192,64},{8,128},{72,192},{136,8},{200,72... | collective-permute-start | bytes 122888 | tf_op jit(solution)/shard_map/ppermute | solution.py:335
  62.4 0.7 collective-permute-start.4
  63.2 3.2 %collective-permute-start.3 = (bf16[80,256]{1,0:T(8,128)(2,1)S(1)}, bf16[80,256]{1,0:T(8,128)(2,1)S(1)}, u32[]{:S(2)}, u32[]{:S(2)}) collective-permute-start(bf16[80,256]{1,0:T(8,128)(2,1)S(1)} %pad_maximum_fusion.2), channel_id=1, source_target_pairs={{0,8},{64,72},{128,136},{192,200},{8,0},{72,64},{136,128},{200,192... | collective-permute-start | bytes 122888 | tf_op jit(solution)/shard_map/ppermute | solution.py:335
  66.4 1.1 %collective-permute-done.4 = bf16[80,256]{1,0:T(8,128)(2,1)S(1)} collective-permute-done((bf16[80,256]{1,0:T(8,128)(2,1)S(1)}, bf16[80,256]{1,0:T(8,128)(2,1)S(1)}, u32[]{:S(2)}, u32[]{:S(2)}) %collective-permute-start.4) | collective-permute-done | bytes 40992 | tf_op jit(solution)/shard_map/ppermute | solution.py:335
  67.4 2.6 %collective-permute-done.3 = bf16[80,256]{1,0:T(8,128)(2,1)S(1)} collective-permute-done((bf16[80,256]{1,0:T(8,128)(2,1)S(1)}, bf16[80,256]{1,0:T(8,128)(2,1)S(1)}, u32[]{:S(2)}, u32[]{:S(2)}) %collective-permute-start.3) | collective-permute-done | bytes 40992 | tf_op jit(solution)/shard_map/ppermute | solution.py:335
  70.1 1.1 %broadcast_in_dim.14 = bf16[32,72,256]{2,1,0:T(8,128)(2,1)} broadcast(bf16[72,256]{1,0:T(8,128)(2,1)S(1)} %add_convert_fusion.1), dimensions={1,2} | broadcast | bytes 1216512 | tf_op jit(solution)/shard_map/broadcast_in_dim | solution.py:343
  71.2 4.8 %all-to-all-start.1 = ((bf16[32,72,256]{2,1,0:T(8,128)(2,1)}), bf16[32,72,256]{2,1,0:T(8,128)(2,1)S(1)}, u32[]{:S(2)}, u32[]{:S(2)}) async-start(bf16[32,72,256]{2,1,0:T(8,128)(2,1)} %broadcast_in_dim.14), calls=%async_computation.1 | async-start | bytes 2359296 | tf_op jit(solution)/shard_map/all_to_all | solution.py:343
  76.0 1.2 %copy-done.7 = bf16[1728,256]{1,0:T(8,128)(2,1)S(1)} copy-done((bf16[1728,256]{1,0:T(8,128)(2,1)S(1)}, bf16[1728,256]{1,0:T(8,128)(2,1)}, u32[]{:S(2)}) %copy-start.7) | copy-done | bytes 884760
  77.2 3.5 %feature.1 = bf16[1536,256]{1,0:T(8,128)(2,1)} custom-call(bf16[1728,256]{1,0:T(8,128)(2,1)S(1)} %copy-done.7, bf16[2304,256]{1,0:T(8,128)(2,1)S(1)} %get-tuple-element.31.k1t), custom_call_target="tpu_custom_call" | custom-call | flops 2500000000 | bytes 2064384 | tf_op jit(solution)/shard_map/feature/pallas_call | solution.py:31
  80.6 10.2 %all-to-all-done.1 = bf16[32,72,256]{2,1,0:T(8,128)(2,1)S(1)} async-done(((bf16[32,72,256]{2,1,0:T(8,128)(2,1)}), bf16[32,72,256]{2,1,0:T(8,128)(2,1)S(1)}, u32[]{:S(2)}, u32[]{:S(2)}) %all-to-all-start.1) | async-done | bytes 1179680 | tf_op jit(solution)/shard_map/all_to_all | solution.py:343
  90.9 4.1 %collective-permute-start.6 = (bf16[2304,256]{1,0:T(8,128)(2,1)S(1)}, bf16[2304,256]{1,0:T(8,128)(2,1)S(1)}, u32[]{:S(2)}, u32[]{:S(2)}) collective-permute-start(bf16[2304,256]{1,0:T(8,128)(2,1)S(1)} %bitcast.16), channel_id=1, source_target_pairs={{0,1},{1,0},{2,3},{3,2},{4,5},{5,4},{6,7},{7,6},{8,9},{9,8},{10,11... | collective-permute-start | bytes 3538952 | tf_op jit(solution)/shard_map/ppermute | solution.py:255
  96.1 2.0 %mine.1 = (f32[2304,256]{1,0:T(8,128)}, f32[2304,256]{1,0:T(8,128)}) custom-call(s32[2]{0:T(128)S(1)} %pad_add_fusion.ids, bf16[2304,256]{1,0:T(8,128)(2,1)S(1)} %bitcast.17), custom_call_target="tpu_custom_call" | custom-call | flops 1000000000 | bytes 1179656 | tf_op jit(solution)/shard_map/mine/pallas_call | solution.py:31
  98.2 2.0 %other.1 = (f32[2304,256]{1,0:T(8,128)}, f32[2304,256]{1,0:T(8,128)}) custom-call(s32[2]{0:T(128)S(1)} %pad_add_fusion.ids, bf16[2304,256]{1,0:T(8,128)(2,1)S(1)} %collective-permute-done.6.other, f32[2304,256]{1,0:T(8,128)} %get-tuple-element.35.g1_in, f32[2304,256]{1,0:T(8,128)} %get-tuple-element.36.g2_in), custom_call_target="tpu_custom_call", output_to_operand_aliasing={{0}: (2, {}), {1}: (3, {})} | custom-call | bytes 5898248 | tf_op jit(solution)/shard_map/other/pallas_call | solution.py:31
  (44 shorter events, 3.8 us)
Async XLA Ops:
  0.6 1.1 %copy-start = (bf16[1,16,96,256]{3,2,1,0:T(8,128)(2,1)S(1)}, bf16[1,16,96,256]{3,2,1,0:T(8,128)(2,1)}, u32[]{:S(2)}) copy-start(bf16[1,16,96,256]{3,2,1,0:T(8,128)(2,1)} %param.6) | copy-start | bytes 2359300
  1.8 0.7 copy-start.1
  2.5 12.3 %collective-permute-start = (bf16[400,256]{1,0:T(8,128)(2,1)S(1)}, bf16[400,256]{1,0:T(8,128)(2,1)S(1)}, u32[]{:S(2)}, u32[]{:S(2)}) collective-permute-start(bf16[400,256]{1,0:T(8,128)(2,1)S(1)} %get-tuple-element.22), channel_id=1, source_target_pairs={{0,64},{64,128},{128,192},{192,8},{8,72},{72,136},{136,200},{200,0... | collective-permute-start | bytes 614408 | tf_op jit(solution)/shard_map/ppermute | solution.py:285
  5.1 9.8 %collective-permute-start.1 = (bf16[400,256]{1,0:T(8,128)(2,1)S(1)}, bf16[400,256]{1,0:T(8,128)(2,1)S(1)}, u32[]{:S(2)}, u32[]{:S(2)}) collective-permute-start(bf16[400,256]{1,0:T(8,128)(2,1)S(1)} %get-tuple-element.23), channel_id=1, source_target_pairs={{0,200},{64,0},{128,64},{192,128},{8,192},{72,8},{136,72},{200,136... | collective-permute-start | bytes 614408 | tf_op jit(solution)/shard_map/ppermute | solution.py:286
  9.8 1.3 %copy-start.2 = (bf16[3,3,256,256]{3,2,1,0:T(8,128)(2,1)S(1)}, bf16[3,3,256,256]{3,2,1,0:T(8,128)(2,1)}, u32[]{:S(2)}) copy-start(bf16[3,3,256,256]{3,2,1,0:T(8,128)(2,1)} %param.7) | copy-start | bytes 3538948
  11.1 1.3 %copy-start.4 = (bf16[3,3,256,256]{3,2,1,0:T(8,128)(2,1)S(1)}, bf16[3,3,256,256]{3,2,1,0:T(8,128)(2,1)}, u32[]{:S(2)}) copy-start(bf16[3,3,256,256]{3,2,1,0:T(8,128)(2,1)} %param.8) | copy-start | bytes 3538948
  12.3 2.5 %copy-start.8 = (bf16[256,3]{0,1:T(4,128)(2,1)S(1)}, bf16[256,3]{0,1:T(4,128)(2,1)}, u32[]{:S(2)}) copy-start(bf16[256,3]{0,1:T(4,128)(2,1)} %param.9) | copy-start | bytes 4612
  12.3 2.6 %copy-start.3 = (bf16[3,3,256,256]{3,2,1,0:T(8,128)(2,1)S(1)}, bf16[3,3,256,256]{3,2,1,0:T(8,128)(2,1)}, u32[]{:S(2)}) copy-start(bf16[3,3,256,256]{3,2,1,0:T(8,128)(2,1)} %param.7) | copy-start | bytes 3538948
  12.3 2.6 %copy-start.5 = (bf16[3,3,256,256]{3,2,1,0:T(8,128)(2,1)S(1)}, bf16[3,3,256,256]{3,2,1,0:T(8,128)(2,1)}, u32[]{:S(2)}) copy-start(bf16[3,3,256,256]{3,2,1,0:T(8,128)(2,1)} %param.8) | copy-start | bytes 3538948
  28.0 0.9 copy-start.6
  29.0 3.7 %collective-permute-start.2 = (bf16[2320,256]{1,0:T(8,128)(2,1)S(1)}, bf16[2320,256]{1,0:T(8,128)(2,1)S(1)}, u32[]{:S(2)}, u32[]{:S(2)}) collective-permute-start(bf16[2320,256]{1,0:T(8,128)(2,1)S(1)} %pad_maximum_fusion.1), channel_id=1, source_target_pairs={{0,1},{1,0},{2,3},{3,2},{4,5},{5,4},{6,7},{7,6},{8,9},{9,8},{10,11... | collective-permute-start | bytes 3563528 | tf_op jit(solution)/shard_map/ppermute | solution.py:255
  59.5 6.9 %collective-permute-start.5 = (bf16[80,256]{1,0:T(8,128)(2,1)S(1)}, bf16[80,256]{1,0:T(8,128)(2,1)S(1)}, u32[]{:S(2)}, u32[]{:S(2)}) collective-permute-start(bf16[80,256]{1,0:T(8,128)(2,1)S(1)} %pad_maximum_fusion.2), channel_id=1, source_target_pairs={{0,136},{64,200},{128,0},{192,64},{8,128},{72,192},{136,8},{200,72... | collective-permute-start | bytes 122888 | tf_op jit(solution)/shard_map/ppermute | solution.py:335
  62.4 5.0 %collective-permute-start.4 = (bf16[80,256]{1,0:T(8,128)(2,1)S(1)}, bf16[80,256]{1,0:T(8,128)(2,1)S(1)}, u32[]{:S(2)}, u32[]{:S(2)}) collective-permute-start(bf16[80,256]{1,0:T(8,128)(2,1)S(1)} %pad_maximum_fusion.2), channel_id=1, source_target_pairs={{0,128},{64,192},{128,8},{192,72},{8,136},{72,200},{136,0},{200,64... | collective-permute-start | bytes 122888 | tf_op jit(solution)/shard_map/ppermute | solution.py:335
  63.2 6.9 %collective-permute-start.3 = (bf16[80,256]{1,0:T(8,128)(2,1)S(1)}, bf16[80,256]{1,0:T(8,128)(2,1)S(1)}, u32[]{:S(2)}, u32[]{:S(2)}) collective-permute-start(bf16[80,256]{1,0:T(8,128)(2,1)S(1)} %pad_maximum_fusion.2), channel_id=1, source_target_pairs={{0,8},{64,72},{128,136},{192,200},{8,0},{72,64},{136,128},{200,192... | collective-permute-start | bytes 122888 | tf_op jit(solution)/shard_map/ppermute | solution.py:335
  71.2 19.7 %all-to-all-start.1 = ((bf16[32,72,256]{2,1,0:T(8,128)(2,1)}), bf16[32,72,256]{2,1,0:T(8,128)(2,1)S(1)}, u32[]{:S(2)}, u32[]{:S(2)}) async-start(bf16[32,72,256]{2,1,0:T(8,128)(2,1)} %broadcast_in_dim.14), calls=%async_computation.1 | async-start | bytes 2359296 | tf_op jit(solution)/shard_map/all_to_all | solution.py:343
  76.0 1.2 %copy-start.7 = (bf16[1728,256]{1,0:T(8,128)(2,1)S(1)}, bf16[1728,256]{1,0:T(8,128)(2,1)}, u32[]{:S(2)}) copy-start(bf16[1728,256]{1,0:T(8,128)(2,1)} %copy-done.6) | copy-start | bytes 2654212
  90.9 7.3 %collective-permute-start.6 = (bf16[2304,256]{1,0:T(8,128)(2,1)S(1)}, bf16[2304,256]{1,0:T(8,128)(2,1)S(1)}, u32[]{:S(2)}, u32[]{:S(2)}) collective-permute-start(bf16[2304,256]{1,0:T(8,128)(2,1)S(1)} %bitcast.16), channel_id=1, source_target_pairs={{0,1},{1,0},{2,3},{3,2},{4,5},{5,4},{6,7},{7,6},{8,9},{9,8},{10,11... | collective-permute-start | bytes 3538952 | tf_op jit(solution)/shard_map/ppermute | solution.py:255

commit v5 on v4

--- a/solution.py
+++ b/solution.py
@@ -12,6 +12,7 @@
 PIX = ROWS * COLS
 EDGE = HALO * COLS
 BLOCK = EDGE + 16
+R2 = 10
 F32 = jnp.float32
 BF16 = jnp.bfloat16
 ROWWISE = (((0,), (0,)), ((), ()))
@@ -91,7 +92,12 @@
     labels[...] = lab[...]
 
 
-def inner_kernel(f, k1, k2, fw, aw, slope, k1t, k2t):
+def flip(src, dst):
+    for t in range(9):
+        dst[t * CH:(t + 1) * CH, :] = src[(8 - t) * CH:(9 - t) * CH, :].T
+
+
+def inner_kernel(f, k1, k2, fw, aw, slope, k2t):
     def widen(t, c):
         store_wide(fw, t * (2 * COLS), load_rows(f, t * (2 * COLS), 2))
         return c
@@ -105,15 +111,17 @@
         slope[pl.ds(at, 2 * COLS), :] = (s * (1.0 + v * (1.0 - s))).reshape(2 * COLS, CH)
         store_wide(aw, at, v * s)
 
-    for t in range(9):
-        for src, dst in ((k1, k1t), (k2, k2t)):
-            dst[t * CH:(t + 1) * CH, :] = src[(8 - t) * CH:(9 - t) * CH, :].T
+    flip(k2, k2t)
 
 
 def make_main(height, scale):
-    def main(ids, above, below, fwi, awi, slopei, k1, k2, k2t, cls, bias, lab, g1, g2, small, fg,
-             fw, aw, sw, fgw, gt, slope, labs):
+    def main(ids, bias, above, below, fwi, awi, slopei, k1, k2, k2t, classes, lab, g1, g2, small, fg,
+             fw, aw, sw, fgw, gt, slope, labs, held, cls32, cls):
         base = ids[0] * ROWS
+        cls32[...] = jnp.zeros_like(cls32)
+        cls32[0:3, :] = classes[...].astype(F32)
+        cls32[3:6, :] = classes[...].astype(F32)
+        cls[...] = cls32[...].astype(BF16)
         fw[EDGE:EDGE + PIX, :] = fwi[...]
         for half in range(2):
             at = half * 2 * COLS
@@ -130,7 +138,7 @@
         lines += [mine[r:r + 1, :] for r in range(ROWS)]
         lines += [tags[1][0:1, 0:COLS], tags[1][1:2, 0:COLS]]
         for r, line in enumerate(lines):
-            labs[r // 10, 0:1, (r % 10) * COLS:(r % 10 + 1) * COLS] = line
+            labs[r // R2, 0:1, (r % R2) * COLS:(r % R2 + 1) * COLS] = line
 
         def first(t, c):
             at = t * (18 * COLS)
@@ -145,39 +153,46 @@
 
         small[...] = jnp.zeros_like(small)
         lane = lax.broadcasted_iota(jnp.int32, (1, CH), 1)
-        pixel = lax.broadcasted_iota(jnp.int32, (1, 10 * COLS), 1)
-
-        def second(t, c):
-            at = t * (10 * COLS)
-            v = conv_rows(aw, at, 10, k2)
+        pixel = lax.broadcasted_iota(jnp.int32, (1, R2 * COLS), 1)
+
+        def wide_act(t):
+            held[t % 2, :, :] = conv_rows(aw, t * (R2 * COLS), R2, k2).reshape(R2 * COLS, CH)
+
+        def second(t):
+            at = t * (R2 * COLS)
+            v = held[t % 2, :, :].reshape(R2, COLS, CH)
             s = sigmoid(v)
-            act = (v * s).astype(BF16).reshape(10 * COLS, CH)
+            act = (v * s).astype(BF16).reshape(R2 * COLS, CH)
             logit = lax.dot_general(
                 cls[...], act, (((1,), (1,)), ((), ())), preferred_element_type=F32
             )
-            rows = [logit[k:k + 1, :] + bias[k:k + 1, 0:1] for k in range(3)]
+            rows = [logit[k:k + 1, :] + bias[k] for k in range(3)]
             top = jnp.maximum(jnp.maximum(rows[0], rows[1]), rows[2])
             ex = [jnp.exp(row - top) for row in rows]
             den = ex[0] + ex[1] + ex[2]
-            label = labs[t][0:1, 0:10 * COLS]
+            label = labs[t, 0:1, 0:R2 * COLS]
             place = pixel + at
             own = jnp.where(jnp.logical_and(place >= 2 * COLS, place < 18 * COLS), 1.0, 0.0)
             dl = [(ex[k] / den - jnp.where(label == k, 1.0, 0.0)) * scale for k in range(3)]
             hi = [d.astype(BF16).astype(F32) for d in dl]
             lo = [d - h for d, h in zip(dl, hi)]
-            zero = jnp.zeros((10, 10 * COLS), F32)
+            zero = jnp.zeros((10, R2 * COLS), F32)
             pack = jnp.concatenate(hi + lo + [zero], axis=0)
             back = lax.dot_general(pack.astype(BF16), cls[...], ROWWISE, preferred_element_type=F32)
-            grad = back.reshape(10, COLS, CH) * (s * (1.0 + v * (1.0 - s)))
-            store_wide(sw, at, keep_rows(grad, base - 2 + t * 10, height))
+            grad = back.reshape(R2, COLS, CH) * (s * (1.0 + v * (1.0 - s)))
+            store_wide(sw, at, keep_rows(grad, base - 2 + t * R2, height))
             part = jnp.dot((pack * own).astype(BF16), act, preferred_element_type=F32)
             sums = [jnp.sum(d * own, axis=1, keepdims=True) for d in dl]
             row = jnp.where(lane == 0, sums[0], jnp.where(lane == 1, sums[1], 0.0))
             small[0:3, :] += part[0:3] + part[3:6]
             small[3:4, :] += jnp.where(lane == 2, sums[2], row)
-            return c
-
-        lax.fori_loop(0, 2, second, 0)
+
+        N2 = 20 // R2
+        for t in range(N2 + 1):
+            if t < N2:
+                wide_act(t)
+            if t > 0:
+                second(t - 1)
 
         def weight(grad_wide, skip, src, src_skip, out):
             gt[...] = grad_wide[skip * COLS:(skip + ROWS) * COLS, CH:2 * CH].T
@@ -203,7 +218,11 @@
     return main
 
 
-def feature_kernel(fg, k1t, out, fgw):
+def feature_kernel(fg, k1, sums, out, classes, bias, fgw, k1t):
+    classes[...] = sums[0:3, :]
+    bias[...] = sums[3:4, 0:3]
+    flip(k1, k1t)
+
     def widen(t, c):
         store_wide(fgw, t * (2 * COLS), load_rows(fg, t * (2 * COLS), 2))
         return c
@@ -219,29 +238,32 @@
     lax.fori_loop(0, 2, step, 0)
 
 
-def convert_out(block, wide, out, sems):
+def convert_out(block, wide, out, row, sems):
     copies = []
-    for t in range(9):
-        at = pl.ds(t * CH, CH)
+    for t in range(block.shape[0] // 384):
+        at = pl.ds(t * 384, 384)
         wide[at, :] = block[at, :].astype(F32)
-        copies.append(pltpu.make_async_copy(wide.at[at], out.at[at], sems.at[t]))
+        copies.append(pltpu.make_async_copy(wide.at[at], out.at[pl.ds(row + t * 384, 384)], sems.at[t]))
         copies[-1].start()
     for copy in copies:
         copy.wait()
 
 
-def mine_kernel(ids, mine, g1, g2, wide, sems):
+def mine_kernel(ids, mine, g1, g2, wide, sems, row=0):
     @pl.when(ids[1] == 0)
     def _():
-        convert_out(mine, wide, g1, sems)
+        convert_out(mine, wide, g1, row, sems)
 
     @pl.when(ids[1] == 1)
     def _():
-        convert_out(mine, wide, g2, sems)
-
-
-def other_kernel(ids, other, g1_in, g2_in, g1, g2, wide, sems):
-    mine_kernel(ids, other, g2, g1, wide, sems)
+        convert_out(mine, wide, g2, row, sems)
+
+
+def other_kernel(row):
+    def other(ids, block, g1_in, g2_in, g1, g2, wide, sems):
+        mine_kernel(ids, block, g2, g1, wide, sems, row)
+
+    return other
 
 
 def ring(step):
@@ -285,20 +307,19 @@
     above = lax.ppermute(down, DEPTH, ring(1))
     below = lax.ppermute(up, DEPTH, ring(7))
 
-    fwi, awi, slopei, k1t, k2t = call(
+    fwi, awi, slopei, k2t = call(
         inner_kernel,
         [((PIX, 3 * CH), BF16), ((14 * COLS, 3 * CH), BF16), ((14 * COLS, CH), F32),
-         ((9 * CH, CH), BF16), ((9 * CH, CH), BF16)],
+         ((9 * CH, CH), BF16)],
         (fv, k1, k2), [VMEM] * 3,
         flops=5_000_000_000, name="inner",
     )
 
-    cls = jnp.pad(jnp.concatenate([classifier.T, classifier.T], axis=0), ((0, 10), (0, 0)))
-    bias = jnp.broadcast_to(jnp.pad(class_bias, (0, 5))[:, None], (8, 128))
     g1, g2, small, fg = call(
         make_main(height, scale),
         [((9 * CH, CH), BF16), ((9 * CH, CH), BF16), ((8, CH), F32), ((18 * COLS, CH), BF16)],
-        (ids, above, below, fwi, awi, slopei, k1, k2, k2t, cls, bias, labels), [SMEM] + [VMEM] * 11,
+        (ids, class_bias, above, below, fwi, awi, slopei, k1, k2, k2t, classifier.T, labels),
+        [SMEM] * 2 + [VMEM] * 10,
         [
             pltpu.VMEM((24 * COLS, 3 * CH), BF16),
             pltpu.VMEM((22 * COLS, 3 * CH), BF16),
@@ -306,15 +327,13 @@
             pltpu.VMEM((18 * COLS, 3 * CH), BF16),
             pltpu.VMEM((CH, PIX), BF16),
             pltpu.VMEM((22 * COLS, CH), F32),
-            pltpu.VMEM((2, 8, 1024), F32),
+            pltpu.VMEM((20 // R2, 8, 1024), F32),
+            pltpu.VMEM((2, R2 * COLS, CH), F32),
+            pltpu.VMEM((16, CH), F32),
+            pltpu.VMEM((16, CH), BF16),
         ],
         limit=40, flops=9_000_000_000, name="main",
     )
-    (grad_features,) = call(
-        feature_kernel, [((PIX, CH), BF16)], (fg, k1t), [VMEM] * 2,
-        [pltpu.VMEM((18 * COLS, 3 * CH), BF16)], limit=16, flops=2_500_000_000, name="feature",
-    )
-
     small = small[0:4]
     keep = jnp.where(core == 0, g1, g2)
     give = jnp.where(core == 0, g2, g1)
@@ -340,23 +359,32 @@
     small = four(small, lambda block: join_small(block[part:]))
     piece = four(piece.astype(F32), lambda block: block[:part].astype(F32)).astype(BF16)
 
+    grad_features, grad_classifier, grad_bias = call(
+        feature_kernel, [((PIX, CH), BF16), ((3, CH), F32), ((1, 3), F32)], (fg, k1, small), [VMEM] * 3,
+        [pltpu.VMEM((18 * COLS, 3 * CH), BF16), pltpu.VMEM((9 * CH, CH), BF16)],
+        limit=16, flops=2_500_000_000, name="feature",
+    )
     full = lax.all_to_all(jnp.broadcast_to(piece, (32, part, CH)), PLANE, 0, 0, tiled=True)
+    full, grad_features = lax.optimization_barrier((full, grad_features))
     mine = full.reshape(9 * CH, CH)
-    other = shift(mine, "c", 1, 2)
+    half = 9 * CH // 2
+    others = [shift(mine[k * half:(k + 1) * half], "c", 1, 2) for k in range(2)]
     outs = [((9 * CH, CH), F32)] * 2
-    scratch = [pltpu.VMEM((9 * CH, CH), F32), pltpu.SemaphoreType.DMA((9,))]
-    halves = call(
+    scratch = [pltpu.VMEM((9 * CH, CH), F32), pltpu.SemaphoreType.DMA((6,))]
+    grads = call(
         mine_kernel, outs, (ids, mine), [SMEM, VMEM], scratch,
         limit=8, flops=1_000_000_000, name="mine", out_specs=(HBM, HBM),
     )
-    grad_first, grad_second = call(
-        other_kernel, outs, (ids, other, *halves), [SMEM, VMEM, HBM, HBM], scratch,
-        limit=8, name="other", out_specs=(HBM, HBM), aliases={2: 0, 3: 1},
-    )
+    for k, other in enumerate(others):
+        grads = call(
+            other_kernel(k * half), outs, (ids, other, *grads), [SMEM, VMEM, HBM, HBM], scratch,
+            limit=8, name="other", out_specs=(HBM, HBM), aliases={2: 0, 3: 1},
+        )
+    grad_first, grad_second = grads
     shape = (3, 3, CH, CH)
     return (
         grad_features.reshape(features.shape), grad_first.reshape(shape), grad_second.reshape(shape),
-        small[0:3].T, small[3, 0:3],
+        grad_classifier.T, grad_bias[0],
     )
 
 

time: 101 us -> 109 us (1.079)
  local copies, waits for them, and re-layouts: 9.22 us -> 17 us
    unnamed x18 -> x36, local copies, waits for them, and re-layouts: 6.28 us -> 15.8 us
    ppermute x2 -> x3, starting transfers between devices: 5.36 us -> 6.6 us  [shift(): lax.ppermute(value, axis, [(i, (i + step) % size) for i in range(size)])]
    pallas_call x6 -> x7, Pallas kernels: 23.1 us -> 23.9 us  [call(): pl.pallas_call(kernel, out_shape=shapes, in_specs=list(ins), input_output...]
    ppermute x2 -> x3, waiting for transfers between devices: 2.49 us -> 2.49 us  [shift(): lax.ppermute(value, axis, [(i, (i + step) % size) for i in range(size)])]
  transfers between devices with their start and end apart: 8 -> 9, of which waited for: 4 -> 4; matrix products, arithmetic and copies ran while one was open for 2% -> 0% of each run, Pallas kernels for 8% -> 9%
where the time goes in v5:
time: 109 us; the launch traced here: 108 us
  blocking collectives  25.9 us (24%)
  Pallas kernels  23.9 us (22%)
  starting transfers between devices  23.9 us (22%)
  local copies, waits for them, and re-layouts  17 us (16%)
  waiting for transfers between devices  15.5 us (14%)
  other arithmetic  1.13 us (1%)
    all_to_all x1, blocking collectives, per_device(): spread = lax.all_to_all(spread, PLANE, 0, 0, tiled=True)  25.9 us
    pallas_call x7, Pallas kernels, call(): pl.pallas_call(kernel, out_shape=shapes, in_specs=list(ins), input_output...  23.9 us
    unnamed x36, local copies, waits for them, and re-layouts  15.8 us
    all_to_all x1, waiting for transfers between devices, per_device(): lax.all_to_all(jnp.broadcast_to(piece, (32, part, CH)), PLANE, 0, 0, tile...  9.71 us
    ppermute x3, starting transfers between devices, per_device(): one, two, three = [lax.ppermute(send, DEPTH, ring(k)) for k in (2, 4, 6)]  6.65 us
    ppermute x3, starting transfers between devices, shift(): lax.ppermute(value, axis, [(i, (i + step) % size) for i in range(size)])  6.6 us
    all_to_all x1, starting transfers between devices, per_device(): lax.all_to_all(jnp.broadcast_to(piece, (32, part, CH)), PLANE, 0, 0, tile...  4.07 us
    ppermute x1, starting transfers between devices, per_device(): below = lax.ppermute(up, DEPTH, ring(7))  4.03 us
  transfers between devices with their start and end apart: 9, of which 4 were waited for; matrix products, arithmetic and copies ran while one was open for 0% of the time, Pallas kernels for 9%

profile of v5, /device:TPU:1, one launch (start us, length us, event | category | flops | bytes accessed | tf_op | source)
XLA Modules:
  0.0 108.4 jit_solution(15062357766689983498)
XLA Ops:
  2.5 2.5 %collective-permute-start = (bf16[400,256]{1,0:T(8,128)(2,1)S(1)}, bf16[400,256]{1,0:T(8,128)(2,1)S(1)}, u32[]{:S(2)}, u32[]{:S(2)}) collective-permute-start(bf16[400,256]{1,0:T(8,128)(2,1)S(1)} %get-tuple-element.28), channel_id=1, source_target_pairs={{0,64},{64,128},{128,192},{192,8},{8,72},{72,136},{136,200},{200,0... | collective-permute-start | bytes 614408 | tf_op jit(solution)/shard_map/ppermute | solution.py:307
  5.1 4.0 %collective-permute-start.1 = (bf16[400,256]{1,0:T(8,128)(2,1)S(1)}, bf16[400,256]{1,0:T(8,128)(2,1)S(1)}, u32[]{:S(2)}, u32[]{:S(2)}) collective-permute-start(bf16[400,256]{1,0:T(8,128)(2,1)S(1)} %get-tuple-element.29), channel_id=1, source_target_pairs={{0,200},{64,0},{128,64},{192,128},{8,192},{72,8},{136,72},{200,136... | collective-permute-start | bytes 614408 | tf_op jit(solution)/shard_map/ppermute | solution.py:308
  9.1 1.3 %copy-done.2 = bf16[3,3,256,256]{3,2,1,0:T(8,128)(2,1)S(1)} copy-done((bf16[3,3,256,256]{3,2,1,0:T(8,128)(2,1)S(1)}, bf16[3,3,256,256]{3,2,1,0:T(8,128)(2,1)}, u32[]{:S(2)}) %copy-start.2) | copy-done | bytes 1179672
  10.4 1.3 %copy-done.4 = bf16[3,3,256,256]{3,2,1,0:T(8,128)(2,1)S(1)} copy-done((bf16[3,3,256,256]{3,2,1,0:T(8,128)(2,1)S(1)}, bf16[3,3,256,256]{3,2,1,0:T(8,128)(2,1)}, u32[]{:S(2)}) %copy-start.4) | copy-done | bytes 1179672
  11.7 2.4 %inner.1 = (bf16[1536,768]{1,0:T(8,128)(2,1)S(1)}, bf16[1344,768]{1,0:T(8,128)(2,1)S(1)}, f32[1344,256]{1,0:T(8,128)S(1)}, bf16[2304,256]{1,0:T(8,128)(2,1)S(1)}) custom-call(bf16[1536,256]{1,0:T(8,128)(2,1)S(1)} %get-tuple-element.30.f, bf16[2304,256]{1,0:T(8,128)(2,1)S(1)} %bitcast.21, bf16[2304,256]{1,0:T(8,128)(2,1)S(1)} %bitcast.19), custom_call_target="tpu_custom_call" | custom-call | flops 5000000000 | bytes 3145728 | tf_op jit(solution)/shard_map/inner/pallas_call | solution.py:32
  14.1 1.4 %copy-done.10 = bf16[1536,768]{1,0:T(8,128)(2,1)} copy-done((bf16[1536,768]{1,0:T(8,128)(2,1)}, bf16[1536,768]{1,0:T(8,128)(2,1)S(1)}, u32[]{:S(2)}) %copy-start.10) | copy-done | bytes 2359320
  15.5 1.3 %copy-done.12 = bf16[1344,768]{1,0:T(8,128)(2,1)} copy-done((bf16[1344,768]{1,0:T(8,128)(2,1)}, bf16[1344,768]{1,0:T(8,128)(2,1)S(1)}, u32[]{:S(2)}) %copy-start.12) | copy-done | bytes 2064408
  19.0 1.7 %copy-done.11 = bf16[1536,768]{1,0:T(8,128)(2,1)S(1)} copy-done((bf16[1536,768]{1,0:T(8,128)(2,1)S(1)}, bf16[1536,768]{1,0:T(8,128)(2,1)}, u32[]{:S(2)}) %copy-start.11) | copy-done | bytes 2359320
  20.7 1.6 %copy-done.13 = bf16[1344,768]{1,0:T(8,128)(2,1)S(1)} copy-done((bf16[1344,768]{1,0:T(8,128)(2,1)S(1)}, bf16[1344,768]{1,0:T(8,128)(2,1)}, u32[]{:S(2)}) %copy-start.13) | copy-done | bytes 2064408
  22.3 1.3 %copy-done.15 = f32[1344,256]{1,0:T(8,128)S(1)} copy-done((f32[1344,256]{1,0:T(8,128)S(1)}, f32[1344,256]{1,0:T(8,128)}, u32[]{:S(2)}) %copy-start.15) | copy-done | bytes 1376280
  23.6 1.3 %copy-done.17 = bf16[2304,256]{1,0:T(8,128)(2,1)S(1)} copy-done((bf16[2304,256]{1,0:T(8,128)(2,1)S(1)}, bf16[2304,256]{1,0:T(8,128)(2,1)}, u32[]{:S(2)}) %copy-start.17) | copy-done | bytes 1179672
  24.9 12.3 %main.1 = (bf16[2304,256]{1,0:T(8,128)(2,1)S(1)}, bf16[2304,256]{1,0:T(8,128)(2,1)S(1)}, f32[8,256]{1,0:T(8,128)S(1)}, bf16[1728,256]{1,0:T(8,128)(2,1)S(1)}) custom-call(s32[2]{0:T(128)S(1)} %pad_add_fusion.ids, f32[3]{0:T(128)S(1)} %copy-done.7, bf16[400,256]{1,0:T(8,128)(2,1)S(1)} %collective-permute-done.above, ...), custom_call_target="tpu_custom_call" | custom-call | flops 8999999488 | bytes 9756180 | tf_op jit(solution)/shard_map/main/pallas_call | solution.py:32
  39.4 2.5 %collective-permute-done.2 = bf16[2320,256]{1,0:T(8,128)(2,1)S(1)} collective-permute-done((bf16[2320,256]{1,0:T(8,128)(2,1)S(1)}, bf16[2320,256]{1,0:T(8,128)(2,1)S(1)}, u32[]{:S(2)}, u32[]{:S(2)}) %collective-permute-start.2) | collective-permute-done | bytes 1187872 | tf_op jit(solution)/shard_map/ppermute | solution.py:277
  42.5 25.9 %all_to_all.10 = bf16[32,80,256]{2,1,0:T(8,128)(2,1)S(1)} all-to-all(bf16[32,80,256]{2,1,0:T(8,128)(2,1)S(1)} %pad_maximum_fusion), channel_id=1, replica_groups=mesh['q'=2,'p'=2,'x'=4,'h'=2,'y'=4,'c'=2] {'p','x','y'}, dimensions={0} | all-to-all | bytes 2621440 | tf_op jit(solution)/shard_map/all_to_all | solution.py:349
  68.7 2.6 %collective-permute-start.5 = (bf16[80,256]{1,0:T(8,128)(2,1)S(1)}, bf16[80,256]{1,0:T(8,128)(2,1)S(1)}, u32[]{:S(2)}, u32[]{:S(2)}) collective-permute-start(bf16[80,256]{1,0:T(8,128)(2,1)S(1)} %pad_maximum_fusion.2), channel_id=1, source_target_pairs={{0,136},{64,200},{128,0},{192,64},{8,128},{72,192},{136,8},{200,72... | collective-permute-start | bytes 122888 | tf_op jit(solution)/shard_map/ppermute | solution.py:354
  71.3 4.0 %collective-permute-start.3 = (bf16[80,256]{1,0:T(8,128)(2,1)S(1)}, bf16[80,256]{1,0:T(8,128)(2,1)S(1)}, u32[]{:S(2)}, u32[]{:S(2)}) collective-permute-start(bf16[80,256]{1,0:T(8,128)(2,1)S(1)} %pad_maximum_fusion.2), channel_id=1, source_target_pairs={{0,8},{64,72},{128,136},{192,200},{8,0},{72,64},{136,128},{200,192... | collective-permute-start | bytes 122888 | tf_op jit(solution)/shard_map/ppermute | solution.py:354
  76.3 2.3 %collective-permute-done.3 = bf16[80,256]{1,0:T(8,128)(2,1)S(1)} collective-permute-done((bf16[80,256]{1,0:T(8,128)(2,1)S(1)}, bf16[80,256]{1,0:T(8,128)(2,1)S(1)}, u32[]{:S(2)}, u32[]{:S(2)}) %collective-permute-start.3) | collective-permute-done | bytes 40992 | tf_op jit(solution)/shard_map/ppermute | solution.py:354
  79.7 4.1 %all-to-all-start.1 = ((bf16[32,72,256]{2,1,0:T(8,128)(2,1)}), bf16[32,72,256]{2,1,0:T(8,128)(2,1)S(1)}, u32[]{:S(2)}, u32[]{:S(2)}) async-start(bf16[32,72,256]{2,1,0:T(8,128)(2,1)} %broadcast_in_dim.7), calls=%async_computation.1 | async-start | bytes 2359296 | tf_op jit(solution)/shard_map/all_to_all | solution.py:367
  83.9 3.8 %feature.1 = (bf16[1536,256]{1,0:T(8,128)(2,1)}, f32[3,256]{1,0:T(4,128)}, f32[1,3]{1,0:T(1,128)}) custom-call(bf16[1728,256]{1,0:T(8,128)(2,1)S(1)} %copy-done.9, bf16[2304,256]{1,0:T(8,128)(2,1)S(1)} %bitcast.23, f32[4,256]{1,0:T(4,128)S(1)} %fusion.5.sums), custom_call_target="tpu_custom_call" | custom-call | flops 2500000000 | bytes 2068480 | tf_op jit(solution)/shard_map/feature/pallas_call | solution.py:32
  87.7 9.7 %all-to-all-done.1 = bf16[32,72,256]{2,1,0:T(8,128)(2,1)S(1)} async-done(((bf16[32,72,256]{2,1,0:T(8,128)(2,1)}), bf16[32,72,256]{2,1,0:T(8,128)(2,1)S(1)}, u32[]{:S(2)}, u32[]{:S(2)}) %all-to-all-start.1) | async-done | bytes 1179680 | tf_op jit(solution)/shard_map/all_to_all | solution.py:367
  97.5 5.3 %collective-permute-start.7 = (bf16[1152,256]{1,0:T(8,128)(2,1)S(1)}, bf16[1152,256]{1,0:T(8,128)(2,1)S(1)}, u32[]{:S(2)}, u32[]{:S(2)}) collective-permute-start(bf16[1152,256]{1,0:T(8,128)(2,1)S(1)} %bitcast.29), channel_id=1, source_target_pairs={{0,1},{1,0},{2,3},{3,2},{4,5},{5,4},{6,7},{7,6},{8,9},{9,8},{10,11... | collective-permute-start | bytes 1769480 | tf_op jit(solution)/shard_map/ppermute | solution.py:277
  102.9 2.0 %mine.1 = (f32[2304,256]{1,0:T(8,128)}, f32[2304,256]{1,0:T(8,128)}) custom-call(s32[2]{0:T(128)S(1)} %pad_add_fusion.ids, bf16[2304,256]{1,0:T(8,128)(2,1)S(1)} %bitcast.16), custom_call_target="tpu_custom_call" | custom-call | flops 1000000000 | bytes 1179656 | tf_op jit(solution)/shard_map/mine/pallas_call | solution.py:32
  104.9 1.6 %other.2 = (f32[2304,256]{1,0:T(8,128)}, f32[2304,256]{1,0:T(8,128)}) custom-call(s32[2]{0:T(128)S(1)} %pad_add_fusion.ids, bf16[1152,256]{1,0:T(8,128)(2,1)S(1)} %collective-permute-done.7.block, f32[2304,256]{1,0:T(8,128)} %get-tuple-element.43.g1_in, f32[2304,256]{1,0:T(8,128)} %get-tuple-element.44.g2_in), custom_call_target="tpu_custom_call", output_to_operand_aliasing={{0}: (2, {}), {1}: (3, {})} | custom-call | bytes 5308424 | tf_op jit(solution)/shard_map/other/pallas_call | solution.py:32
  106.6 1.6 %other.3 = (f32[2304,256]{1,0:T(8,128)}, f32[2304,256]{1,0:T(8,128)}) custom-call(s32[2]{0:T(128)S(1)} %pad_add_fusion.ids, bf16[1152,256]{1,0:T(8,128)(2,1)S(1)} %collective-permute-done.6.block, f32[2304,256]{1,0:T(8,128)} %get-tuple-element.45.g1_in, f32[2304,256]{1,0:T(8,128)} %get-tuple-element.46.g2_in), custom_call_target="tpu_custom_call", output_to_operand_aliasing={{0}: (2, {}), {1}: (3, {})} | custom-call | bytes 5308424 | tf_op jit(solution)/shard_map/other/pallas_call | solution.py:32
  (61 shorter events, 9.4 us)
Async XLA Ops:
  0.6 1.1 %copy-start = (bf16[1,16,96,256]{3,2,1,0:T(8,128)(2,1)S(1)}, bf16[1,16,96,256]{3,2,1,0:T(8,128)(2,1)}, u32[]{:S(2)}) copy-start(bf16[1,16,96,256]{3,2,1,0:T(8,128)(2,1)} %param.6) | copy-start | bytes 2359300
  2.5 16.4 %collective-permute-start = (bf16[400,256]{1,0:T(8,128)(2,1)S(1)}, bf16[400,256]{1,0:T(8,128)(2,1)S(1)}, u32[]{:S(2)}, u32[]{:S(2)}) collective-permute-start(bf16[400,256]{1,0:T(8,128)(2,1)S(1)} %get-tuple-element.28), channel_id=1, source_target_pairs={{0,64},{64,128},{128,192},{192,8},{8,72},{72,136},{136,200},{200,0... | collective-permute-start | bytes 614408 | tf_op jit(solution)/shard_map/ppermute | solution.py:307
  5.1 13.9 %collective-permute-start.1 = (bf16[400,256]{1,0:T(8,128)(2,1)S(1)}, bf16[400,256]{1,0:T(8,128)(2,1)S(1)}, u32[]{:S(2)}, u32[]{:S(2)}) collective-permute-start(bf16[400,256]{1,0:T(8,128)(2,1)S(1)} %get-tuple-element.29), channel_id=1, source_target_pairs={{0,200},{64,0},{128,64},{192,128},{8,192},{72,8},{136,72},{200,136... | collective-permute-start | bytes 614408 | tf_op jit(solution)/shard_map/ppermute | solution.py:308
  9.1 1.3 %copy-start.2 = (bf16[3,3,256,256]{3,2,1,0:T(8,128)(2,1)S(1)}, bf16[3,3,256,256]{3,2,1,0:T(8,128)(2,1)}, u32[]{:S(2)}) copy-start(bf16[3,3,256,256]{3,2,1,0:T(8,128)(2,1)} %param.8) | copy-start | bytes 3538948
  10.4 1.3 %copy-start.4 = (bf16[3,3,256,256]{3,2,1,0:T(8,128)(2,1)S(1)}, bf16[3,3,256,256]{3,2,1,0:T(8,128)(2,1)}, u32[]{:S(2)}) copy-start(bf16[3,3,256,256]{3,2,1,0:T(8,128)(2,1)} %param.7) | copy-start | bytes 3538948
  11.7 7.3 %copy-start.3 = (bf16[3,3,256,256]{3,2,1,0:T(8,128)(2,1)S(1)}, bf16[3,3,256,256]{3,2,1,0:T(8,128)(2,1)}, u32[]{:S(2)}) copy-start(bf16[3,3,256,256]{3,2,1,0:T(8,128)(2,1)} %param.8) | copy-start | bytes 3538948
  11.7 7.3 %copy-start.5 = (bf16[3,3,256,256]{3,2,1,0:T(8,128)(2,1)S(1)}, bf16[3,3,256,256]{3,2,1,0:T(8,128)(2,1)}, u32[]{:S(2)}) copy-start(bf16[3,3,256,256]{3,2,1,0:T(8,128)(2,1)} %param.7) | copy-start | bytes 3538948
  11.7 7.3 %copy-start.6 = (bf16[256,3]{0,1:T(4,128)(2,1)S(1)}, bf16[256,3]{0,1:T(4,128)(2,1)}, u32[]{:S(2)}) copy-start(bf16[256,3]{0,1:T(4,128)(2,1)} %param.9) | copy-start | bytes 4612
  11.7 7.3 %copy-start.7 = (f32[3]{0:T(128)S(1)}, f32[3]{0:T(128)}, u32[]{:S(2)}) copy-start(f32[3]{0:T(128)} %bias.1) | copy-start | bytes 40
  14.1 1.4 %copy-start.10 = (bf16[1536,768]{1,0:T(8,128)(2,1)}, bf16[1536,768]{1,0:T(8,128)(2,1)S(1)}, u32[]{:S(2)}) copy-start(bf16[1536,768]{1,0:T(8,128)(2,1)S(1)} %get-tuple-element.31.fwi) | copy-start | bytes 7077892
  15.5 1.3 %copy-start.12 = (bf16[1344,768]{1,0:T(8,128)(2,1)}, bf16[1344,768]{1,0:T(8,128)(2,1)S(1)}, u32[]{:S(2)}) copy-start(bf16[1344,768]{1,0:T(8,128)(2,1)S(1)} %get-tuple-element.32.awi) | copy-start | bytes 6193156
  16.8 1.1 %copy-start.14 = (f32[1344,256]{1,0:T(8,128)}, f32[1344,256]{1,0:T(8,128)S(1)}, u32[]{:S(2)}) copy-start(f32[1344,256]{1,0:T(8,128)S(1)} %get-tuple-element.33.slopei) | copy-start | bytes 4128772
  19.0 1.7 %copy-start.11 = (bf16[1536,768]{1,0:T(8,128)(2,1)S(1)}, bf16[1536,768]{1,0:T(8,128)(2,1)}, u32[]{:S(2)}) copy-start(bf16[1536,768]{1,0:T(8,128)(2,1)} %copy-done.10) | copy-start | bytes 7077892
  20.7 1.6 %copy-start.13 = (bf16[1344,768]{1,0:T(8,128)(2,1)S(1)}, bf16[1344,768]{1,0:T(8,128)(2,1)}, u32[]{:S(2)}) copy-start(bf16[1344,768]{1,0:T(8,128)(2,1)} %copy-done.12) | copy-start | bytes 6193156
  22.3 1.3 %copy-start.15 = (f32[1344,256]{1,0:T(8,128)S(1)}, f32[1344,256]{1,0:T(8,128)}, u32[]{:S(2)}) copy-start(f32[1344,256]{1,0:T(8,128)} %copy-done.14) | copy-start | bytes 4128772
  23.6 1.3 %copy-start.17 = (bf16[2304,256]{1,0:T(8,128)(2,1)S(1)}, bf16[2304,256]{1,0:T(8,128)(2,1)}, u32[]{:S(2)}) copy-start(bf16[2304,256]{1,0:T(8,128)(2,1)} %copy-done.16) | copy-start | bytes 3538948
  38.2 3.7 %collective-permute-start.2 = (bf16[2320,256]{1,0:T(8,128)(2,1)S(1)}, bf16[2320,256]{1,0:T(8,128)(2,1)S(1)}, u32[]{:S(2)}, u32[]{:S(2)}) collective-permute-start(bf16[2320,256]{1,0:T(8,128)(2,1)S(1)} %pad_maximum_fusion.1), channel_id=1, source_target_pairs={{0,1},{1,0},{2,3},{3,2},{4,5},{5,4},{6,7},{7,6},{8,9},{9,8},{10,11... | collective-permute-start | bytes 3563528 | tf_op jit(solution)/shard_map/ppermute | solution.py:277
  68.7 6.7 %collective-permute-start.5 = (bf16[80,256]{1,0:T(8,128)(2,1)S(1)}, bf16[80,256]{1,0:T(8,128)(2,1)S(1)}, u32[]{:S(2)}, u32[]{:S(2)}) collective-permute-start(bf16[80,256]{1,0:T(8,128)(2,1)S(1)} %pad_maximum_fusion.2), channel_id=1, source_target_pairs={{0,136},{64,200},{128,0},{192,64},{8,128},{72,192},{136,8},{200,72... | collective-permute-start | bytes 122888 | tf_op jit(solution)/shard_map/ppermute | solution.py:354
  71.3 5.0 %collective-permute-start.4 = (bf16[80,256]{1,0:T(8,128)(2,1)S(1)}, bf16[80,256]{1,0:T(8,128)(2,1)S(1)}, u32[]{:S(2)}, u32[]{:S(2)}) collective-permute-start(bf16[80,256]{1,0:T(8,128)(2,1)S(1)} %pad_maximum_fusion.2), channel_id=1, source_target_pairs={{0,128},{64,192},{128,8},{192,72},{8,136},{72,200},{136,0},{200,64... | collective-permute-start | bytes 122888 | tf_op jit(solution)/shard_map/ppermute | solution.py:354
  71.3 7.3 %collective-permute-start.3 = (bf16[80,256]{1,0:T(8,128)(2,1)S(1)}, bf16[80,256]{1,0:T(8,128)(2,1)S(1)}, u32[]{:S(2)}, u32[]{:S(2)}) collective-permute-start(bf16[80,256]{1,0:T(8,128)(2,1)S(1)} %pad_maximum_fusion.2), channel_id=1, source_target_pairs={{0,8},{64,72},{128,136},{192,200},{8,0},{72,64},{136,128},{200,192... | collective-permute-start | bytes 122888 | tf_op jit(solution)/shard_map/ppermute | solution.py:354
  79.7 4.1 %copy-start.9 = (bf16[1728,256]{1,0:T(8,128)(2,1)S(1)}, bf16[1728,256]{1,0:T(8,128)(2,1)}, u32[]{:S(2)}) copy-start(bf16[1728,256]{1,0:T(8,128)(2,1)} %copy-done.8) | copy-start | bytes 2654212
  79.7 17.7 %all-to-all-start.1 = ((bf16[32,72,256]{2,1,0:T(8,128)(2,1)}), bf16[32,72,256]{2,1,0:T(8,128)(2,1)S(1)}, u32[]{:S(2)}, u32[]{:S(2)}) async-start(bf16[32,72,256]{2,1,0:T(8,128)(2,1)} %broadcast_in_dim.7), calls=%async_computation.1 | async-start | bytes 2359296 | tf_op jit(solution)/shard_map/all_to_all | solution.py:367
  97.5 7.4 %collective-permute-start.7 = (bf16[1152,256]{1,0:T(8,128)(2,1)S(1)}, bf16[1152,256]{1,0:T(8,128)(2,1)S(1)}, u32[]{:S(2)}, u32[]{:S(2)}) collective-permute-start(bf16[1152,256]{1,0:T(8,128)(2,1)S(1)} %bitcast.29), channel_id=1, source_target_pairs={{0,1},{1,0},{2,3},{3,2},{4,5},{5,4},{6,7},{7,6},{8,9},{9,8},{10,11... | collective-permute-start | bytes 1769480 | tf_op jit(solution)/shard_map/ppermute | solution.py:277
  102.8 3.8 %collective-permute-start.6 = (bf16[1152,256]{1,0:T(8,128)(2,1)S(1)}, bf16[1152,256]{1,0:T(8,128)(2,1)S(1)}, u32[]{:S(2)}, u32[]{:S(2)}) collective-permute-start(bf16[1152,256]{1,0:T(8,128)(2,1)S(1)} %bitcast.28), channel_id=1, source_target_pairs={{0,1},{1,0},{2,3},{3,2},{4,5},{5,4},{6,7},{7,6},{8,9},{9,8},{10,11... | collective-permute-start | bytes 1769480 | tf_op jit(solution)/shard_map/ppermute | solution.py:277
  (3 other events, 2.6 us)

commit v6 on v5

--- a/solution.py
+++ b/solution.py
@@ -238,32 +238,29 @@
     lax.fori_loop(0, 2, step, 0)
 
 
-def convert_out(block, wide, out, row, sems):
+def convert_out(block, wide, out, sems):
     copies = []
-    for t in range(block.shape[0] // 384):
+    for t in range(6):
         at = pl.ds(t * 384, 384)
         wide[at, :] = block[at, :].astype(F32)
-        copies.append(pltpu.make_async_copy(wide.at[at], out.at[pl.ds(row + t * 384, 384)], sems.at[t]))
+        copies.append(pltpu.make_async_copy(wide.at[at], out.at[at], sems.at[t]))
         copies[-1].start()
     for copy in copies:
         copy.wait()
 
 
-def mine_kernel(ids, mine, g1, g2, wide, sems, row=0):
+def mine_kernel(ids, mine, g1, g2, wide, sems):
     @pl.when(ids[1] == 0)
     def _():
-        convert_out(mine, wide, g1, row, sems)
+        convert_out(mine, wide, g1, sems)
 
     @pl.when(ids[1] == 1)
     def _():
-        convert_out(mine, wide, g2, row, sems)
-
-
-def other_kernel(row):
-    def other(ids, block, g1_in, g2_in, g1, g2, wide, sems):
-        mine_kernel(ids, block, g2, g1, wide, sems, row)
-
-    return other
+        convert_out(mine, wide, g2, sems)
+
+
+def other_kernel(ids, other, g1_in, g2_in, g1, g2, wide, sems):
+    mine_kernel(ids, other, g2, g1, wide, sems)
 
 
 def ring(step):
@@ -304,6 +301,8 @@
         [((BLOCK, CH), BF16), ((BLOCK, CH), BF16), ((PIX, CH), BF16), ((ROWS, COLS), jnp.int32)],
         (flat, lab), [VMEM] * 2, [pltpu.VMEM((16, CH), F32)], limit=8, name="edge",
     )
+    first = core == 0
+    up, down, ids, first = lax.optimization_barrier((up, down, ids, first))
     above = lax.ppermute(down, DEPTH, ring(1))
     below = lax.ppermute(up, DEPTH, ring(7))
 
@@ -312,7 +311,7 @@
         [((PIX, 3 * CH), BF16), ((14 * COLS, 3 * CH), BF16), ((14 * COLS, CH), F32),
          ((9 * CH, CH), BF16)],
         (fv, k1, k2), [VMEM] * 3,
-        flops=5_000_000_000, name="inner",
+        flops=5_000_000_000, limit=12, name="inner",
     )
 
     g1, g2, small, fg = call(
@@ -332,11 +331,11 @@
             pltpu.VMEM((16, CH), F32),
             pltpu.VMEM((16, CH), BF16),
         ],
-        limit=40, flops=9_000_000_000, name="main",
+        limit=22, flops=9_000_000_000, name="main",
     )
     small = small[0:4]
-    keep = jnp.where(core == 0, g1, g2)
-    give = jnp.where(core == 0, g2, g1)
+    keep = jnp.where(first, g1, g2)
+    give = jnp.where(first, g2, g1)
     tail = jnp.pad(split_small(small), ((0, 8), (0, 0)))
     got = shift(jnp.concatenate([give, tail], axis=0), "c", 1, 2)
     total = (keep.astype(F32) + got[:9 * CH].astype(F32)).astype(BF16)
@@ -362,25 +361,22 @@
     grad_features, grad_classifier, grad_bias = call(
         feature_kernel, [((PIX, CH), BF16), ((3, CH), F32), ((1, 3), F32)], (fg, k1, small), [VMEM] * 3,
         [pltpu.VMEM((18 * COLS, 3 * CH), BF16), pltpu.VMEM((9 * CH, CH), BF16)],
-        limit=16, flops=2_500_000_000, name="feature",
+        limit=12, flops=2_500_000_000, name="feature",
     )
     full = lax.all_to_all(jnp.broadcast_to(piece, (32, part, CH)), PLANE, 0, 0, tiled=True)
     full, grad_features = lax.optimization_barrier((full, grad_features))
     mine = full.reshape(9 * CH, CH)
-    half = 9 * CH // 2
-    others = [shift(mine[k * half:(k + 1) * half], "c", 1, 2) for k in range(2)]
+    other = shift(mine, "c", 1, 2)
     outs = [((9 * CH, CH), F32)] * 2
     scratch = [pltpu.VMEM((9 * CH, CH), F32), pltpu.SemaphoreType.DMA((6,))]
-    grads = call(
+    halves = call(
         mine_kernel, outs, (ids, mine), [SMEM, VMEM], scratch,
         limit=8, flops=1_000_000_000, name="mine", out_specs=(HBM, HBM),
     )
-    for k, other in enumerate(others):
-        grads = call(
-            other_kernel(k * half), outs, (ids, other, *grads), [SMEM, VMEM, HBM, HBM], scratch,
-            limit=8, name="other", out_specs=(HBM, HBM), aliases={2: 0, 3: 1},
-        )
-    grad_first, grad_second = grads
+    grad_first, grad_second = call(
+        other_kernel, outs, (ids, other, *halves), [SMEM, VMEM, HBM, HBM], scratch,
+        limit=8, name="other", out_specs=(HBM, HBM), aliases={2: 0, 3: 1},
+    )
     shape = (3, 3, CH, CH)
     return (
         grad_features.reshape(features.shape), grad_first.reshape(shape), grad_second.reshape(shape),

time: 109 us -> 98.2 us (0.901)
  local copies, waits for them, and re-layouts: 17 us -> 5.48 us
  waiting for transfers between devices: 15.5 us -> 17 us
  Pallas kernels: 23.9 us -> 22.8 us
    unnamed x36 -> x16, local copies, waits for them, and re-layouts: 15.8 us -> 4.38 us
    pallas_call x7 -> x6, Pallas kernels: 23.9 us -> 22.8 us  [call(): pl.pallas_call(kernel, out_shape=shapes, in_specs=list(ins), input_output...]
    ppermute x3 -> x2, starting transfers between devices: 6.6 us -> 5.51 us  [shift(): lax.ppermute(value, axis, [(i, (i + step) % size) for i in range(size)])]
    ppermute x3 -> x2, waiting for transfers between devices: 2.49 us -> 2.93 us  [shift(): lax.ppermute(value, axis, [(i, (i + step) % size) for i in range(size)])]
  transfers between devices with their start and end apart: 9 -> 8, of which waited for: 4 -> 5; matrix products, arithmetic and copies ran while one was open for 0% -> 0% of each run, Pallas kernels for 9% -> 8%
where the time goes in v6:
time: 98.2 us; the launch traced here: 97.8 us
  blocking collectives  26.1 us (27%)
  starting transfers between devices  24.3 us (25%)
  Pallas kernels  22.8 us (23%)
  waiting for transfers between devices  17 us (17%)
  local copies, waits for them, and re-layouts  5.48 us (6%)
  other arithmetic  1.14 us (1%)
  between operations  1 us (1%)
    all_to_all x1, blocking collectives, per_device(): spread = lax.all_to_all(spread, PLANE, 0, 0, tiled=True)  26.1 us
    pallas_call x6, Pallas kernels, call(): pl.pallas_call(kernel, out_shape=shapes, in_specs=list(ins), input_output...  22.8 us
    all_to_all x1, waiting for transfers between devices, per_device(): lax.all_to_all(jnp.broadcast_to(piece, (32, part, CH)), PLANE, 0, 0, tile...  10.4 us
    ppermute x3, starting transfers between devices, per_device(): one, two, three = [lax.ppermute(send, DEPTH, ring(k)) for k in (2, 4, 6)]  7.65 us
    ppermute x2, starting transfers between devices, shift(): lax.ppermute(value, axis, [(i, (i + step) % size) for i in range(size)])  5.51 us
    all_to_all x1, starting transfers between devices, per_device(): lax.all_to_all(jnp.broadcast_to(piece, (32, part, CH)), PLANE, 0, 0, tile...  4.54 us
    unnamed x16, local copies, waits for them, and re-layouts  4.38 us
    ppermute x1, starting transfers between devices, per_device(): below = lax.ppermute(up, DEPTH, ring(7))  4.03 us
  transfers between devices with their start and end apart: 8, of which 5 were waited for; matrix products, arithmetic and copies ran while one was open for 0% of the time, Pallas kernels for 8%

profile of v6, /device:TPU:1, one launch (start us, length us, event | category | flops | bytes accessed | tf_op | source)
XLA Modules:
  0.0 97.8 jit_solution(8875418315652124840)
XLA Ops:
  0.7 1.1 %copy-done = bf16[1,16,96,256]{3,2,1,0:T(8,128)(2,1)S(1)} copy-done((bf16[1,16,96,256]{3,2,1,0:T(8,128)(2,1)S(1)}, bf16[1,16,96,256]{3,2,1,0:T(8,128)(2,1)}, u32[]{:S(2)}) %copy-start) | copy-done | bytes 786456
  1.9 0.7 copy-done.1
  2.6 2.5 %collective-permute-start = (bf16[400,256]{1,0:T(8,128)(2,1)S(1)}, bf16[400,256]{1,0:T(8,128)(2,1)S(1)}, u32[]{:S(2)}, u32[]{:S(2)}) collective-permute-start(bf16[400,256]{1,0:T(8,128)(2,1)S(1)} %get-tuple-element.34), channel_id=1, source_target_pairs={{0,64},{64,128},{128,192},{192,8},{8,72},{72,136},{136,200},{200,0... | collective-permute-start | bytes 614408 | tf_op jit(solution)/shard_map/ppermute | solution.py:306
  5.2 4.0 %collective-permute-start.1 = (bf16[400,256]{1,0:T(8,128)(2,1)S(1)}, bf16[400,256]{1,0:T(8,128)(2,1)S(1)}, u32[]{:S(2)}, u32[]{:S(2)}) collective-permute-start(bf16[400,256]{1,0:T(8,128)(2,1)S(1)} %get-tuple-element.35), channel_id=1, source_target_pairs={{0,200},{64,0},{128,64},{192,128},{8,192},{72,8},{136,72},{200,136... | collective-permute-start | bytes 614408 | tf_op jit(solution)/shard_map/ppermute | solution.py:307
  9.2 1.3 %copy-done.2 = bf16[3,3,256,256]{3,2,1,0:T(8,128)(2,1)S(1)} copy-done((bf16[3,3,256,256]{3,2,1,0:T(8,128)(2,1)S(1)}, bf16[3,3,256,256]{3,2,1,0:T(8,128)(2,1)}, u32[]{:S(2)}) %copy-start.2) | copy-done | bytes 1179672
  10.5 1.3 %copy-done.4 = bf16[3,3,256,256]{3,2,1,0:T(8,128)(2,1)S(1)} copy-done((bf16[3,3,256,256]{3,2,1,0:T(8,128)(2,1)S(1)}, bf16[3,3,256,256]{3,2,1,0:T(8,128)(2,1)}, u32[]{:S(2)}) %copy-start.4) | copy-done | bytes 1179672
  11.8 2.4 %inner.1 = (bf16[1536,768]{1,0:T(8,128)(2,1)S(1)}, bf16[1344,768]{1,0:T(8,128)(2,1)S(1)}, f32[1344,256]{1,0:T(8,128)S(1)}, bf16[2304,256]{1,0:T(8,128)(2,1)S(1)}) custom-call(bf16[1536,256]{1,0:T(8,128)(2,1)S(1)} %get-tuple-element.36.f, bf16[2304,256]{1,0:T(8,128)(2,1)S(1)} %bitcast.20, bf16[2304,256]{1,0:T(8,128)(2,1)S(1)} %bitcast.18), custom_call_target="tpu_custom_call" | custom-call | flops 5000000000 | bytes 3145728 | tf_op jit(solution)/shard_map/inner/pallas_call | solution.py:32
  14.2 12.4 %main.1 = (bf16[2304,256]{1,0:T(8,128)(2,1)S(1)}, bf16[2304,256]{1,0:T(8,128)(2,1)S(1)}, f32[8,256]{1,0:T(8,128)S(1)}, bf16[1728,256]{1,0:T(8,128)(2,1)S(1)}) custom-call(s32[2]{0:T(128)S(1)} %pad_add_fusion.ids, f32[3]{0:T(128)S(1)} %copy-done.7, bf16[400,256]{1,0:T(8,128)(2,1)S(1)} %collective-permute-done.above, ...), custom_call_target="tpu_custom_call" | custom-call | flops 8999999488 | bytes 9756180 | tf_op jit(solution)/shard_map/main/pallas_call | solution.py:32
  26.9 1.0 %collective-permute-start.2 = (bf16[2320,256]{1,0:T(8,128)(2,1)S(1)}, bf16[2320,256]{1,0:T(8,128)(2,1)S(1)}, u32[]{:S(2)}, u32[]{:S(2)}) collective-permute-start(bf16[2320,256]{1,0:T(8,128)(2,1)S(1)} %pad_maximum_fusion.1), channel_id=1, source_target_pairs={{0,1},{1,0},{2,3},{3,2},{4,5},{5,4},{6,7},{7,6},{8,9},{9,8},{10,11... | collective-permute-start | bytes 3563528 | tf_op jit(solution)/shard_map/ppermute | solution.py:274
  27.9 2.5 %collective-permute-done.2 = bf16[2320,256]{1,0:T(8,128)(2,1)S(1)} collective-permute-done((bf16[2320,256]{1,0:T(8,128)(2,1)S(1)}, bf16[2320,256]{1,0:T(8,128)(2,1)S(1)}, u32[]{:S(2)}, u32[]{:S(2)}) %collective-permute-start.2) | collective-permute-done | bytes 1187872 | tf_op jit(solution)/shard_map/ppermute | solution.py:274
  31.0 26.1 %all_to_all.10 = bf16[32,80,256]{2,1,0:T(8,128)(2,1)S(1)} all-to-all(bf16[32,80,256]{2,1,0:T(8,128)(2,1)S(1)} %pad_maximum_fusion), channel_id=1, replica_groups=mesh['q'=2,'p'=2,'x'=4,'h'=2,'y'=4,'c'=2] {'p','x','y'}, dimensions={0} | all-to-all | bytes 2621440 | tf_op jit(solution)/shard_map/all_to_all | solution.py:348
  57.3 3.7 %collective-permute-start.5 = (bf16[80,256]{1,0:T(8,128)(2,1)S(1)}, bf16[80,256]{1,0:T(8,128)(2,1)S(1)}, u32[]{:S(2)}, u32[]{:S(2)}) collective-permute-start(bf16[80,256]{1,0:T(8,128)(2,1)S(1)} %pad_maximum_fusion.2), channel_id=1, source_target_pairs={{0,136},{64,200},{128,0},{192,64},{8,128},{72,192},{136,8},{200,72... | collective-permute-start | bytes 122888 | tf_op jit(solution)/shard_map/ppermute | solution.py:353
  61.1 0.7 collective-permute-start.4
  61.8 3.2 %collective-permute-start.3 = (bf16[80,256]{1,0:T(8,128)(2,1)S(1)}, bf16[80,256]{1,0:T(8,128)(2,1)S(1)}, u32[]{:S(2)}, u32[]{:S(2)}) collective-permute-start(bf16[80,256]{1,0:T(8,128)(2,1)S(1)} %pad_maximum_fusion.2), channel_id=1, source_target_pairs={{0,8},{64,72},{128,136},{192,200},{8,0},{72,64},{136,128},{200,192... | collective-permute-start | bytes 122888 | tf_op jit(solution)/shard_map/ppermute | solution.py:353
  65.0 1.1 %collective-permute-done.4 = bf16[80,256]{1,0:T(8,128)(2,1)S(1)} collective-permute-done((bf16[80,256]{1,0:T(8,128)(2,1)S(1)}, bf16[80,256]{1,0:T(8,128)(2,1)S(1)}, u32[]{:S(2)}, u32[]{:S(2)}) %collective-permute-start.4) | collective-permute-done | bytes 40992 | tf_op jit(solution)/shard_map/ppermute | solution.py:353
  66.1 2.6 %collective-permute-done.3 = bf16[80,256]{1,0:T(8,128)(2,1)S(1)} collective-permute-done((bf16[80,256]{1,0:T(8,128)(2,1)S(1)}, bf16[80,256]{1,0:T(8,128)(2,1)S(1)}, u32[]{:S(2)}, u32[]{:S(2)}) %collective-permute-start.3) | collective-permute-done | bytes 40992 | tf_op jit(solution)/shard_map/ppermute | solution.py:353
  68.7 1.1 %broadcast_in_dim.7 = bf16[32,72,256]{2,1,0:T(8,128)(2,1)} broadcast(bf16[72,256]{1,0:T(8,128)(2,1)S(1)} %add_convert_fusion.1), dimensions={1,2} | broadcast | bytes 1216512 | tf_op jit(solution)/shard_map/broadcast_in_dim | solution.py:366
  69.8 4.5 %all-to-all-start.1 = ((bf16[32,72,256]{2,1,0:T(8,128)(2,1)}), bf16[32,72,256]{2,1,0:T(8,128)(2,1)S(1)}, u32[]{:S(2)}, u32[]{:S(2)}) async-start(bf16[32,72,256]{2,1,0:T(8,128)(2,1)} %broadcast_in_dim.7), calls=%async_computation.1 | async-start | bytes 2359296 | tf_op jit(solution)/shard_map/all_to_all | solution.py:366
  74.4 3.9 %feature.1 = (bf16[1536,256]{1,0:T(8,128)(2,1)}, f32[3,256]{1,0:T(4,128)}, f32[1,3]{1,0:T(1,128)}) custom-call(bf16[1728,256]{1,0:T(8,128)(2,1)S(1)} %get-tuple-element.45.fg, bf16[2304,256]{1,0:T(8,128)(2,1)S(1)} %bitcast.22, f32[4,256]{1,0:T(4,128)S(1)} %fusion.5.sums), custom_call_target="tpu_custom_call" | custom-call | flops 2500000000 | bytes 2068480 | tf_op jit(solution)/shard_map/feature/pallas_call | solution.py:32
  78.2 10.4 %all-to-all-done.1 = bf16[32,72,256]{2,1,0:T(8,128)(2,1)S(1)} async-done(((bf16[32,72,256]{2,1,0:T(8,128)(2,1)}), bf16[32,72,256]{2,1,0:T(8,128)(2,1)S(1)}, u32[]{:S(2)}, u32[]{:S(2)}) %all-to-all-start.1) | async-done | bytes 1179680 | tf_op jit(solution)/shard_map/all_to_all | solution.py:366
  88.7 4.5 %collective-permute-start.6 = (bf16[2304,256]{1,0:T(8,128)(2,1)S(1)}, bf16[2304,256]{1,0:T(8,128)(2,1)S(1)}, u32[]{:S(2)}, u32[]{:S(2)}) collective-permute-start(bf16[2304,256]{1,0:T(8,128)(2,1)S(1)} %bitcast.14), channel_id=1, source_target_pairs={{0,1},{1,0},{2,3},{3,2},{4,5},{5,4},{6,7},{7,6},{8,9},{9,8},{10,11... | collective-permute-start | bytes 3538952 | tf_op jit(solution)/shard_map/ppermute | solution.py:274
  93.1 2.0 %mine.1 = (f32[2304,256]{1,0:T(8,128)}, f32[2304,256]{1,0:T(8,128)}) custom-call(s32[2]{0:T(128)S(1)} %pad_add_fusion.ids, bf16[2304,256]{1,0:T(8,128)(2,1)S(1)} %bitcast.15), custom_call_target="tpu_custom_call" | custom-call | flops 1000000000 | bytes 1179656 | tf_op jit(solution)/shard_map/mine/pallas_call | solution.py:32
  95.2 0.4 collective-permute-done.6.other
  95.6 2.0 %other.1 = (f32[2304,256]{1,0:T(8,128)}, f32[2304,256]{1,0:T(8,128)}) custom-call(s32[2]{0:T(128)S(1)} %pad_add_fusion.ids, bf16[2304,256]{1,0:T(8,128)(2,1)S(1)} %collective-permute-done.6.other, f32[2304,256]{1,0:T(8,128)} %get-tuple-element.49.g1_in, f32[2304,256]{1,0:T(8,128)} %get-tuple-element.50.g2_in), custom_call_target="tpu_custom_call", output_to_operand_aliasing={{0}: (2, {}), {1}: (3, {})} | custom-call | bytes 5898248 | tf_op jit(solution)/shard_map/other/pallas_call | solution.py:32
  (37 shorter events, 1.3 us)
Async XLA Ops:
  0.7 1.1 %copy-start = (bf16[1,16,96,256]{3,2,1,0:T(8,128)(2,1)S(1)}, bf16[1,16,96,256]{3,2,1,0:T(8,128)(2,1)}, u32[]{:S(2)}) copy-start(bf16[1,16,96,256]{3,2,1,0:T(8,128)(2,1)} %param.6) | copy-start | bytes 2359300
  1.8 0.7 copy-start.1
  2.6 11.5 %collective-permute-start = (bf16[400,256]{1,0:T(8,128)(2,1)S(1)}, bf16[400,256]{1,0:T(8,128)(2,1)S(1)}, u32[]{:S(2)}, u32[]{:S(2)}) collective-permute-start(bf16[400,256]{1,0:T(8,128)(2,1)S(1)} %get-tuple-element.34), channel_id=1, source_target_pairs={{0,64},{64,128},{128,192},{192,8},{8,72},{72,136},{136,200},{200,0... | collective-permute-start | bytes 614408 | tf_op jit(solution)/shard_map/ppermute | solution.py:306
  5.2 9.0 %collective-permute-start.1 = (bf16[400,256]{1,0:T(8,128)(2,1)S(1)}, bf16[400,256]{1,0:T(8,128)(2,1)S(1)}, u32[]{:S(2)}, u32[]{:S(2)}) collective-permute-start(bf16[400,256]{1,0:T(8,128)(2,1)S(1)} %get-tuple-element.35), channel_id=1, source_target_pairs={{0,200},{64,0},{128,64},{192,128},{8,192},{72,8},{136,72},{200,136... | collective-permute-start | bytes 614408 | tf_op jit(solution)/shard_map/ppermute | solution.py:307
  9.2 1.3 %copy-start.2 = (bf16[3,3,256,256]{3,2,1,0:T(8,128)(2,1)S(1)}, bf16[3,3,256,256]{3,2,1,0:T(8,128)(2,1)}, u32[]{:S(2)}) copy-start(bf16[3,3,256,256]{3,2,1,0:T(8,128)(2,1)} %param.8) | copy-start | bytes 3538948
  10.5 1.3 %copy-start.4 = (bf16[3,3,256,256]{3,2,1,0:T(8,128)(2,1)S(1)}, bf16[3,3,256,256]{3,2,1,0:T(8,128)(2,1)}, u32[]{:S(2)}) copy-start(bf16[3,3,256,256]{3,2,1,0:T(8,128)(2,1)} %param.7) | copy-start | bytes 3538948
  11.7 2.4 %copy-start.3 = (bf16[3,3,256,256]{3,2,1,0:T(8,128)(2,1)S(1)}, bf16[3,3,256,256]{3,2,1,0:T(8,128)(2,1)}, u32[]{:S(2)}) copy-start(bf16[3,3,256,256]{3,2,1,0:T(8,128)(2,1)} %param.8) | copy-start | bytes 3538948
  11.7 2.5 %copy-start.5 = (bf16[3,3,256,256]{3,2,1,0:T(8,128)(2,1)S(1)}, bf16[3,3,256,256]{3,2,1,0:T(8,128)(2,1)}, u32[]{:S(2)}) copy-start(bf16[3,3,256,256]{3,2,1,0:T(8,128)(2,1)} %param.7) | copy-start | bytes 3538948
  11.8 2.5 %copy-start.6 = (bf16[256,3]{0,1:T(4,128)(2,1)S(1)}, bf16[256,3]{0,1:T(4,128)(2,1)}, u32[]{:S(2)}) copy-start(bf16[256,3]{0,1:T(4,128)(2,1)} %param.9) | copy-start | bytes 4612
  11.8 2.5 %copy-start.7 = (f32[3]{0:T(128)S(1)}, f32[3]{0:T(128)}, u32[]{:S(2)}) copy-start(f32[3]{0:T(128)} %bias.1) | copy-start | bytes 40
  26.9 3.5 %collective-permute-start.2 = (bf16[2320,256]{1,0:T(8,128)(2,1)S(1)}, bf16[2320,256]{1,0:T(8,128)(2,1)S(1)}, u32[]{:S(2)}, u32[]{:S(2)}) collective-permute-start(bf16[2320,256]{1,0:T(8,128)(2,1)S(1)} %pad_maximum_fusion.1), channel_id=1, source_target_pairs={{0,1},{1,0},{2,3},{3,2},{4,5},{5,4},{6,7},{7,6},{8,9},{9,8},{10,11... | collective-permute-start | bytes 3563528 | tf_op jit(solution)/shard_map/ppermute | solution.py:274
  57.3 7.7 %collective-permute-start.5 = (bf16[80,256]{1,0:T(8,128)(2,1)S(1)}, bf16[80,256]{1,0:T(8,128)(2,1)S(1)}, u32[]{:S(2)}, u32[]{:S(2)}) collective-permute-start(bf16[80,256]{1,0:T(8,128)(2,1)S(1)} %pad_maximum_fusion.2), channel_id=1, source_target_pairs={{0,136},{64,200},{128,0},{192,64},{8,128},{72,192},{136,8},{200,72... | collective-permute-start | bytes 122888 | tf_op jit(solution)/shard_map/ppermute | solution.py:353
  61.1 5.0 %collective-permute-start.4 = (bf16[80,256]{1,0:T(8,128)(2,1)S(1)}, bf16[80,256]{1,0:T(8,128)(2,1)S(1)}, u32[]{:S(2)}, u32[]{:S(2)}) collective-permute-start(bf16[80,256]{1,0:T(8,128)(2,1)S(1)} %pad_maximum_fusion.2), channel_id=1, source_target_pairs={{0,128},{64,192},{128,8},{192,72},{8,136},{72,200},{136,0},{200,64... | collective-permute-start | bytes 122888 | tf_op jit(solution)/shard_map/ppermute | solution.py:353
  61.8 6.9 %collective-permute-start.3 = (bf16[80,256]{1,0:T(8,128)(2,1)S(1)}, bf16[80,256]{1,0:T(8,128)(2,1)S(1)}, u32[]{:S(2)}, u32[]{:S(2)}) collective-permute-start(bf16[80,256]{1,0:T(8,128)(2,1)S(1)} %pad_maximum_fusion.2), channel_id=1, source_target_pairs={{0,8},{64,72},{128,136},{192,200},{8,0},{72,64},{136,128},{200,192... | collective-permute-start | bytes 122888 | tf_op jit(solution)/shard_map/ppermute | solution.py:353
  69.8 18.9 %all-to-all-start.1 = ((bf16[32,72,256]{2,1,0:T(8,128)(2,1)}), bf16[32,72,256]{2,1,0:T(8,128)(2,1)S(1)}, u32[]{:S(2)}, u32[]{:S(2)}) async-start(bf16[32,72,256]{2,1,0:T(8,128)(2,1)} %broadcast_in_dim.7), calls=%async_computation.1 | async-start | bytes 2359296 | tf_op jit(solution)/shard_map/all_to_all | solution.py:366
  88.7 7.0 %collective-permute-start.6 = (bf16[2304,256]{1,0:T(8,128)(2,1)S(1)}, bf16[2304,256]{1,0:T(8,128)(2,1)S(1)}, u32[]{:S(2)}, u32[]{:S(2)}) collective-permute-start(bf16[2304,256]{1,0:T(8,128)(2,1)S(1)} %bitcast.14), channel_id=1, source_target_pairs={{0,1},{1,0},{2,3},{3,2},{4,5},{5,4},{6,7},{7,6},{8,9},{9,8},{10,11... | collective-permute-start | bytes 3538952 | tf_op jit(solution)/shard_map/ppermute | solution.py:274

commit v7 on v6

--- a/solution.py
+++ b/solution.py
@@ -17,7 +17,6 @@
 BF16 = jnp.bfloat16
 ROWWISE = (((0,), (0,)), ((), ()))
 VMEM = pl.BlockSpec(memory_space=pltpu.VMEM)
-SMEM = pl.BlockSpec(memory_space=pltpu.SMEM)
 HBM = pl.BlockSpec(memory_space=pltpu.HBM)
 AXES = ("q", "p", "x", "h", "y", "c")
 BAND = ("q", "p")
@@ -115,9 +114,9 @@
 
 
 def make_main(height, scale):
-    def main(ids, bias, above, below, fwi, awi, slopei, k1, k2, k2t, classes, lab, g1, g2, small, fg,
+    def main(bias, above, below, fwi, awi, slopei, k1, k2, k2t, classes, lab, g1, g2, small, fg,
              fw, aw, sw, fgw, gt, slope, labs, held, cls32, cls):
-        base = ids[0] * ROWS
+        base = (lax.axis_index("q") * 2 + lax.axis_index("p")) * ROWS
         cls32[...] = jnp.zeros_like(cls32)
         cls32[0:3, :] = classes[...].astype(F32)
         cls32[3:6, :] = classes[...].astype(F32)
@@ -166,7 +165,7 @@
             logit = lax.dot_general(
                 cls[...], act, (((1,), (1,)), ((), ())), preferred_element_type=F32
             )
-            rows = [logit[k:k + 1, :] + bias[k] for k in range(3)]
+            rows = [logit[k:k + 1, :] + bias[0:1, k:k + 1] for k in range(3)]
             top = jnp.maximum(jnp.maximum(rows[0], rows[1]), rows[2])
             ex = [jnp.exp(row - top) for row in rows]
             den = ex[0] + ex[1] + ex[2]
@@ -249,18 +248,20 @@
         copy.wait()
 
 
-def mine_kernel(ids, mine, g1, g2, wide, sems):
-    @pl.when(ids[1] == 0)
+def mine_kernel(mine, g1, g2, wide, sems):
+    core = lax.axis_index("c")
+
+    @pl.when(core == 0)
     def _():
         convert_out(mine, wide, g1, sems)
 
-    @pl.when(ids[1] == 1)
+    @pl.when(core == 1)
     def _():
         convert_out(mine, wide, g2, sems)
 
 
-def other_kernel(ids, other, g1_in, g2_in, g1, g2, wide, sems):
-    mine_kernel(ids, other, g2, g1, wide, sems)
+def other_kernel(other, g1_in, g2_in, g1, g2, wide, sems):
+    mine_kernel(other, g2, g1, wide, sems)
 
 
 def ring(step):
@@ -288,9 +289,7 @@
     height = ROWS * lax.axis_size(BAND)
     count = height * COLS * lax.axis_size(RAIL)
     scale = float(count) ** (-0.5)
-    band = lax.axis_index(BAND)
     core = lax.axis_index("c")
-    ids = jnp.stack([band, core])
 
     flat = features.reshape(PIX, CH)
     lab = labels.reshape(ROWS, COLS)
@@ -302,7 +301,7 @@
         (flat, lab), [VMEM] * 2, [pltpu.VMEM((16, CH), F32)], limit=8, name="edge",
     )
     first = core == 0
-    up, down, ids, first = lax.optimization_barrier((up, down, ids, first))
+    up, down, first = lax.optimization_barrier((up, down, first))
     above = lax.ppermute(down, DEPTH, ring(1))
     below = lax.ppermute(up, DEPTH, ring(7))
 
@@ -317,8 +316,8 @@
     g1, g2, small, fg = call(
         make_main(height, scale),
         [((9 * CH, CH), BF16), ((9 * CH, CH), BF16), ((8, CH), F32), ((18 * COLS, CH), BF16)],
-        (ids, class_bias, above, below, fwi, awi, slopei, k1, k2, k2t, classifier.T, labels),
-        [SMEM] * 2 + [VMEM] * 10,
+        (class_bias.reshape(1, 3), above, below, fwi, awi, slopei, k1, k2, k2t, classifier.T, labels),
+        [VMEM] * 11,
         [
             pltpu.VMEM((24 * COLS, 3 * CH), BF16),
             pltpu.VMEM((22 * COLS, 3 * CH), BF16),
@@ -370,12 +369,12 @@
     outs = [((9 * CH, CH), F32)] * 2
     scratch = [pltpu.VMEM((9 * CH, CH), F32), pltpu.SemaphoreType.DMA((6,))]
     halves = call(
-        mine_kernel, outs, (ids, mine), [SMEM, VMEM], scratch,
+        mine_kernel, outs, (mine,), [VMEM], scratch,
         limit=8, flops=1_000_000_000, name="mine", out_specs=(HBM, HBM),
     )
     grad_first, grad_second = call(
-        other_kernel, outs, (ids, other, *halves), [SMEM, VMEM, HBM, HBM], scratch,
-        limit=8, name="other", out_specs=(HBM, HBM), aliases={2: 0, 3: 1},
+        other_kernel, outs, (other, *halves), [VMEM, HBM, HBM], scratch,
+        limit=8, name="other", out_specs=(HBM, HBM), aliases={1: 0, 2: 1},
     )
     shape = (3, 3, CH, CH)
     return (

time: 98.2 us -> 97 us (0.988)
  Pallas kernels: 22.8 us -> 21.1 us
    pallas_call x6, Pallas kernels: 22.8 us -> 21.1 us  [call(): pl.pallas_call(kernel, out_shape=shapes, in_specs=list(ins), input_output...]
where the time goes in v7:
time: 97 us; the launch traced here: 96.6 us
  blocking collectives  25.9 us (27%)
  starting transfers between devices  24.4 us (25%)
  Pallas kernels  21.1 us (22%)
  waiting for transfers between devices  17.6 us (18%)
  local copies, waits for them, and re-layouts  5.48 us (6%)
  other arithmetic  1.15 us (1%)
  between operations  1 us (1%)
    all_to_all x1, blocking collectives, per_device(): spread = lax.all_to_all(spread, PLANE, 0, 0, tiled=True)  25.9 us
    pallas_call x6, Pallas kernels, call(): pl.pallas_call(kernel, out_shape=shapes, in_specs=list(ins), input_output...  21.1 us
    all_to_all x1, waiting for transfers between devices, per_device(): lax.all_to_all(jnp.broadcast_to(piece, (32, part, CH)), PLANE, 0, 0, tile...  10.5 us
    ppermute x3, starting transfers between devices, per_device(): one, two, three = [lax.ppermute(send, DEPTH, ring(k)) for k in (2, 4, 6)]  7.63 us
    ppermute x2, starting transfers between devices, shift(): lax.ppermute(value, axis, [(i, (i + step) % size) for i in range(size)])  5.64 us
    all_to_all x1, starting transfers between devices, per_device(): lax.all_to_all(jnp.broadcast_to(piece, (32, part, CH)), PLANE, 0, 0, tile...  4.54 us
    unnamed x16, local copies, waits for them, and re-layouts  4.38 us
    ppermute x1, starting transfers between devices, per_device(): below = lax.ppermute(up, DEPTH, ring(7))  4.03 us
  transfers between devices with their start and end apart: 8, of which 5 were waited for; matrix products, arithmetic and copies ran while one was open for 0% of the time, Pallas kernels for 8%

profile of v7, /device:TPU:1, one launch (start us, length us, event | category | flops | bytes accessed | tf_op | source)
XLA Modules:
  0.0 96.6 jit_solution(6594724121812032690)
XLA Ops:
  0.6 1.1 %copy-done = bf16[1,16,96,256]{3,2,1,0:T(8,128)(2,1)S(1)} copy-done((bf16[1,16,96,256]{3,2,1,0:T(8,128)(2,1)S(1)}, bf16[1,16,96,256]{3,2,1,0:T(8,128)(2,1)}, u32[]{:S(2)}) %copy-start) | copy-done | bytes 786456
  1.8 0.7 copy-done.1
  2.6 2.5 %collective-permute-start = (bf16[400,256]{1,0:T(8,128)(2,1)S(1)}, bf16[400,256]{1,0:T(8,128)(2,1)S(1)}, u32[]{:S(2)}, u32[]{:S(2)}) collective-permute-start(bf16[400,256]{1,0:T(8,128)(2,1)S(1)} %get-tuple-element.32), channel_id=1, source_target_pairs={{0,64},{64,128},{128,192},{192,8},{8,72},{72,136},{136,200},{200,0... | collective-permute-start | bytes 614408 | tf_op jit(solution)/shard_map/ppermute | solution.py:305
  5.1 4.0 %collective-permute-start.1 = (bf16[400,256]{1,0:T(8,128)(2,1)S(1)}, bf16[400,256]{1,0:T(8,128)(2,1)S(1)}, u32[]{:S(2)}, u32[]{:S(2)}) collective-permute-start(bf16[400,256]{1,0:T(8,128)(2,1)S(1)} %get-tuple-element.33), channel_id=1, source_target_pairs={{0,200},{64,0},{128,64},{192,128},{8,192},{72,8},{136,72},{200,136... | collective-permute-start | bytes 614408 | tf_op jit(solution)/shard_map/ppermute | solution.py:306
  9.1 1.3 %copy-done.2 = bf16[3,3,256,256]{3,2,1,0:T(8,128)(2,1)S(1)} copy-done((bf16[3,3,256,256]{3,2,1,0:T(8,128)(2,1)S(1)}, bf16[3,3,256,256]{3,2,1,0:T(8,128)(2,1)}, u32[]{:S(2)}) %copy-start.2) | copy-done | bytes 1179672
  10.4 1.3 %copy-done.4 = bf16[3,3,256,256]{3,2,1,0:T(8,128)(2,1)S(1)} copy-done((bf16[3,3,256,256]{3,2,1,0:T(8,128)(2,1)S(1)}, bf16[3,3,256,256]{3,2,1,0:T(8,128)(2,1)}, u32[]{:S(2)}) %copy-start.4) | copy-done | bytes 1179672
  11.7 2.4 %inner.1 = (bf16[1536,768]{1,0:T(8,128)(2,1)S(1)}, bf16[1344,768]{1,0:T(8,128)(2,1)S(1)}, f32[1344,256]{1,0:T(8,128)S(1)}, bf16[2304,256]{1,0:T(8,128)(2,1)S(1)}) custom-call(bf16[1536,256]{1,0:T(8,128)(2,1)S(1)} %get-tuple-element.34.f, bf16[2304,256]{1,0:T(8,128)(2,1)S(1)} %bitcast.19, bf16[2304,256]{1,0:T(8,128)(2,1)S(1)} %bitcast.17), custom_call_target="tpu_custom_call" | custom-call | flops 5000000000 | bytes 3145728 | tf_op jit(solution)/shard_map/inner/pallas_call | solution.py:31
  14.2 11.8 %main.1 = (bf16[2304,256]{1,0:T(8,128)(2,1)S(1)}, bf16[2304,256]{1,0:T(8,128)(2,1)S(1)}, f32[8,256]{1,0:T(8,128)S(1)}, bf16[1728,256]{1,0:T(8,128)(2,1)S(1)}) custom-call(f32[1,3]{1,0:T(1,128)S(1)} %bitcast.23, bf16[400,256]{1,0:T(8,128)(2,1)S(1)} %collective-permute-done.above, bf16[400,256]{1,0:T(8,128)(2,1)S(1)} %collective-permute-done.1.below, ...), custom_call_target="tpu_custom_call" | custom-call | flops 8999999488 | bytes 9756172 | tf_op jit(solution)/shard_map/main/pallas_call | solution.py:31
  26.2 1.2 %collective-permute-start.2 = (bf16[2320,256]{1,0:T(8,128)(2,1)S(1)}, bf16[2320,256]{1,0:T(8,128)(2,1)S(1)}, u32[]{:S(2)}, u32[]{:S(2)}) collective-permute-start(bf16[2320,256]{1,0:T(8,128)(2,1)S(1)} %pad_maximum_fusion.1), channel_id=1, source_target_pairs={{0,1},{1,0},{2,3},{3,2},{4,5},{5,4},{6,7},{7,6},{8,9},{9,8},{10,11... | collective-permute-start | bytes 3563528 | tf_op jit(solution)/shard_map/ppermute | solution.py:275
  27.4 2.5 %collective-permute-done.2 = bf16[2320,256]{1,0:T(8,128)(2,1)S(1)} collective-permute-done((bf16[2320,256]{1,0:T(8,128)(2,1)S(1)}, bf16[2320,256]{1,0:T(8,128)(2,1)S(1)}, u32[]{:S(2)}, u32[]{:S(2)}) %collective-permute-start.2) | collective-permute-done | bytes 1187872 | tf_op jit(solution)/shard_map/ppermute | solution.py:275
  30.6 25.9 %all_to_all.10 = bf16[32,80,256]{2,1,0:T(8,128)(2,1)S(1)} all-to-all(bf16[32,80,256]{2,1,0:T(8,128)(2,1)S(1)} %pad_maximum_fusion), channel_id=1, replica_groups=mesh['q'=2,'p'=2,'x'=4,'h'=2,'y'=4,'c'=2] {'p','x','y'}, dimensions={0} | all-to-all | bytes 2621440 | tf_op jit(solution)/shard_map/all_to_all | solution.py:347
  56.8 3.7 %collective-permute-start.5 = (bf16[80,256]{1,0:T(8,128)(2,1)S(1)}, bf16[80,256]{1,0:T(8,128)(2,1)S(1)}, u32[]{:S(2)}, u32[]{:S(2)}) collective-permute-start(bf16[80,256]{1,0:T(8,128)(2,1)S(1)} %pad_maximum_fusion.2), channel_id=1, source_target_pairs={{0,136},{64,200},{128,0},{192,64},{8,128},{72,192},{136,8},{200,72... | collective-permute-start | bytes 122888 | tf_op jit(solution)/shard_map/ppermute | solution.py:352
  60.5 0.7 collective-permute-start.4
  61.2 3.2 %collective-permute-start.3 = (bf16[80,256]{1,0:T(8,128)(2,1)S(1)}, bf16[80,256]{1,0:T(8,128)(2,1)S(1)}, u32[]{:S(2)}, u32[]{:S(2)}) collective-permute-start(bf16[80,256]{1,0:T(8,128)(2,1)S(1)} %pad_maximum_fusion.2), channel_id=1, source_target_pairs={{0,8},{64,72},{128,136},{192,200},{8,0},{72,64},{136,128},{200,192... | collective-permute-start | bytes 122888 | tf_op jit(solution)/shard_map/ppermute | solution.py:352
  64.4 1.1 %collective-permute-done.4 = bf16[80,256]{1,0:T(8,128)(2,1)S(1)} collective-permute-done((bf16[80,256]{1,0:T(8,128)(2,1)S(1)}, bf16[80,256]{1,0:T(8,128)(2,1)S(1)}, u32[]{:S(2)}, u32[]{:S(2)}) %collective-permute-start.4) | collective-permute-done | bytes 40992 | tf_op jit(solution)/shard_map/ppermute | solution.py:352
  65.5 2.6 %collective-permute-done.3 = bf16[80,256]{1,0:T(8,128)(2,1)S(1)} collective-permute-done((bf16[80,256]{1,0:T(8,128)(2,1)S(1)}, bf16[80,256]{1,0:T(8,128)(2,1)S(1)}, u32[]{:S(2)}, u32[]{:S(2)}) %collective-permute-start.3) | collective-permute-done | bytes 40992 | tf_op jit(solution)/shard_map/ppermute | solution.py:352
  68.1 1.1 %broadcast_in_dim.7 = bf16[32,72,256]{2,1,0:T(8,128)(2,1)} broadcast(bf16[72,256]{1,0:T(8,128)(2,1)S(1)} %add_convert_fusion.1), dimensions={1,2} | broadcast | bytes 1216512 | tf_op jit(solution)/shard_map/broadcast_in_dim | solution.py:365
  69.2 4.5 %all-to-all-start.1 = ((bf16[32,72,256]{2,1,0:T(8,128)(2,1)}), bf16[32,72,256]{2,1,0:T(8,128)(2,1)S(1)}, u32[]{:S(2)}, u32[]{:S(2)}) async-start(bf16[32,72,256]{2,1,0:T(8,128)(2,1)} %broadcast_in_dim.7), calls=%async_computation.1 | async-start | bytes 2359296 | tf_op jit(solution)/shard_map/all_to_all | solution.py:365
  73.8 3.8 %feature.1 = (bf16[1536,256]{1,0:T(8,128)(2,1)}, f32[3,256]{1,0:T(4,128)}, f32[1,3]{1,0:T(1,128)}) custom-call(bf16[1728,256]{1,0:T(8,128)(2,1)S(1)} %get-tuple-element.43.fg, bf16[2304,256]{1,0:T(8,128)(2,1)S(1)} %bitcast.21, f32[4,256]{1,0:T(4,128)S(1)} %fusion.5.sums), custom_call_target="tpu_custom_call" | custom-call | flops 2500000000 | bytes 2068480 | tf_op jit(solution)/shard_map/feature/pallas_call | solution.py:31
  77.6 10.5 %all-to-all-done.1 = bf16[32,72,256]{2,1,0:T(8,128)(2,1)S(1)} async-done(((bf16[32,72,256]{2,1,0:T(8,128)(2,1)}), bf16[32,72,256]{2,1,0:T(8,128)(2,1)S(1)}, u32[]{:S(2)}, u32[]{:S(2)}) %all-to-all-start.1) | async-done | bytes 1179680 | tf_op jit(solution)/shard_map/all_to_all | solution.py:365
  88.1 4.4 %collective-permute-start.6 = (bf16[2304,256]{1,0:T(8,128)(2,1)S(1)}, bf16[2304,256]{1,0:T(8,128)(2,1)S(1)}, u32[]{:S(2)}, u32[]{:S(2)}) collective-permute-start(bf16[2304,256]{1,0:T(8,128)(2,1)S(1)} %bitcast.13), channel_id=1, source_target_pairs={{0,1},{1,0},{2,3},{3,2},{4,5},{5,4},{6,7},{7,6},{8,9},{9,8},{10,11... | collective-permute-start | bytes 3538952 | tf_op jit(solution)/shard_map/ppermute | solution.py:275
  92.5 1.5 %mine.1 = (f32[2304,256]{1,0:T(8,128)}, f32[2304,256]{1,0:T(8,128)}) custom-call(bf16[2304,256]{1,0:T(8,128)(2,1)S(1)} %bitcast.14), custom_call_target="tpu_custom_call" | custom-call | flops 1000000000 | bytes 1179648 | tf_op jit(solution)/shard_map/mine/pallas_call | solution.py:31
  94.0 1.0 %collective-permute-done.6.other = bf16[2304,256]{1,0:T(8,128)(2,1)S(1)} collective-permute-done((bf16[2304,256]{1,0:T(8,128)(2,1)S(1)}, bf16[2304,256]{1,0:T(8,128)(2,1)S(1)}, u32[]{:S(2)}, u32[]{:S(2)}) %collective-permute-start.6) | collective-permute-done | bytes 1179680 | tf_op jit(solution)/shard_map/ppermute | solution.py:275
  95.0 1.5 %other.1 = (f32[2304,256]{1,0:T(8,128)}, f32[2304,256]{1,0:T(8,128)}) custom-call(bf16[2304,256]{1,0:T(8,128)(2,1)S(1)} %collective-permute-done.6.other, f32[2304,256]{1,0:T(8,128)} %get-tuple-element.47.g1_in, f32[2304,256]{1,0:T(8,128)} %get-tuple-element.48.g2_in), custom_call_target="tpu_custom_call", output_to_operand_aliasing={{0}: (1, {}), {1}: (2, {})} | custom-call | bytes 5898240 | tf_op jit(solution)/shard_map/other/pallas_call | solution.py:31
  (36 shorter events, 1.3 us)
Async XLA Ops:
  0.6 1.1 %copy-start = (bf16[1,16,96,256]{3,2,1,0:T(8,128)(2,1)S(1)}, bf16[1,16,96,256]{3,2,1,0:T(8,128)(2,1)}, u32[]{:S(2)}) copy-start(bf16[1,16,96,256]{3,2,1,0:T(8,128)(2,1)} %param.6) | copy-start | bytes 2359300
  1.8 0.7 copy-start.1
  2.6 11.5 %collective-permute-start = (bf16[400,256]{1,0:T(8,128)(2,1)S(1)}, bf16[400,256]{1,0:T(8,128)(2,1)S(1)}, u32[]{:S(2)}, u32[]{:S(2)}) collective-permute-start(bf16[400,256]{1,0:T(8,128)(2,1)S(1)} %get-tuple-element.32), channel_id=1, source_target_pairs={{0,64},{64,128},{128,192},{192,8},{8,72},{72,136},{136,200},{200,0... | collective-permute-start | bytes 614408 | tf_op jit(solution)/shard_map/ppermute | solution.py:305
  5.1 9.0 %collective-permute-start.1 = (bf16[400,256]{1,0:T(8,128)(2,1)S(1)}, bf16[400,256]{1,0:T(8,128)(2,1)S(1)}, u32[]{:S(2)}, u32[]{:S(2)}) collective-permute-start(bf16[400,256]{1,0:T(8,128)(2,1)S(1)} %get-tuple-element.33), channel_id=1, source_target_pairs={{0,200},{64,0},{128,64},{192,128},{8,192},{72,8},{136,72},{200,136... | collective-permute-start | bytes 614408 | tf_op jit(solution)/shard_map/ppermute | solution.py:306
  9.1 1.3 %copy-start.2 = (bf16[3,3,256,256]{3,2,1,0:T(8,128)(2,1)S(1)}, bf16[3,3,256,256]{3,2,1,0:T(8,128)(2,1)}, u32[]{:S(2)}) copy-start(bf16[3,3,256,256]{3,2,1,0:T(8,128)(2,1)} %param.8) | copy-start | bytes 3538948
  10.4 1.3 %copy-start.4 = (bf16[3,3,256,256]{3,2,1,0:T(8,128)(2,1)S(1)}, bf16[3,3,256,256]{3,2,1,0:T(8,128)(2,1)}, u32[]{:S(2)}) copy-start(bf16[3,3,256,256]{3,2,1,0:T(8,128)(2,1)} %param.7) | copy-start | bytes 3538948
  11.7 2.5 %copy-start.3 = (bf16[3,3,256,256]{3,2,1,0:T(8,128)(2,1)S(1)}, bf16[3,3,256,256]{3,2,1,0:T(8,128)(2,1)}, u32[]{:S(2)}) copy-start(bf16[3,3,256,256]{3,2,1,0:T(8,128)(2,1)} %param.8) | copy-start | bytes 3538948
  11.7 2.5 %copy-start.5 = (bf16[3,3,256,256]{3,2,1,0:T(8,128)(2,1)S(1)}, bf16[3,3,256,256]{3,2,1,0:T(8,128)(2,1)}, u32[]{:S(2)}) copy-start(bf16[3,3,256,256]{3,2,1,0:T(8,128)(2,1)} %param.7) | copy-start | bytes 3538948
  11.7 2.5 %copy-start.6 = (bf16[256,3]{0,1:T(4,128)(2,1)S(1)}, bf16[256,3]{0,1:T(4,128)(2,1)}, u32[]{:S(2)}) copy-start(bf16[256,3]{0,1:T(4,128)(2,1)} %param.9) | copy-start | bytes 4612
  11.7 2.5 %copy-start.7 = (f32[3]{0:T(128)S(1)}, f32[3]{0:T(128)}, u32[]{:S(2)}) copy-start(f32[3]{0:T(128)} %param.10) | copy-start | bytes 40
  26.2 3.7 %collective-permute-start.2 = (bf16[2320,256]{1,0:T(8,128)(2,1)S(1)}, bf16[2320,256]{1,0:T(8,128)(2,1)S(1)}, u32[]{:S(2)}, u32[]{:S(2)}) collective-permute-start(bf16[2320,256]{1,0:T(8,128)(2,1)S(1)} %pad_maximum_fusion.1), channel_id=1, source_target_pairs={{0,1},{1,0},{2,3},{3,2},{4,5},{5,4},{6,7},{7,6},{8,9},{9,8},{10,11... | collective-permute-start | bytes 3563528 | tf_op jit(solution)/shard_map/ppermute | solution.py:275
  56.8 7.6 %collective-permute-start.5 = (bf16[80,256]{1,0:T(8,128)(2,1)S(1)}, bf16[80,256]{1,0:T(8,128)(2,1)S(1)}, u32[]{:S(2)}, u32[]{:S(2)}) collective-permute-start(bf16[80,256]{1,0:T(8,128)(2,1)S(1)} %pad_maximum_fusion.2), channel_id=1, source_target_pairs={{0,136},{64,200},{128,0},{192,64},{8,128},{72,192},{136,8},{200,72... | collective-permute-start | bytes 122888 | tf_op jit(solution)/shard_map/ppermute | solution.py:352
  60.5 5.0 %collective-permute-start.4 = (bf16[80,256]{1,0:T(8,128)(2,1)S(1)}, bf16[80,256]{1,0:T(8,128)(2,1)S(1)}, u32[]{:S(2)}, u32[]{:S(2)}) collective-permute-start(bf16[80,256]{1,0:T(8,128)(2,1)S(1)} %pad_maximum_fusion.2), channel_id=1, source_target_pairs={{0,128},{64,192},{128,8},{192,72},{8,136},{72,200},{136,0},{200,64... | collective-permute-start | bytes 122888 | tf_op jit(solution)/shard_map/ppermute | solution.py:352
  61.2 6.9 %collective-permute-start.3 = (bf16[80,256]{1,0:T(8,128)(2,1)S(1)}, bf16[80,256]{1,0:T(8,128)(2,1)S(1)}, u32[]{:S(2)}, u32[]{:S(2)}) collective-permute-start(bf16[80,256]{1,0:T(8,128)(2,1)S(1)} %pad_maximum_fusion.2), channel_id=1, source_target_pairs={{0,8},{64,72},{128,136},{192,200},{8,0},{72,64},{136,128},{200,192... | collective-permute-start | bytes 122888 | tf_op jit(solution)/shard_map/ppermute | solution.py:352
  69.2 18.9 %all-to-all-start.1 = ((bf16[32,72,256]{2,1,0:T(8,128)(2,1)}), bf16[32,72,256]{2,1,0:T(8,128)(2,1)S(1)}, u32[]{:S(2)}, u32[]{:S(2)}) async-start(bf16[32,72,256]{2,1,0:T(8,128)(2,1)} %broadcast_in_dim.7), calls=%async_computation.1 | async-start | bytes 2359296 | tf_op jit(solution)/shard_map/all_to_all | solution.py:365
  88.1 6.9 %collective-permute-start.6 = (bf16[2304,256]{1,0:T(8,128)(2,1)S(1)}, bf16[2304,256]{1,0:T(8,128)(2,1)S(1)}, u32[]{:S(2)}, u32[]{:S(2)}) collective-permute-start(bf16[2304,256]{1,0:T(8,128)(2,1)S(1)} %bitcast.13), channel_id=1, source_target_pairs={{0,1},{1,0},{2,3},{3,2},{4,5},{5,4},{6,7},{7,6},{8,9},{9,8},{10,11... | collective-permute-start | bytes 3538952 | tf_op jit(solution)/shard_map/ppermute | solution.py:275

commit v8 on v7

--- a/solution.py
+++ b/solution.py
@@ -12,6 +12,7 @@
 PIX = ROWS * COLS
 EDGE = HALO * COLS
 BLOCK = EDGE + 16
+HALF = 9 * CH // 2
 R2 = 10
 F32 = jnp.float32
 BF16 = jnp.bfloat16
@@ -81,14 +82,13 @@
     return jnp.stack(parts)
 
 
-def edge_kernel(f, lab, up, down, fv, labels, tag):
+def edge_kernel(f, lab, up, down, fv, tag):
     for out, row, label in ((up, 0, 0), (down, ROWS - HALO, ROWS - 2)):
         out[0:EDGE, :] = f[row * COLS:(row + HALO) * COLS, :]
         tag[...] = jnp.zeros_like(tag)
         tag[0:2, 0:COLS] = lab[label:label + 2, :].astype(F32)
         out[EDGE:BLOCK, :] = tag[...].astype(BF16)
     fv[...] = f[...]
-    labels[...] = lab[...]
 
 
 def flip(src, dst):
@@ -113,23 +113,38 @@
     flip(k2, k2t)
 
 
-def make_main(height, scale):
-    def main(bias, above, below, fwi, awi, slopei, k1, k2, k2t, classes, lab, g1, g2, small, fg,
-             fw, aw, sw, fgw, gt, slope, labs, held, cls32, cls):
-        base = (lax.axis_index("q") * 2 + lax.axis_index("p")) * ROWS
+def weight_grad(grad_wide, skip, src, src_skip, out, gt):
+    gt[...] = grad_wide[skip * COLS:(skip + ROWS) * COLS, CH:2 * CH].T
+    for a in range(3):
+        win = src[(src_skip + a) * COLS:(src_skip + a + ROWS) * COLS, :]
+        res = jnp.dot(gt[...], win, preferred_element_type=F32)
+        for b in range(3):
+            out[(3 * a + b) * CH:(3 * a + b + 1) * CH, :] = (
+                res[:, b * CH:(b + 1) * CH].T.astype(BF16)
+            )
+
+
+def band_start():
+    return (lax.axis_index("q") * 2 + lax.axis_index("p")) * ROWS
+
+
+def make_upper(height, scale):
+    def upper(bias, above, below, fwi, awi, k1, k2, classes, lab, g2, small, sw, slope,
+              fw, aw, gt, labs, held, cls32, cls):
+        base = band_start()
         cls32[...] = jnp.zeros_like(cls32)
         cls32[0:3, :] = classes[...].astype(F32)
         cls32[3:6, :] = classes[...].astype(F32)
         cls[...] = cls32[...].astype(BF16)
-        fw[EDGE:EDGE + PIX, :] = fwi[...]
+        fw[4 * COLS:6 * COLS, :] = fwi[0:2 * COLS, :]
+        fw[6 * COLS:8 * COLS, :] = fwi[14 * COLS:16 * COLS, :]
         for half in range(2):
             at = half * 2 * COLS
             rows = keep_rows(load_rows(above, at, 2), base - HALO + half * 2, height)
             store_wide(fw, at, rows)
             rows = keep_rows(load_rows(below, at, 2), base + ROWS + half * 2, height)
-            store_wide(fw, EDGE + PIX + at, rows)
+            store_wide(fw, 8 * COLS + at, rows)
         aw[4 * COLS:18 * COLS, :] = awi[...]
-        slope[4 * COLS:18 * COLS, :] = slopei[...]
 
         tags = [above[EDGE:BLOCK, :].astype(F32), below[EDGE:BLOCK, :].astype(F32)]
         mine = lab[...].astype(F32)
@@ -139,16 +154,13 @@
         for r, line in enumerate(lines):
             labs[r // R2, 0:1, (r % R2) * COLS:(r % R2 + 1) * COLS] = line
 
-        def first(t, c):
-            at = t * (18 * COLS)
-            v = conv_rows(fw, at, 4, k1)
+        for t in range(2):
+            v = conv_rows(fw, t * (6 * COLS), 4, k1)
             s = sigmoid(v)
-            rows = pl.ds(aligned(at), 4 * COLS)
-            slope[rows, :] = (s * (1.0 + v * (1.0 - s))).reshape(4 * COLS, CH)
-            store_wide(aw, at, keep_rows(v * s, base - 3 + t * 18, height))
-            return c
-
-        lax.fori_loop(0, 2, first, 0)
+            slope[t * 4 * COLS:(t + 1) * 4 * COLS, :] = (
+                s * (1.0 + v * (1.0 - s))
+            ).reshape(4 * COLS, CH)
+            store_wide(aw, t * (18 * COLS), keep_rows(v * s, base - 3 + t * 18, height))
 
         small[...] = jnp.zeros_like(small)
         lane = lax.broadcasted_iota(jnp.int32, (1, CH), 1)
@@ -193,28 +205,29 @@
             if t > 0:
                 second(t - 1)
 
-        def weight(grad_wide, skip, src, src_skip, out):
-            gt[...] = grad_wide[skip * COLS:(skip + ROWS) * COLS, CH:2 * CH].T
-            for a in range(3):
-                win = src[(src_skip + a) * COLS:(src_skip + a + ROWS) * COLS, :]
-                res = jnp.dot(gt[...], win, preferred_element_type=F32)
-                for b in range(3):
-                    out[(3 * a + b) * CH:(3 * a + b + 1) * CH, :] = (
-                        res[:, b * CH:(b + 1) * CH].T.astype(BF16)
-                    )
-
-        weight(sw, 2, aw, 2, g2)
-
+        weight_grad(sw, 2, aw, 2, g2, gt)
+
+    return upper
+
+
+def make_lower(height):
+    def lower(above, below, fwi, slopei, slope_ends, sw, k2t, g1, fg, fw, fgw, gt, slope):
+        base = band_start()
+        fw[COLS:17 * COLS, :] = fwi[...]
+        store_wide(fw, 0, keep_rows(load_rows(above, 3 * COLS, 1), base - 1, height))
+        store_wide(fw, 17 * COLS, keep_rows(load_rows(below, 0, 1), base + ROWS, height))
+        slope[0:2 * COLS, :] = slope_ends[2 * COLS:4 * COLS, :]
+        slope[2 * COLS:16 * COLS, :] = slopei[...]
+        slope[16 * COLS:18 * COLS, :] = slope_ends[4 * COLS:6 * COLS, :]
         for t in range(6):
             at = t * (3 * COLS)
             v = conv_rows(sw, at, 3, k2t)
-            sl = slope[pl.ds(at + 2 * COLS, 3 * COLS), :]
-            g = keep_rows(v * sl.reshape(3, COLS, CH), base - 1 + t * 3, height)
+            g = keep_rows(v * load_rows(slope, at, 3), base - 1 + t * 3, height)
             store_wide(fgw, at, g)
-        weight(fgw, 1, fw, 3, g1)
+        weight_grad(fgw, 1, fw, 0, g1, gt)
         fg[...] = fgw[:, CH:2 * CH]
 
-    return main
+    return lower
 
 
 def feature_kernel(fg, k1, sums, out, classes, bias, fgw, k1t):
@@ -237,31 +250,25 @@
     lax.fori_loop(0, 2, step, 0)
 
 
-def convert_out(block, wide, out, sems):
+def convert_out(block, owner, g1, g2, wide, sems):
     copies = []
     for t in range(6):
         at = pl.ds(t * 384, 384)
+        out = g1 if t < 3 else g2
+        row = pl.multiple_of(owner * HALF + (t % 3) * 384, 384)
         wide[at, :] = block[at, :].astype(F32)
-        copies.append(pltpu.make_async_copy(wide.at[at], out.at[at], sems.at[t]))
+        copies.append(pltpu.make_async_copy(wide.at[at], out.at[pl.ds(row, 384)], sems.at[t]))
         copies[-1].start()
     for copy in copies:
         copy.wait()
 
 
 def mine_kernel(mine, g1, g2, wide, sems):
-    core = lax.axis_index("c")
-
-    @pl.when(core == 0)
-    def _():
-        convert_out(mine, wide, g1, sems)
-
-    @pl.when(core == 1)
-    def _():
-        convert_out(mine, wide, g2, sems)
+    convert_out(mine, lax.axis_index("c"), g1, g2, wide, sems)
 
 
 def other_kernel(other, g1_in, g2_in, g1, g2, wide, sems):
-    mine_kernel(other, g2, g1, wide, sems)
+    convert_out(other, 1 - lax.axis_index("c"), g1, g2, wide, sems)
 
 
 def ring(step):
@@ -273,6 +280,11 @@
 
 def shift(value, axis, step, size):
     return lax.ppermute(value, axis, [(i, (i + step) % size) for i in range(size)])
+
+
+def halves(first, grad):
+    low, high = grad[:HALF], grad[HALF:]
+    return jnp.where(first, low, high), jnp.where(first, high, low)
 
 
 def split_small(small):
@@ -295,9 +307,9 @@
     lab = labels.reshape(ROWS, COLS)
     k1 = first_kernel.reshape(9 * CH, CH)
     k2 = second_kernel.reshape(9 * CH, CH)
-    up, down, fv, labels = call(
+    up, down, fv = call(
         edge_kernel,
-        [((BLOCK, CH), BF16), ((BLOCK, CH), BF16), ((PIX, CH), BF16), ((ROWS, COLS), jnp.int32)],
+        [((BLOCK, CH), BF16), ((BLOCK, CH), BF16), ((PIX, CH), BF16)],
         (flat, lab), [VMEM] * 2, [pltpu.VMEM((16, CH), F32)], limit=8, name="edge",
     )
     first = core == 0
@@ -313,32 +325,41 @@
         flops=5_000_000_000, limit=12, name="inner",
     )
 
-    g1, g2, small, fg = call(
-        make_main(height, scale),
-        [((9 * CH, CH), BF16), ((9 * CH, CH), BF16), ((8, CH), F32), ((18 * COLS, CH), BF16)],
-        (class_bias.reshape(1, 3), above, below, fwi, awi, slopei, k1, k2, k2t, classifier.T, labels),
-        [VMEM] * 11,
+    g2, small, sw, slope_ends = call(
+        make_upper(height, scale),
+        [((9 * CH, CH), BF16), ((8, CH), F32), ((20 * COLS, 3 * CH), BF16), ((8 * COLS, CH), F32)],
+        (class_bias.reshape(1, 3), above, below, fwi, awi, k1, k2, classifier.T, lab), [VMEM] * 9,
         [
-            pltpu.VMEM((24 * COLS, 3 * CH), BF16),
+            pltpu.VMEM((12 * COLS, 3 * CH), BF16),
             pltpu.VMEM((22 * COLS, 3 * CH), BF16),
-            pltpu.VMEM((20 * COLS, 3 * CH), BF16),
-            pltpu.VMEM((18 * COLS, 3 * CH), BF16),
             pltpu.VMEM((CH, PIX), BF16),
-            pltpu.VMEM((22 * COLS, CH), F32),
             pltpu.VMEM((20 // R2, 8, 1024), F32),
             pltpu.VMEM((2, R2 * COLS, CH), F32),
             pltpu.VMEM((16, CH), F32),
             pltpu.VMEM((16, CH), BF16),
         ],
-        limit=22, flops=9_000_000_000, name="main",
+        limit=18, flops=6_000_000_000, name="upper",
     )
     small = small[0:4]
-    keep = jnp.where(first, g1, g2)
-    give = jnp.where(first, g2, g1)
+    keep, give = halves(first, g2)
     tail = jnp.pad(split_small(small), ((0, 8), (0, 0)))
     got = shift(jnp.concatenate([give, tail], axis=0), "c", 1, 2)
-    total = (keep.astype(F32) + got[:9 * CH].astype(F32)).astype(BF16)
-    small = small + join_small(got[9 * CH:])
+    g1, fg = call(
+        make_lower(height), [((9 * CH, CH), BF16), ((18 * COLS, CH), BF16)],
+        (above, below, fwi, slopei, slope_ends, sw, k2t), [VMEM] * 7,
+        [
+            pltpu.VMEM((18 * COLS, 3 * CH), BF16),
+            pltpu.VMEM((18 * COLS, 3 * CH), BF16),
+            pltpu.VMEM((CH, PIX), BF16),
+            pltpu.VMEM((18 * COLS, CH), F32),
+        ],
+        limit=18, flops=4_000_000_000, name="lower",
+    )
+    total_second = (keep.astype(F32) + got[:HALF].astype(F32)).astype(BF16)
+    small = small + join_small(got[HALF:])
+    keep, give = halves(first, g1)
+    total_first = (keep.astype(F32) + shift(give, "c", 1, 2).astype(F32)).astype(BF16)
+    total = jnp.concatenate([total_first, total_second], axis=0)
 
     part = 9 * CH // 32
     spread = jnp.concatenate(
@@ -368,12 +389,12 @@
     other = shift(mine, "c", 1, 2)
     outs = [((9 * CH, CH), F32)] * 2
     scratch = [pltpu.VMEM((9 * CH, CH), F32), pltpu.SemaphoreType.DMA((6,))]
-    halves = call(
+    parts = call(
         mine_kernel, outs, (mine,), [VMEM], scratch,
         limit=8, flops=1_000_000_000, name="mine", out_specs=(HBM, HBM),
     )
     grad_first, grad_second = call(
-        other_kernel, outs, (other, *halves), [VMEM, HBM, HBM], scratch,
+        other_kernel, outs, (other, *parts), [VMEM, HBM, HBM], scratch,
         limit=8, name="other", out_specs=(HBM, HBM), aliases={1: 0, 2: 1},
     )
     shape = (3, 3, CH, CH)

time: 97 us -> 95.8 us (0.988)
    pallas_call x6 -> x7, Pallas kernels: 21.1 us -> 20.3 us  [call(): pl.pallas_call(kernel, out_shape=shapes, in_specs=list(ins), input_output...]
    ppermute x2 -> x3, waiting for transfers between devices: 3.48 us -> 2.91 us  [shift(): lax.ppermute(value, axis, [(i, (i + step) % size) for i in range(size)])]
    ppermute x2 -> x3, starting transfers between devices: 5.64 us -> 5.8 us  [shift(): lax.ppermute(value, axis, [(i, (i + step) % size) for i in range(size)])]
    unnamed x16 -> x18, local copies, waits for them, and re-layouts: 4.38 us -> 4.38 us
  transfers between devices with their start and end apart: 8 -> 9, of which waited for: 5 -> 6; matrix products, arithmetic and copies ran while one was open for 0% -> 0% of each run, Pallas kernels for 8% -> 8%
where the time goes in v8:
time: 95.8 us; the launch traced here: 95.4 us
  blocking collectives  25.9 us (27%)
  starting transfers between devices  24.6 us (26%)
  Pallas kernels  20.3 us (21%)
  waiting for transfers between devices  17 us (18%)
  local copies, waits for them, and re-layouts  5.48 us (6%)
  other arithmetic  1.16 us (1%)
  between operations  1.03 us (1%)
    all_to_all x1, blocking collectives, per_device(): spread = lax.all_to_all(spread, PLANE, 0, 0, tiled=True)  25.9 us
    pallas_call x7, Pallas kernels, call(): pl.pallas_call(kernel, out_shape=shapes, in_specs=list(ins), input_output...  20.3 us
    all_to_all x1, waiting for transfers between devices, per_device(): lax.all_to_all(jnp.broadcast_to(piece, (32, part, CH)), PLANE, 0, 0, tile...  10.5 us
    ppermute x3, starting transfers between devices, per_device(): one, two, three = [lax.ppermute(send, DEPTH, ring(k)) for k in (2, 4, 6)]  7.64 us
    ppermute x3, starting transfers between devices, shift(): lax.ppermute(value, axis, [(i, (i + step) % size) for i in range(size)])  5.8 us
    all_to_all x1, starting transfers between devices, per_device(): lax.all_to_all(jnp.broadcast_to(piece, (32, part, CH)), PLANE, 0, 0, tile...  4.54 us
    unnamed x18, local copies, waits for them, and re-layouts  4.38 us
    ppermute x1, starting transfers between devices, per_device(): below = lax.ppermute(up, DEPTH, ring(7))  4.03 us
  transfers between devices with their start and end apart: 9, of which 6 were waited for; matrix products, arithmetic and copies ran while one was open for 0% of the time, Pallas kernels for 8%

profile of v8, /device:TPU:1, one launch (start us, length us, event | category | flops | bytes accessed | tf_op | source)
XLA Modules:
  0.0 95.4 jit_solution(11231159801978553835)
XLA Ops:
  0.6 1.1 %copy-done = bf16[1,16,96,256]{3,2,1,0:T(8,128)(2,1)S(1)} copy-done((bf16[1,16,96,256]{3,2,1,0:T(8,128)(2,1)S(1)}, bf16[1,16,96,256]{3,2,1,0:T(8,128)(2,1)}, u32[]{:S(2)}) %copy-start) | copy-done | bytes 786456
  2.6 2.5 %collective-permute-start = (bf16[400,256]{1,0:T(8,128)(2,1)S(1)}, bf16[400,256]{1,0:T(8,128)(2,1)S(1)}, u32[]{:S(2)}, u32[]{:S(2)}) collective-permute-start(bf16[400,256]{1,0:T(8,128)(2,1)S(1)} %get-tuple-element.33), channel_id=1, source_target_pairs={{0,64},{64,128},{128,192},{192,8},{8,72},{72,136},{136,200},{200,0... | collective-permute-start | bytes 614408 | tf_op jit(solution)/shard_map/ppermute | solution.py:317
  5.1 4.0 %collective-permute-start.1 = (bf16[400,256]{1,0:T(8,128)(2,1)S(1)}, bf16[400,256]{1,0:T(8,128)(2,1)S(1)}, u32[]{:S(2)}, u32[]{:S(2)}) collective-permute-start(bf16[400,256]{1,0:T(8,128)(2,1)S(1)} %get-tuple-element.34), channel_id=1, source_target_pairs={{0,200},{64,0},{128,64},{192,128},{8,192},{72,8},{136,72},{200,136... | collective-permute-start | bytes 614408 | tf_op jit(solution)/shard_map/ppermute | solution.py:318
  9.1 1.3 %copy-done.3 = bf16[3,3,256,256]{3,2,1,0:T(8,128)(2,1)S(1)} copy-done((bf16[3,3,256,256]{3,2,1,0:T(8,128)(2,1)S(1)}, bf16[3,3,256,256]{3,2,1,0:T(8,128)(2,1)}, u32[]{:S(2)}) %copy-start.3) | copy-done | bytes 1179672
  10.4 1.3 %copy-done.5 = bf16[3,3,256,256]{3,2,1,0:T(8,128)(2,1)S(1)} copy-done((bf16[3,3,256,256]{3,2,1,0:T(8,128)(2,1)S(1)}, bf16[3,3,256,256]{3,2,1,0:T(8,128)(2,1)}, u32[]{:S(2)}) %copy-start.5) | copy-done | bytes 1179672
  11.7 2.4 %inner.1 = (bf16[1536,768]{1,0:T(8,128)(2,1)S(1)}, bf16[1344,768]{1,0:T(8,128)(2,1)S(1)}, f32[1344,256]{1,0:T(8,128)S(1)}, bf16[2304,256]{1,0:T(8,128)(2,1)S(1)}) custom-call(bf16[1536,256]{1,0:T(8,128)(2,1)S(1)} %get-tuple-element.35.f, bf16[2304,256]{1,0:T(8,128)(2,1)S(1)} %bitcast.20, bf16[2304,256]{1,0:T(8,128)(2,1)S(1)} %bitcast.18), custom_call_target="tpu_custom_call" | custom-call | flops 5000000000 | bytes 3145728 | tf_op jit(solution)/shard_map/inner/pallas_call | solution.py:32
  14.2 6.8 %upper.1 = (bf16[2304,256]{1,0:T(8,128)(2,1)S(1)}, f32[8,256]{1,0:T(8,128)S(1)}, bf16[1920,768]{1,0:T(8,128)(2,1)S(1)}, f32[768,256]{1,0:T(8,128)S(1)}) custom-call(f32[1,3]{1,0:T(1,128)S(1)} %bitcast.24, bf16[400,256]{1,0:T(8,128)(2,1)S(1)} %collective-permute-done.above, bf16[400,256]{1,0:T(8,128)(2,1)S(1)} %collective-permute-done.1.below, ...), custom_call_target="tpu_custom_call" | custom-call | flops 6000000000 | bytes 7200268 | tf_op jit(solution)/shard_map/upper/pallas_call | solution.py:32
  20.9 4.2 %lower.1 = (bf16[2304,256]{1,0:T(8,128)(2,1)S(1)}, bf16[1728,256]{1,0:T(8,128)(2,1)S(1)}) custom-call(bf16[400,256]{1,0:T(8,128)(2,1)S(1)} %collective-permute-done.above, bf16[400,256]{1,0:T(8,128)(2,1)S(1)} %collective-permute-done.1.below, bf16[1536,768]{1,0:T(8,128)(2,1)S(1)} %get-tuple-element.36.fwi, f32[1344,256]{1,0:T(8,128)S(1)} %get-tuple-element.37.slopei, ...), custom_call_target="tpu_custom_call" | custom-call | flops 4000000000 | bytes 9060352 | tf_op jit(solution)/shard_map/lower/pallas_call | solution.py:32
  25.3 1.0 %collective-permute-start.2 = (bf16[1152,256]{1,0:T(8,128)(2,1)S(1)}, bf16[1152,256]{1,0:T(8,128)(2,1)S(1)}, u32[]{:S(2)}, u32[]{:S(2)}) collective-permute-start(bf16[1152,256]{1,0:T(8,128)(2,1)S(1)} %broadcast_select_fusion.1), channel_id=1, source_target_pairs={{0,1},{1,0},{2,3},{3,2},{4,5},{5,4},{6,7},{7,6},{8,9},{9,8},{10,11... | collective-permute-start | bytes 1769480 | tf_op jit(solution)/shard_map/ppermute | solution.py:282
  26.7 1.3 %collective-permute-done.2 = bf16[1152,256]{1,0:T(8,128)(2,1)S(1)} collective-permute-done((bf16[1152,256]{1,0:T(8,128)(2,1)S(1)}, bf16[1152,256]{1,0:T(8,128)(2,1)S(1)}, u32[]{:S(2)}, u32[]{:S(2)}) %collective-permute-start.2) | collective-permute-done | bytes 589856 | tf_op jit(solution)/shard_map/ppermute | solution.py:282
  29.3 25.9 %all_to_all.10 = bf16[32,80,256]{2,1,0:T(8,128)(2,1)S(1)} all-to-all(bf16[32,80,256]{2,1,0:T(8,128)(2,1)S(1)} %pad_maximum_fusion), channel_id=1, replica_groups=mesh['q'=2,'p'=2,'x'=4,'h'=2,'y'=4,'c'=2] {'p','x','y'}, dimensions={0} | all-to-all | bytes 2621440 | tf_op jit(solution)/shard_map/all_to_all | solution.py:368
  55.5 3.7 %collective-permute-start.6 = (bf16[80,256]{1,0:T(8,128)(2,1)S(1)}, bf16[80,256]{1,0:T(8,128)(2,1)S(1)}, u32[]{:S(2)}, u32[]{:S(2)}) collective-permute-start(bf16[80,256]{1,0:T(8,128)(2,1)S(1)} %pad_maximum_fusion.3), channel_id=1, source_target_pairs={{0,136},{64,200},{128,0},{192,64},{8,128},{72,192},{136,8},{200,72... | collective-permute-start | bytes 122888 | tf_op jit(solution)/shard_map/ppermute | solution.py:373
  59.2 0.7 collective-permute-start.5
  60.0 3.2 %collective-permute-start.4 = (bf16[80,256]{1,0:T(8,128)(2,1)S(1)}, bf16[80,256]{1,0:T(8,128)(2,1)S(1)}, u32[]{:S(2)}, u32[]{:S(2)}) collective-permute-start(bf16[80,256]{1,0:T(8,128)(2,1)S(1)} %pad_maximum_fusion.3), channel_id=1, source_target_pairs={{0,8},{64,72},{128,136},{192,200},{8,0},{72,64},{136,128},{200,192... | collective-permute-start | bytes 122888 | tf_op jit(solution)/shard_map/ppermute | solution.py:373
  63.2 1.1 %collective-permute-done.5 = bf16[80,256]{1,0:T(8,128)(2,1)S(1)} collective-permute-done((bf16[80,256]{1,0:T(8,128)(2,1)S(1)}, bf16[80,256]{1,0:T(8,128)(2,1)S(1)}, u32[]{:S(2)}, u32[]{:S(2)}) %collective-permute-start.5) | collective-permute-done | bytes 40992 | tf_op jit(solution)/shard_map/ppermute | solution.py:373
  64.2 2.6 %collective-permute-done.4 = bf16[80,256]{1,0:T(8,128)(2,1)S(1)} collective-permute-done((bf16[80,256]{1,0:T(8,128)(2,1)S(1)}, bf16[80,256]{1,0:T(8,128)(2,1)S(1)}, u32[]{:S(2)}, u32[]{:S(2)}) %collective-permute-start.4) | collective-permute-done | bytes 40992 | tf_op jit(solution)/shard_map/ppermute | solution.py:373
  66.9 1.1 %broadcast_in_dim.7 = bf16[32,72,256]{2,1,0:T(8,128)(2,1)} broadcast(bf16[72,256]{1,0:T(8,128)(2,1)S(1)} %add_convert_fusion.2), dimensions={1,2} | broadcast | bytes 1216512 | tf_op jit(solution)/shard_map/broadcast_in_dim | solution.py:386
  67.9 4.5 %all-to-all-start.1 = ((bf16[32,72,256]{2,1,0:T(8,128)(2,1)}), bf16[32,72,256]{2,1,0:T(8,128)(2,1)S(1)}, u32[]{:S(2)}, u32[]{:S(2)}) async-start(bf16[32,72,256]{2,1,0:T(8,128)(2,1)} %broadcast_in_dim.7), calls=%async_computation.1 | async-start | bytes 2359296 | tf_op jit(solution)/shard_map/all_to_all | solution.py:386
  72.5 3.8 %feature.1 = (bf16[1536,256]{1,0:T(8,128)(2,1)}, f32[3,256]{1,0:T(4,128)}, f32[1,3]{1,0:T(1,128)}) custom-call(bf16[1728,256]{1,0:T(8,128)(2,1)S(1)} %get-tuple-element.45.fg, bf16[2304,256]{1,0:T(8,128)(2,1)S(1)} %bitcast.22, f32[4,256]{1,0:T(4,128)S(1)} %fusion.5.sums), custom_call_target="tpu_custom_call" | custom-call | flops 2500000000 | bytes 2068480 | tf_op jit(solution)/shard_map/feature/pallas_call | solution.py:32
  76.4 10.5 %all-to-all-done.1 = bf16[32,72,256]{2,1,0:T(8,128)(2,1)S(1)} async-done(((bf16[32,72,256]{2,1,0:T(8,128)(2,1)}), bf16[32,72,256]{2,1,0:T(8,128)(2,1)S(1)}, u32[]{:S(2)}, u32[]{:S(2)}) %all-to-all-start.1) | async-done | bytes 1179680 | tf_op jit(solution)/shard_map/all_to_all | solution.py:386
  86.9 4.5 %collective-permute-start.7 = (bf16[2304,256]{1,0:T(8,128)(2,1)S(1)}, bf16[2304,256]{1,0:T(8,128)(2,1)S(1)}, u32[]{:S(2)}, u32[]{:S(2)}) collective-permute-start(bf16[2304,256]{1,0:T(8,128)(2,1)S(1)} %bitcast.13), channel_id=1, source_target_pairs={{0,1},{1,0},{2,3},{3,2},{4,5},{5,4},{6,7},{7,6},{8,9},{9,8},{10,11... | collective-permute-start | bytes 3538952 | tf_op jit(solution)/shard_map/ppermute | solution.py:282
  91.3 1.5 %mine.1 = (f32[2304,256]{1,0:T(8,128)}, f32[2304,256]{1,0:T(8,128)}) custom-call(bf16[2304,256]{1,0:T(8,128)(2,1)S(1)} %bitcast.14), custom_call_target="tpu_custom_call" | custom-call | flops 1000000000 | bytes 1179648 | tf_op jit(solution)/shard_map/mine/pallas_call | solution.py:32
  92.8 1.0 %collective-permute-done.7.other = bf16[2304,256]{1,0:T(8,128)(2,1)S(1)} collective-permute-done((bf16[2304,256]{1,0:T(8,128)(2,1)S(1)}, bf16[2304,256]{1,0:T(8,128)(2,1)S(1)}, u32[]{:S(2)}, u32[]{:S(2)}) %collective-permute-start.7) | collective-permute-done | bytes 1179680 | tf_op jit(solution)/shard_map/ppermute | solution.py:282
  93.8 1.5 %other.1 = (f32[2304,256]{1,0:T(8,128)}, f32[2304,256]{1,0:T(8,128)}) custom-call(bf16[2304,256]{1,0:T(8,128)(2,1)S(1)} %collective-permute-done.7.other, f32[2304,256]{1,0:T(8,128)} %get-tuple-element.49.g1_in, f32[2304,256]{1,0:T(8,128)} %get-tuple-element.50.g2_in), custom_call_target="tpu_custom_call", output_to_operand_aliasing={{0}: (1, {}), {1}: (2, {})} | custom-call | bytes 5898240 | tf_op jit(solution)/shard_map/other/pallas_call | solution.py:32
  (44 shorter events, 2.9 us)
Async XLA Ops:
  0.6 1.1 %copy-start = (bf16[1,16,96,256]{3,2,1,0:T(8,128)(2,1)S(1)}, bf16[1,16,96,256]{3,2,1,0:T(8,128)(2,1)}, u32[]{:S(2)}) copy-start(bf16[1,16,96,256]{3,2,1,0:T(8,128)(2,1)} %param.6) | copy-start | bytes 2359300
  1.8 0.7 copy-start.1
  2.6 11.5 %collective-permute-start = (bf16[400,256]{1,0:T(8,128)(2,1)S(1)}, bf16[400,256]{1,0:T(8,128)(2,1)S(1)}, u32[]{:S(2)}, u32[]{:S(2)}) collective-permute-start(bf16[400,256]{1,0:T(8,128)(2,1)S(1)} %get-tuple-element.33), channel_id=1, source_target_pairs={{0,64},{64,128},{128,192},{192,8},{8,72},{72,136},{136,200},{200,0... | collective-permute-start | bytes 614408 | tf_op jit(solution)/shard_map/ppermute | solution.py:317
  5.1 9.0 %collective-permute-start.1 = (bf16[400,256]{1,0:T(8,128)(2,1)S(1)}, bf16[400,256]{1,0:T(8,128)(2,1)S(1)}, u32[]{:S(2)}, u32[]{:S(2)}) collective-permute-start(bf16[400,256]{1,0:T(8,128)(2,1)S(1)} %get-tuple-element.34), channel_id=1, source_target_pairs={{0,200},{64,0},{128,64},{192,128},{8,192},{72,8},{136,72},{200,136... | collective-permute-start | bytes 614408 | tf_op jit(solution)/shard_map/ppermute | solution.py:318
  9.1 1.3 %copy-start.3 = (bf16[3,3,256,256]{3,2,1,0:T(8,128)(2,1)S(1)}, bf16[3,3,256,256]{3,2,1,0:T(8,128)(2,1)}, u32[]{:S(2)}) copy-start(bf16[3,3,256,256]{3,2,1,0:T(8,128)(2,1)} %param.8) | copy-start | bytes 3538948
  10.4 1.3 %copy-start.5 = (bf16[3,3,256,256]{3,2,1,0:T(8,128)(2,1)S(1)}, bf16[3,3,256,256]{3,2,1,0:T(8,128)(2,1)}, u32[]{:S(2)}) copy-start(bf16[3,3,256,256]{3,2,1,0:T(8,128)(2,1)} %param.7) | copy-start | bytes 3538948
  11.7 2.4 %copy-start.2 = (s32[1,16,96]{2,1,0:T(8,128)S(1)}, s32[1,16,96]{2,1,0:T(8,128)}, u32[]{:S(2)}) copy-start(s32[1,16,96]{2,1,0:T(8,128)} %param.11) | copy-start | bytes 18436
  11.7 2.4 %copy-start.4 = (bf16[3,3,256,256]{3,2,1,0:T(8,128)(2,1)S(1)}, bf16[3,3,256,256]{3,2,1,0:T(8,128)(2,1)}, u32[]{:S(2)}) copy-start(bf16[3,3,256,256]{3,2,1,0:T(8,128)(2,1)} %param.8) | copy-start | bytes 3538948
  11.7 2.5 %copy-start.6 = (bf16[3,3,256,256]{3,2,1,0:T(8,128)(2,1)S(1)}, bf16[3,3,256,256]{3,2,1,0:T(8,128)(2,1)}, u32[]{:S(2)}) copy-start(bf16[3,3,256,256]{3,2,1,0:T(8,128)(2,1)} %param.7) | copy-start | bytes 3538948
  11.7 2.5 %copy-start.7 = (bf16[256,3]{0,1:T(4,128)(2,1)S(1)}, bf16[256,3]{0,1:T(4,128)(2,1)}, u32[]{:S(2)}) copy-start(bf16[256,3]{0,1:T(4,128)(2,1)} %param.9) | copy-start | bytes 4612
  11.7 2.5 %copy-start.8 = (f32[3]{0:T(128)S(1)}, f32[3]{0:T(128)}, u32[]{:S(2)}) copy-start(f32[3]{0:T(128)} %param.10) | copy-start | bytes 40
  25.3 2.7 %collective-permute-start.2 = (bf16[1152,256]{1,0:T(8,128)(2,1)S(1)}, bf16[1152,256]{1,0:T(8,128)(2,1)S(1)}, u32[]{:S(2)}, u32[]{:S(2)}) collective-permute-start(bf16[1152,256]{1,0:T(8,128)(2,1)S(1)} %broadcast_select_fusion.1), channel_id=1, source_target_pairs={{0,1},{1,0},{2,3},{3,2},{4,5},{5,4},{6,7},{7,6},{8,9},{9,8},{10,11... | collective-permute-start | bytes 1769480 | tf_op jit(solution)/shard_map/ppermute | solution.py:282
  26.4 2.4 %collective-permute-start.3 = (bf16[1168,256]{1,0:T(8,128)(2,1)S(1)}, bf16[1168,256]{1,0:T(8,128)(2,1)S(1)}, u32[]{:S(2)}, u32[]{:S(2)}) collective-permute-start(bf16[1168,256]{1,0:T(8,128)(2,1)S(1)} %pad_maximum_fusion.2), channel_id=1, source_target_pairs={{0,1},{1,0},{2,3},{3,2},{4,5},{5,4},{6,7},{7,6},{8,9},{9,8},{10,11... | collective-permute-start | bytes 1794056 | tf_op jit(solution)/shard_map/ppermute | solution.py:282
  55.5 7.6 %collective-permute-start.6 = (bf16[80,256]{1,0:T(8,128)(2,1)S(1)}, bf16[80,256]{1,0:T(8,128)(2,1)S(1)}, u32[]{:S(2)}, u32[]{:S(2)}) collective-permute-start(bf16[80,256]{1,0:T(8,128)(2,1)S(1)} %pad_maximum_fusion.3), channel_id=1, source_target_pairs={{0,136},{64,200},{128,0},{192,64},{8,128},{72,192},{136,8},{200,72... | collective-permute-start | bytes 122888 | tf_op jit(solution)/shard_map/ppermute | solution.py:373
  59.2 5.0 %collective-permute-start.5 = (bf16[80,256]{1,0:T(8,128)(2,1)S(1)}, bf16[80,256]{1,0:T(8,128)(2,1)S(1)}, u32[]{:S(2)}, u32[]{:S(2)}) collective-permute-start(bf16[80,256]{1,0:T(8,128)(2,1)S(1)} %pad_maximum_fusion.3), channel_id=1, source_target_pairs={{0,128},{64,192},{128,8},{192,72},{8,136},{72,200},{136,0},{200,64... | collective-permute-start | bytes 122888 | tf_op jit(solution)/shard_map/ppermute | solution.py:373
  60.0 6.9 %collective-permute-start.4 = (bf16[80,256]{1,0:T(8,128)(2,1)S(1)}, bf16[80,256]{1,0:T(8,128)(2,1)S(1)}, u32[]{:S(2)}, u32[]{:S(2)}) collective-permute-start(bf16[80,256]{1,0:T(8,128)(2,1)S(1)} %pad_maximum_fusion.3), channel_id=1, source_target_pairs={{0,8},{64,72},{128,136},{192,200},{8,0},{72,64},{136,128},{200,192... | collective-permute-start | bytes 122888 | tf_op jit(solution)/shard_map/ppermute | solution.py:373
  67.9 18.9 %all-to-all-start.1 = ((bf16[32,72,256]{2,1,0:T(8,128)(2,1)}), bf16[32,72,256]{2,1,0:T(8,128)(2,1)S(1)}, u32[]{:S(2)}, u32[]{:S(2)}) async-start(bf16[32,72,256]{2,1,0:T(8,128)(2,1)} %broadcast_in_dim.7), calls=%async_computation.1 | async-start | bytes 2359296 | tf_op jit(solution)/shard_map/all_to_all | solution.py:386
  86.9 6.9 %collective-permute-start.7 = (bf16[2304,256]{1,0:T(8,128)(2,1)S(1)}, bf16[2304,256]{1,0:T(8,128)(2,1)S(1)}, u32[]{:S(2)}, u32[]{:S(2)}) collective-permute-start(bf16[2304,256]{1,0:T(8,128)(2,1)S(1)} %bitcast.13), channel_id=1, source_target_pairs={{0,1},{1,0},{2,3},{3,2},{4,5},{5,4},{6,7},{7,6},{8,9},{9,8},{10,11... | collective-permute-start | bytes 3538952 | tf_op jit(solution)/shard_map/ppermute | solution.py:282

commit v9 on v8

--- a/solution.py
+++ b/solution.py
@@ -267,8 +267,17 @@
     convert_out(mine, lax.axis_index("c"), g1, g2, wide, sems)
 
 
-def other_kernel(other, g1_in, g2_in, g1, g2, wide, sems):
-    convert_out(other, 1 - lax.axis_index("c"), g1, g2, wide, sems)
+def other_kernel(block, _, out, wide, sems):
+    owner = 1 - lax.axis_index("c")
+    copies = []
+    for t in range(3):
+        at = pl.ds(t * 384, 384)
+        row = pl.multiple_of(owner * HALF + t * 384, 384)
+        wide[at, :] = block[at, :].astype(F32)
+        copies.append(pltpu.make_async_copy(wide.at[at], out.at[pl.ds(row, 384)], sems.at[t]))
+        copies[-1].start()
+    for copy in copies:
+        copy.wait()
 
 
 def ring(step):
@@ -386,17 +395,21 @@
     full = lax.all_to_all(jnp.broadcast_to(piece, (32, part, CH)), PLANE, 0, 0, tiled=True)
     full, grad_features = lax.optimization_barrier((full, grad_features))
     mine = full.reshape(9 * CH, CH)
-    other = shift(mine, "c", 1, 2)
+    others = [shift(mine[k * HALF:(k + 1) * HALF], "c", 1, 2) for k in range(2)]
     outs = [((9 * CH, CH), F32)] * 2
     scratch = [pltpu.VMEM((9 * CH, CH), F32), pltpu.SemaphoreType.DMA((6,))]
     parts = call(
         mine_kernel, outs, (mine,), [VMEM], scratch,
         limit=8, flops=1_000_000_000, name="mine", out_specs=(HBM, HBM),
     )
-    grad_first, grad_second = call(
-        other_kernel, outs, (other, *parts), [VMEM, HBM, HBM], scratch,
-        limit=8, name="other", out_specs=(HBM, HBM), aliases={1: 0, 2: 1},
-    )
+    scratch = [pltpu.VMEM((HALF, CH), F32), pltpu.SemaphoreType.DMA((3,))]
+    grad_first, grad_second = [
+        call(
+            other_kernel, outs[:1], (block, part_out), [VMEM, HBM], scratch,
+            limit=8, name="other", out_specs=(HBM,), aliases={1: 0},
+        )[0]
+        for block, part_out in zip(others, parts)
+    ]
     shape = (3, 3, CH, CH)
     return (
         grad_features.reshape(features.shape), grad_first.reshape(shape), grad_second.reshape(shape),

time: 95.8 us -> 96 us (level)
    ppermute x3 -> x4, waiting for transfers between devices: 2.91 us -> 1.92 us  [shift(): lax.ppermute(value, axis, [(i, (i + step) % size) for i in range(size)])]
    pallas_call x7 -> x8, Pallas kernels: 20.3 us -> 21.2 us  [call(): pl.pallas_call(kernel, out_shape=shapes, in_specs=list(ins), input_output...]
    ppermute x3 -> x4, starting transfers between devices: 5.8 us -> 5.96 us  [shift(): lax.ppermute(value, axis, [(i, (i + step) % size) for i in range(size)])]
  transfers between devices with their start and end apart: 9 -> 10, of which waited for: 6 -> 6; matrix products, arithmetic and copies ran while one was open for 0% -> 0% of each run, Pallas kernels for 8% -> 9%
where the time goes in v9:
time: 96 us; the launch traced here: 95.6 us
  blocking collectives  25.9 us (27%)
  starting transfers between devices  24.7 us (26%)
  Pallas kernels  21.2 us (22%)
  waiting for transfers between devices  16.1 us (17%)
  local copies, waits for them, and re-layouts  5.56 us (6%)
  other arithmetic  1.16 us (1%)
  between operations  1.05 us (1%)
    all_to_all x1, blocking collectives, per_device(): spread = lax.all_to_all(spread, PLANE, 0, 0, tiled=True)  25.9 us
    pallas_call x8, Pallas kernels, call(): pl.pallas_call(kernel, out_shape=shapes, in_specs=list(ins), input_output...  21.2 us
    all_to_all x1, waiting for transfers between devices, per_device(): lax.all_to_all(jnp.broadcast_to(piece, (32, part, CH)), PLANE, 0, 0, tile...  10.5 us
    ppermute x3, starting transfers between devices, per_device(): one, two, three = [lax.ppermute(send, DEPTH, ring(k)) for k in (2, 4, 6)]  7.6 us
    ppermute x4, starting transfers between devices, shift(): lax.ppermute(value, axis, [(i, (i + step) % size) for i in range(size)])  5.96 us
    all_to_all x1, starting transfers between devices, per_device(): lax.all_to_all(jnp.broadcast_to(piece, (32, part, CH)), PLANE, 0, 0, tile...  4.54 us
    unnamed x18, local copies, waits for them, and re-layouts  4.38 us
    ppermute x1, starting transfers between devices, per_device(): below = lax.ppermute(up, DEPTH, ring(7))  4.03 us
  transfers between devices with their start and end apart: 10, of which 6 were waited for; matrix products, arithmetic and copies ran while one was open for 0% of the time, Pallas kernels for 9%

profile of v9, /device:TPU:1, one launch (start us, length us, event | category | flops | bytes accessed | tf_op | source)
XLA Modules:
  0.0 95.6 jit_solution(6997457819029394183)
XLA Ops:
  0.6 1.1 %copy-done = bf16[1,16,96,256]{3,2,1,0:T(8,128)(2,1)S(1)} copy-done((bf16[1,16,96,256]{3,2,1,0:T(8,128)(2,1)S(1)}, bf16[1,16,96,256]{3,2,1,0:T(8,128)(2,1)}, u32[]{:S(2)}) %copy-start) | copy-done | bytes 786456
  2.6 2.5 %collective-permute-start = (bf16[400,256]{1,0:T(8,128)(2,1)S(1)}, bf16[400,256]{1,0:T(8,128)(2,1)S(1)}, u32[]{:S(2)}, u32[]{:S(2)}) collective-permute-start(bf16[400,256]{1,0:T(8,128)(2,1)S(1)} %get-tuple-element.31), channel_id=1, source_target_pairs={{0,64},{64,128},{128,192},{192,8},{8,72},{72,136},{136,200},{200,0... | collective-permute-start | bytes 614408 | tf_op jit(solution)/shard_map/ppermute | solution.py:326
  5.1 4.0 %collective-permute-start.1 = (bf16[400,256]{1,0:T(8,128)(2,1)S(1)}, bf16[400,256]{1,0:T(8,128)(2,1)S(1)}, u32[]{:S(2)}, u32[]{:S(2)}) collective-permute-start(bf16[400,256]{1,0:T(8,128)(2,1)S(1)} %get-tuple-element.32), channel_id=1, source_target_pairs={{0,200},{64,0},{128,64},{192,128},{8,192},{72,8},{136,72},{200,136... | collective-permute-start | bytes 614408 | tf_op jit(solution)/shard_map/ppermute | solution.py:327
  9.1 1.3 %copy-done.3 = bf16[3,3,256,256]{3,2,1,0:T(8,128)(2,1)S(1)} copy-done((bf16[3,3,256,256]{3,2,1,0:T(8,128)(2,1)S(1)}, bf16[3,3,256,256]{3,2,1,0:T(8,128)(2,1)}, u32[]{:S(2)}) %copy-start.3) | copy-done | bytes 1179672
  10.4 1.3 %copy-done.5 = bf16[3,3,256,256]{3,2,1,0:T(8,128)(2,1)S(1)} copy-done((bf16[3,3,256,256]{3,2,1,0:T(8,128)(2,1)S(1)}, bf16[3,3,256,256]{3,2,1,0:T(8,128)(2,1)}, u32[]{:S(2)}) %copy-start.5) | copy-done | bytes 1179672
  11.7 2.4 %inner.1 = (bf16[1536,768]{1,0:T(8,128)(2,1)S(1)}, bf16[1344,768]{1,0:T(8,128)(2,1)S(1)}, f32[1344,256]{1,0:T(8,128)S(1)}, bf16[2304,256]{1,0:T(8,128)(2,1)S(1)}) custom-call(bf16[1536,256]{1,0:T(8,128)(2,1)S(1)} %get-tuple-element.33.f, bf16[2304,256]{1,0:T(8,128)(2,1)S(1)} %bitcast.21, bf16[2304,256]{1,0:T(8,128)(2,1)S(1)} %bitcast.19), custom_call_target="tpu_custom_call" | custom-call | flops 5000000000 | bytes 3145728 | tf_op jit(solution)/shard_map/inner/pallas_call | solution.py:32
  14.2 6.9 %upper.1 = (bf16[2304,256]{1,0:T(8,128)(2,1)S(1)}, f32[8,256]{1,0:T(8,128)S(1)}, bf16[1920,768]{1,0:T(8,128)(2,1)S(1)}, f32[768,256]{1,0:T(8,128)S(1)}) custom-call(f32[1,3]{1,0:T(1,128)S(1)} %bitcast.25, bf16[400,256]{1,0:T(8,128)(2,1)S(1)} %collective-permute-done.above, bf16[400,256]{1,0:T(8,128)(2,1)S(1)} %collective-permute-done.1.below, ...), custom_call_target="tpu_custom_call" | custom-call | flops 6000000000 | bytes 7200268 | tf_op jit(solution)/shard_map/upper/pallas_call | solution.py:32
  21.1 4.3 %lower.1 = (bf16[2304,256]{1,0:T(8,128)(2,1)S(1)}, bf16[1728,256]{1,0:T(8,128)(2,1)S(1)}) custom-call(bf16[400,256]{1,0:T(8,128)(2,1)S(1)} %collective-permute-done.above, bf16[400,256]{1,0:T(8,128)(2,1)S(1)} %collective-permute-done.1.below, bf16[1536,768]{1,0:T(8,128)(2,1)S(1)} %get-tuple-element.34.fwi, f32[1344,256]{1,0:T(8,128)S(1)} %get-tuple-element.35.slopei, ...), custom_call_target="tpu_custom_call" | custom-call | flops 4000000000 | bytes 9060352 | tf_op jit(solution)/shard_map/lower/pallas_call | solution.py:32
  25.6 1.1 %collective-permute-start.2 = (bf16[1152,256]{1,0:T(8,128)(2,1)S(1)}, bf16[1152,256]{1,0:T(8,128)(2,1)S(1)}, u32[]{:S(2)}, u32[]{:S(2)}) collective-permute-start(bf16[1152,256]{1,0:T(8,128)(2,1)S(1)} %broadcast_select_fusion.1), channel_id=1, source_target_pairs={{0,1},{1,0},{2,3},{3,2},{4,5},{5,4},{6,7},{7,6},{8,9},{9,8},{10,11... | collective-permute-start | bytes 1769480 | tf_op jit(solution)/shard_map/ppermute | solution.py:291
  27.0 1.3 %collective-permute-done.2 = bf16[1152,256]{1,0:T(8,128)(2,1)S(1)} collective-permute-done((bf16[1152,256]{1,0:T(8,128)(2,1)S(1)}, bf16[1152,256]{1,0:T(8,128)(2,1)S(1)}, u32[]{:S(2)}, u32[]{:S(2)}) %collective-permute-start.2) | collective-permute-done | bytes 589856 | tf_op jit(solution)/shard_map/ppermute | solution.py:291
  29.6 25.9 %all_to_all.10 = bf16[32,80,256]{2,1,0:T(8,128)(2,1)S(1)} all-to-all(bf16[32,80,256]{2,1,0:T(8,128)(2,1)S(1)} %pad_maximum_fusion), channel_id=1, replica_groups=mesh['q'=2,'p'=2,'x'=4,'h'=2,'y'=4,'c'=2] {'p','x','y'}, dimensions={0} | all-to-all | bytes 2621440 | tf_op jit(solution)/shard_map/all_to_all | solution.py:377
  55.8 3.7 %collective-permute-start.6 = (bf16[80,256]{1,0:T(8,128)(2,1)S(1)}, bf16[80,256]{1,0:T(8,128)(2,1)S(1)}, u32[]{:S(2)}, u32[]{:S(2)}) collective-permute-start(bf16[80,256]{1,0:T(8,128)(2,1)S(1)} %pad_maximum_fusion.3), channel_id=1, source_target_pairs={{0,136},{64,200},{128,0},{192,64},{8,128},{72,192},{136,8},{200,72... | collective-permute-start | bytes 122888 | tf_op jit(solution)/shard_map/ppermute | solution.py:382
  59.4 0.7 collective-permute-start.5
  60.2 3.2 %collective-permute-start.4 = (bf16[80,256]{1,0:T(8,128)(2,1)S(1)}, bf16[80,256]{1,0:T(8,128)(2,1)S(1)}, u32[]{:S(2)}, u32[]{:S(2)}) collective-permute-start(bf16[80,256]{1,0:T(8,128)(2,1)S(1)} %pad_maximum_fusion.3), channel_id=1, source_target_pairs={{0,8},{64,72},{128,136},{192,200},{8,0},{72,64},{136,128},{200,192... | collective-permute-start | bytes 122888 | tf_op jit(solution)/shard_map/ppermute | solution.py:382
  63.4 1.1 %collective-permute-done.5 = bf16[80,256]{1,0:T(8,128)(2,1)S(1)} collective-permute-done((bf16[80,256]{1,0:T(8,128)(2,1)S(1)}, bf16[80,256]{1,0:T(8,128)(2,1)S(1)}, u32[]{:S(2)}, u32[]{:S(2)}) %collective-permute-start.5) | collective-permute-done | bytes 40992 | tf_op jit(solution)/shard_map/ppermute | solution.py:382
  64.4 2.6 %collective-permute-done.4 = bf16[80,256]{1,0:T(8,128)(2,1)S(1)} collective-permute-done((bf16[80,256]{1,0:T(8,128)(2,1)S(1)}, bf16[80,256]{1,0:T(8,128)(2,1)S(1)}, u32[]{:S(2)}, u32[]{:S(2)}) %collective-permute-start.4) | collective-permute-done | bytes 40992 | tf_op jit(solution)/shard_map/ppermute | solution.py:382
  67.1 1.1 %broadcast_in_dim.7 = bf16[32,72,256]{2,1,0:T(8,128)(2,1)} broadcast(bf16[72,256]{1,0:T(8,128)(2,1)S(1)} %add_convert_fusion.2), dimensions={1,2} | broadcast | bytes 1216512 | tf_op jit(solution)/shard_map/broadcast_in_dim | solution.py:395
  68.1 4.5 %all-to-all-start.1 = ((bf16[32,72,256]{2,1,0:T(8,128)(2,1)}), bf16[32,72,256]{2,1,0:T(8,128)(2,1)S(1)}, u32[]{:S(2)}, u32[]{:S(2)}) async-start(bf16[32,72,256]{2,1,0:T(8,128)(2,1)} %broadcast_in_dim.7), calls=%async_computation.1 | async-start | bytes 2359296 | tf_op jit(solution)/shard_map/all_to_all | solution.py:395
  72.7 3.8 %feature.1 = (bf16[1536,256]{1,0:T(8,128)(2,1)}, f32[3,256]{1,0:T(4,128)}, f32[1,3]{1,0:T(1,128)}) custom-call(bf16[1728,256]{1,0:T(8,128)(2,1)S(1)} %get-tuple-element.43.fg, bf16[2304,256]{1,0:T(8,128)(2,1)S(1)} %bitcast.23, f32[4,256]{1,0:T(4,128)S(1)} %fusion.5.sums), custom_call_target="tpu_custom_call" | custom-call | flops 2500000000 | bytes 2068480 | tf_op jit(solution)/shard_map/feature/pallas_call | solution.py:32
  76.6 10.5 %all-to-all-done.1 = bf16[32,72,256]{2,1,0:T(8,128)(2,1)S(1)} async-done(((bf16[32,72,256]{2,1,0:T(8,128)(2,1)}), bf16[32,72,256]{2,1,0:T(8,128)(2,1)S(1)}, u32[]{:S(2)}, u32[]{:S(2)}) %all-to-all-start.1) | async-done | bytes 1179680 | tf_op jit(solution)/shard_map/all_to_all | solution.py:395
  87.2 4.5 %collective-permute-start.7 = (bf16[1152,256]{1,0:T(8,128)(2,1)S(1)}, bf16[1152,256]{1,0:T(8,128)(2,1)S(1)}, u32[]{:S(2)}, u32[]{:S(2)}) collective-permute-start(bf16[1152,256]{1,0:T(8,128)(2,1)S(1)} %bitcast.30), channel_id=1, source_target_pairs={{0,1},{1,0},{2,3},{3,2},{4,5},{5,4},{6,7},{7,6},{8,9},{9,8},{10,11... | collective-permute-start | bytes 1769480 | tf_op jit(solution)/shard_map/ppermute | solution.py:291
  91.8 1.5 %mine.1 = (f32[2304,256]{1,0:T(8,128)}, f32[2304,256]{1,0:T(8,128)}) custom-call(bf16[2304,256]{1,0:T(8,128)(2,1)S(1)} %bitcast.15), custom_call_target="tpu_custom_call" | custom-call | flops 1000000000 | bytes 1179648 | tf_op jit(solution)/shard_map/mine/pallas_call | solution.py:32
  93.3 1.1 %other.2 = f32[2304,256]{1,0:T(8,128)} custom-call(bf16[1152,256]{1,0:T(8,128)(2,1)S(1)} %collective-permute-done.7.block, f32[2304,256]{1,0:T(8,128)} %get-tuple-element.47._), custom_call_target="tpu_custom_call", output_to_operand_aliasing={{}: (1, {})} | custom-call | bytes 2949120 | tf_op jit(solution)/shard_map/other/pallas_call | solution.py:32
  94.4 1.1 %other.3 = f32[2304,256]{1,0:T(8,128)} custom-call(bf16[1152,256]{1,0:T(8,128)(2,1)S(1)} %collective-permute-done.8.block, f32[2304,256]{1,0:T(8,128)} %get-tuple-element.48._), custom_call_target="tpu_custom_call", output_to_operand_aliasing={{}: (1, {})} | custom-call | bytes 2949120 | tf_op jit(solution)/shard_map/other/pallas_call | solution.py:32
  (48 shorter events, 3.1 us)
Async XLA Ops:
  0.6 1.1 %copy-start = (bf16[1,16,96,256]{3,2,1,0:T(8,128)(2,1)S(1)}, bf16[1,16,96,256]{3,2,1,0:T(8,128)(2,1)}, u32[]{:S(2)}) copy-start(bf16[1,16,96,256]{3,2,1,0:T(8,128)(2,1)} %param.6) | copy-start | bytes 2359300
  1.8 0.7 copy-start.1
  2.6 11.6 %collective-permute-start = (bf16[400,256]{1,0:T(8,128)(2,1)S(1)}, bf16[400,256]{1,0:T(8,128)(2,1)S(1)}, u32[]{:S(2)}, u32[]{:S(2)}) collective-permute-start(bf16[400,256]{1,0:T(8,128)(2,1)S(1)} %get-tuple-element.31), channel_id=1, source_target_pairs={{0,64},{64,128},{128,192},{192,8},{8,72},{72,136},{136,200},{200,0... | collective-permute-start | bytes 614408 | tf_op jit(solution)/shard_map/ppermute | solution.py:326
  5.1 9.0 %collective-permute-start.1 = (bf16[400,256]{1,0:T(8,128)(2,1)S(1)}, bf16[400,256]{1,0:T(8,128)(2,1)S(1)}, u32[]{:S(2)}, u32[]{:S(2)}) collective-permute-start(bf16[400,256]{1,0:T(8,128)(2,1)S(1)} %get-tuple-element.32), channel_id=1, source_target_pairs={{0,200},{64,0},{128,64},{192,128},{8,192},{72,8},{136,72},{200,136... | collective-permute-start | bytes 614408 | tf_op jit(solution)/shard_map/ppermute | solution.py:327
  9.1 1.3 %copy-start.3 = (bf16[3,3,256,256]{3,2,1,0:T(8,128)(2,1)S(1)}, bf16[3,3,256,256]{3,2,1,0:T(8,128)(2,1)}, u32[]{:S(2)}) copy-start(bf16[3,3,256,256]{3,2,1,0:T(8,128)(2,1)} %param.8) | copy-start | bytes 3538948
  10.4 1.3 %copy-start.5 = (bf16[3,3,256,256]{3,2,1,0:T(8,128)(2,1)S(1)}, bf16[3,3,256,256]{3,2,1,0:T(8,128)(2,1)}, u32[]{:S(2)}) copy-start(bf16[3,3,256,256]{3,2,1,0:T(8,128)(2,1)} %param.7) | copy-start | bytes 3538948
  11.7 2.5 %copy-start.2 = (s32[1,16,96]{2,1,0:T(8,128)S(1)}, s32[1,16,96]{2,1,0:T(8,128)}, u32[]{:S(2)}) copy-start(s32[1,16,96]{2,1,0:T(8,128)} %param.11) | copy-start | bytes 18436
  11.7 2.5 %copy-start.4 = (bf16[3,3,256,256]{3,2,1,0:T(8,128)(2,1)S(1)}, bf16[3,3,256,256]{3,2,1,0:T(8,128)(2,1)}, u32[]{:S(2)}) copy-start(bf16[3,3,256,256]{3,2,1,0:T(8,128)(2,1)} %param.8) | copy-start | bytes 3538948
  11.7 2.5 %copy-start.6 = (bf16[3,3,256,256]{3,2,1,0:T(8,128)(2,1)S(1)}, bf16[3,3,256,256]{3,2,1,0:T(8,128)(2,1)}, u32[]{:S(2)}) copy-start(bf16[3,3,256,256]{3,2,1,0:T(8,128)(2,1)} %param.7) | copy-start | bytes 3538948
  11.7 2.5 %copy-start.7 = (bf16[256,3]{0,1:T(4,128)(2,1)S(1)}, bf16[256,3]{0,1:T(4,128)(2,1)}, u32[]{:S(2)}) copy-start(bf16[256,3]{0,1:T(4,128)(2,1)} %param.9) | copy-start | bytes 4612
  11.7 2.5 %copy-start.8 = (f32[3]{0:T(128)S(1)}, f32[3]{0:T(128)}, u32[]{:S(2)}) copy-start(f32[3]{0:T(128)} %param.10) | copy-start | bytes 40
  25.6 2.7 %collective-permute-start.2 = (bf16[1152,256]{1,0:T(8,128)(2,1)S(1)}, bf16[1152,256]{1,0:T(8,128)(2,1)S(1)}, u32[]{:S(2)}, u32[]{:S(2)}) collective-permute-start(bf16[1152,256]{1,0:T(8,128)(2,1)S(1)} %broadcast_select_fusion.1), channel_id=1, source_target_pairs={{0,1},{1,0},{2,3},{3,2},{4,5},{5,4},{6,7},{7,6},{8,9},{9,8},{10,11... | collective-permute-start | bytes 1769480 | tf_op jit(solution)/shard_map/ppermute | solution.py:291
  26.7 2.4 %collective-permute-start.3 = (bf16[1168,256]{1,0:T(8,128)(2,1)S(1)}, bf16[1168,256]{1,0:T(8,128)(2,1)S(1)}, u32[]{:S(2)}, u32[]{:S(2)}) collective-permute-start(bf16[1168,256]{1,0:T(8,128)(2,1)S(1)} %pad_maximum_fusion.2), channel_id=1, source_target_pairs={{0,1},{1,0},{2,3},{3,2},{4,5},{5,4},{6,7},{7,6},{8,9},{9,8},{10,11... | collective-permute-start | bytes 1794056 | tf_op jit(solution)/shard_map/ppermute | solution.py:291
  55.8 7.6 %collective-permute-start.6 = (bf16[80,256]{1,0:T(8,128)(2,1)S(1)}, bf16[80,256]{1,0:T(8,128)(2,1)S(1)}, u32[]{:S(2)}, u32[]{:S(2)}) collective-permute-start(bf16[80,256]{1,0:T(8,128)(2,1)S(1)} %pad_maximum_fusion.3), channel_id=1, source_target_pairs={{0,136},{64,200},{128,0},{192,64},{8,128},{72,192},{136,8},{200,72... | collective-permute-start | bytes 122888 | tf_op jit(solution)/shard_map/ppermute | solution.py:382
  59.4 5.0 %collective-permute-start.5 = (bf16[80,256]{1,0:T(8,128)(2,1)S(1)}, bf16[80,256]{1,0:T(8,128)(2,1)S(1)}, u32[]{:S(2)}, u32[]{:S(2)}) collective-permute-start(bf16[80,256]{1,0:T(8,128)(2,1)S(1)} %pad_maximum_fusion.3), channel_id=1, source_target_pairs={{0,128},{64,192},{128,8},{192,72},{8,136},{72,200},{136,0},{200,64... | collective-permute-start | bytes 122888 | tf_op jit(solution)/shard_map/ppermute | solution.py:382
  60.2 6.9 %collective-permute-start.4 = (bf16[80,256]{1,0:T(8,128)(2,1)S(1)}, bf16[80,256]{1,0:T(8,128)(2,1)S(1)}, u32[]{:S(2)}, u32[]{:S(2)}) collective-permute-start(bf16[80,256]{1,0:T(8,128)(2,1)S(1)} %pad_maximum_fusion.3), channel_id=1, source_target_pairs={{0,8},{64,72},{128,136},{192,200},{8,0},{72,64},{136,128},{200,192... | collective-permute-start | bytes 122888 | tf_op jit(solution)/shard_map/ppermute | solution.py:382
  68.1 19.0 %all-to-all-start.1 = ((bf16[32,72,256]{2,1,0:T(8,128)(2,1)}), bf16[32,72,256]{2,1,0:T(8,128)(2,1)S(1)}, u32[]{:S(2)}, u32[]{:S(2)}) async-start(bf16[32,72,256]{2,1,0:T(8,128)(2,1)} %broadcast_in_dim.7), calls=%async_computation.1 | async-start | bytes 2359296 | tf_op jit(solution)/shard_map/all_to_all | solution.py:395
  87.2 6.1 %collective-permute-start.7 = (bf16[1152,256]{1,0:T(8,128)(2,1)S(1)}, bf16[1152,256]{1,0:T(8,128)(2,1)S(1)}, u32[]{:S(2)}, u32[]{:S(2)}) collective-permute-start(bf16[1152,256]{1,0:T(8,128)(2,1)S(1)} %bitcast.30), channel_id=1, source_target_pairs={{0,1},{1,0},{2,3},{3,2},{4,5},{5,4},{6,7},{7,6},{8,9},{9,8},{10,11... | collective-permute-start | bytes 1769480 | tf_op jit(solution)/shard_map/ppermute | solution.py:291
  91.7 2.7 %collective-permute-start.8 = (bf16[1152,256]{1,0:T(8,128)(2,1)S(1)}, bf16[1152,256]{1,0:T(8,128)(2,1)S(1)}, u32[]{:S(2)}, u32[]{:S(2)}) collective-permute-start(bf16[1152,256]{1,0:T(8,128)(2,1)S(1)} %bitcast.29), channel_id=1, source_target_pairs={{0,1},{1,0},{2,3},{3,2},{4,5},{5,4},{6,7},{7,6},{8,9},{9,8},{10,11... | collective-permute-start | bytes 1769480 | tf_op jit(solution)/shard_map/ppermute | solution.py:291
